TPU v7x, 256 devices: a whole 4x4x8 slice. The times are simulated.
256 devices in a mesh: vid: 32 (over z, y), head: 8 (over x, core).
Axes of the slice: x: 4, y: 4, z: 8, core: 2. Of those that a mesh axis runs over, the one named last changes fastest.
Arguments:
- queries: bfloat16 [2048, 8192], P('vid', 'head'), may hold values from -6 to 6
- out_grad: bfloat16 [2048, 8192], P('vid', 'head'), may hold values from -1024 to 1024
- log_totals: bfloat16 [64, 2048], P('head', 'vid'), as said below
- out_dots: bfloat16 [64, 2048], P('head', 'vid'), may hold values from -4096 to 4096
- lengths: int32 [32], replicated, may hold values from 1 to 64, 1024 in all
- vis_keys: bfloat16 [16384, 1024], P('vid', 'head'), may hold values from -6 to 6
- vis_values: bfloat16 [16384, 1024], P('vid', 'head'), may hold values from -6 to 6
- key_weight: bfloat16 [8192, 1024], P('head'), may hold values from -0.0625 to 0.0625
- value_weight: bfloat16 [8192, 1024], P('head'), may hold values from -0.0625 to 0.0625
- frame_owner: int32 [1024, 1], replicated, may hold values from 0 to 31; in each aligned block of 32 rows (0 to 31, 32 to 63, ...) at most 2 rows name the same one
Outputs:
- query_grad: bfloat16 [2048, 8192], P('vid', 'head')
- owned_grad: bfloat16 [32768, 8192], P('vid', 'head')
Inputs may be any that keep to these rules, and one draw needn't show every extreme that they name: `lengths`: the entries sum to exactly 1024; rows t * 64 + lengths[t] to t * 64 + 63 of a thread are padding. `frame_owner`: in each aligned block of 32 frames, no owner is named more than 2 times. `log_totals`: each entry lies between log(16384) + 0.25 and log(16384) + 1.35.
All inputs are finite; a program needn't handle non-finite values.
Results may differ from a plain program's by a relative error of at most 0.0057.
Values may be sent and summed in bfloat16 or wider, within the bound.
No kernel may reach another device: no remote copies, remote signals or barrier semaphores. Data moves between devices by JAX's collectives and lax.ppermute only.
A program may use at most 128 MiB of HBM per device.

v0:
```python
import jax
import jax.numpy as jnp
from jax import lax
from jax.sharding import PartitionSpec as P

QH = 64
KVH = 8
HD = 128
TPF = 16


def attend_block(sums_in, query_blk, grad_blk, total_blk, dot_blk, valid_blk, key_rows, value_rows):
    score_scale = HD ** (-0.5)
    scores = (
        jnp.einsum("bhgd,vhd->hgbv", query_blk, key_rows, preferred_element_type=jnp.float32)
        * score_scale
    )
    probs = jnp.exp(scores - total_blk[..., None]) * valid_blk[None, None, :, None]
    grad_probs = jnp.einsum(
        "bhgd,vhd->hgbv", grad_blk, value_rows, preferred_element_type=jnp.float32
    )
    grad_scores = (probs * (grad_probs - dot_blk[..., None])).astype(jnp.bfloat16)
    probs_b = probs.astype(jnp.bfloat16)
    key_acc, value_acc = sums_in
    value_acc = value_acc + jnp.einsum(
        "hgbv,bhgd->vhd", probs_b, grad_blk, preferred_element_type=jnp.float32
    )
    key_acc = key_acc + jnp.einsum(
        "hgbv,bhgd->vhd", grad_scores, query_blk, preferred_element_type=jnp.float32
    )
    query_part = (
        jnp.einsum("hgbv,vhd->bhgd", grad_scores, key_rows, preferred_element_type=jnp.float32)
        * score_scale
    )
    return ((key_acc, value_acc), query_part)


def on_device(
    queries,
    out_grad,
    log_totals,
    out_dots,
    lengths,
    vis_keys,
    vis_values,
    key_weight,
    value_weight,
    frame_owner,
):
    vid_count = lax.axis_size("vid")
    vid_index = lax.axis_index("vid")
    kv_local = vis_keys.shape[1] // HD
    group_size = QH // KVH
    width = queries.shape[1]
    vis_local = vis_keys.shape[0]
    thread_rows = queries.shape[0]
    score_scale = HD ** (-0.5)
    key_local = vis_keys.reshape(vis_local, kv_local, HD)
    value_local = vis_values.reshape(vis_local, kv_local, HD)
    empty_sums = (
        jnp.zeros((vis_local, kv_local, HD), jnp.float32),
        jnp.zeros((vis_local, kv_local, HD), jnp.float32),
    )
    query_all, grad_all, total_all, dot_all = (
        lax.all_gather(queries, "vid", axis=0, tiled=True),
        lax.all_gather(out_grad, "vid", axis=0, tiled=True),
        lax.all_gather(log_totals, "vid", axis=1, tiled=True),
        lax.all_gather(out_dots, "vid", axis=1, tiled=True),
    )
    rows_all = thread_rows * vid_count
    position = jnp.arange(rows_all, dtype=jnp.int32)
    thread = position // thread_rows
    in_thread = position - thread * thread_rows
    valid_pad = in_thread < jnp.take(lengths, thread)
    total_all = total_all.astype(jnp.float32)
    dot_all = dot_all.astype(jnp.float32)
    query_use, grad_use, total_use, dot_use = (query_all, grad_all, total_all, dot_all)
    valid_use = valid_pad.astype(jnp.float32)
    block_rows = min(512, rows_all)
    block_count = rows_all // block_rows
    query_blocks = query_use.reshape(block_count, block_rows, kv_local, group_size, HD)
    grad_blocks = grad_use.reshape(block_count, block_rows, kv_local, group_size, HD)
    total_blocks = total_use.reshape(kv_local, group_size, block_count, block_rows).transpose(
        2, 0, 1, 3
    )
    dot_blocks = dot_use.reshape(kv_local, group_size, block_count, block_rows).transpose(
        2, 0, 1, 3
    )
    valid_blocks = valid_use.reshape(block_count, block_rows)

    def block_step(sums_in, operands):
        query_blk, grad_blk, total_blk, dot_blk, valid_blk = operands
        return attend_block(
            sums_in, query_blk, grad_blk, total_blk, dot_blk, valid_blk, key_local, value_local
        )

    (key_sum, value_sum), query_parts = lax.scan(
        block_step, empty_sums, (query_blocks, grad_blocks, total_blocks, dot_blocks, valid_blocks)
    )
    query_parts = query_parts.reshape(rows_all, width)
    query_grad = lax.psum_scatter(query_parts, "vid", scatter_dimension=0, tiled=True).astype(
        jnp.bfloat16
    )
    key_grad = (key_sum * score_scale).reshape(vis_local, kv_local * HD)
    value_grad = value_sum.reshape(vis_local, kv_local * HD)
    key_all, value_all = (
        lax.all_gather(key_grad.astype(jnp.bfloat16), "head", axis=1, tiled=True),
        lax.all_gather(value_grad.astype(jnp.bfloat16), "head", axis=1, tiled=True),
    )
    contract = (((1,), (1,)), ((), ()))
    vis_grad = lax.dot_general(key_all, key_weight, contract, preferred_element_type=jnp.float32)
    vis_grad = vis_grad + lax.dot_general(
        value_all, value_weight, contract, preferred_element_type=jnp.float32
    )
    vis_grad = vis_grad.astype(jnp.bfloat16)
    columns = vis_grad.shape[1]
    frames_local = vis_local // TPF
    slot_most = max(2, 2 * frames_local // vid_count)
    owners = lax.dynamic_slice_in_dim(frame_owner[:, 0], vid_index * frames_local, frames_local)
    onehot = (owners[:, None] == jnp.arange(vid_count, dtype=jnp.int32)[None, :]).astype(jnp.int32)
    before = jnp.cumsum(onehot, axis=0) - onehot
    slot_rank = jnp.sum(onehot * before, axis=1)
    selector = onehot[:, :, None] * (
        slot_rank[:, None, None] == jnp.arange(slot_most, dtype=jnp.int32)[None, None, :]
    ).astype(jnp.int32)
    selector = selector.reshape(frames_local, vid_count * slot_most).astype(jnp.bfloat16)
    frames = vis_grad.reshape(frames_local, TPF, columns)
    outgoing = jnp.einsum(
        "fs,ftc->stc", selector, frames, preferred_element_type=jnp.float32
    ).astype(jnp.bfloat16)
    outgoing = outgoing.reshape(vid_count * slot_most * TPF, columns)
    owned_rows = lax.all_to_all(outgoing, "vid", split_axis=0, concat_axis=0, tiled=True)
    return (query_grad, owned_rows)


def solution(mesh):
    in_specs = (
        P("vid", "head"),
        P("vid", "head"),
        P("head", "vid"),
        P("head", "vid"),
        P(),
        P("vid", "head"),
        P("vid", "head"),
        P("head", None),
        P("head", None),
        P(),
    )
    out_specs = (P("vid", "head"), P("vid", "head"))
    return jax.shard_map(
        on_device, mesh=mesh, in_specs=in_specs, out_specs=out_specs, check_vma=False
    )
```

profile of v0, /device:TPU:1, one launch (start us, length us, event | category | flops | bytes accessed | tf_op | source)
XLA Modules:
  0.0 547.6 jit_solution(9519825501218049166)
XLA Ops:
  7.2 0.7 all-gather.9.cloned.1.call-update
  8.0 0.7 all-gather.11.cloned.1.call-update
  8.7 0.0 all-gather.13.cloned.1.call-start
  8.7 0.1 compare_reduce_fusion.24
  9.9 1.8 fusion.31
  11.7 2.1 fusion.30
  13.8 4.3 compare_select_fusion.1
  18.2 15.6 %select_select_fusion = s32[2048]{0:T(1024)S(1)} fusion(pred[2048]{0:T(1024)(128)(4,1)S(1)} %compare_reduce_fusion, pred[2048]{0:T(1024)(128)(4,1)S(1)} %compare_reduce_fusion.1, pred[2048]{0:T(1024)(128)(4,1)S(1)} %compare_reduce_fusion.2, pred[2048]{0:T(1024)(128)(4,1)S(1)} %compare_reduce_fusion.3, pred[2048]{0:T(1024)(128)(4,1)S(1)} %compare_reduce_fusion.4, ...), kind=kLoop, calls=%fused_computation.84 | loop fusion | flops 51200 | bytes 67684 | tf_op jit(solution)/shard_map/jit(_take)/gather | solution.py:74
  33.8 42.9 %all-gather.2 = bf16[32,64,8]{1,2,0:T(8,128)(2,1)S(1)} all-gather(bf16[1,64,8]{1,2,0:T(8,128)(2,1)} %bitcast.235), channel_id=1, replica_groups=mesh['vid'=32,'head'=8] {'vid'}, dimensions={0}, use_global_device_ids=true | all-gather | bytes 33792 | tf_op jit(solution)/shard_map/all_gather | solution.py:67
  76.7 0.1 reshape.339
  76.8 37.7 %all-gather.3 = bf16[32,64,8]{1,2,0:T(8,128)(2,1)S(1)} all-gather(bf16[1,64,8]{1,2,0:T(8,128)(2,1)} %bitcast.236), channel_id=1, replica_groups=mesh['vid'=32,'head'=8] {'vid'}, dimensions={0}, use_global_device_ids=true | all-gather | bytes 33792 | tf_op jit(solution)/shard_map/all_gather | solution.py:68
  114.6 0.1 reshape.340
  114.8 5.2 copy.52
  120.0 55.5 %all-gather.11.cloned.1.call-done = bf16[2048,1024]{1,0:T(8,128)(2,1)} async-done(((bf16[64,1024]{1,0:T(8,128)(2,1)}), bf16[2048,1024]{1,0:T(8,128)(2,1)}) %all-gather.11.cloned.1.call-update) | async-done | bytes 4194320 | tf_op jit(solution)/shard_map/all_gather | solution.py:66
  175.5 5.3 copy.53
  180.8 53.0 %while.15 = (s32[]{:T(128)}, f32[512,1,128]{0,2,1:T(8,128)S(1)}, f32[512,1,128]{0,2,1:T(8,128)S(1)}, f32[4,512,1,8,128]{4,3,1,0,2:T(8,128)}, bf16[4,512,1,8,128]...) while((s32[]{:T(128)}, f32[512,1,128]{0,2,1:T(8,128)S(1)}, ...), condition=%wide.region_1.2_spmd.clone, body=%wide.region_0.1_spmd.clone.sunk | while | flops 2706112512 | bytes 54059164 | solution.py:97
  180.9 1.7 constant_dynamic-slice_fusion.8
  182.5 1.3 fusion.53
  183.8 2.4 fusion.56
  186.2 3.2 fusion.54
  189.4 0.8 fusion.55
  190.2 1.2 multiply_bitcast_fusion.2
  191.5 2.6 copy_dynamic-update-slice_fusion.2
  194.1 1.7 constant_dynamic-slice_fusion.8
  195.8 1.3 fusion.53
  197.1 2.4 fusion.56
  199.5 3.2 fusion.54
  202.7 0.8 fusion.55
  203.5 1.2 multiply_bitcast_fusion.2
  204.8 2.5 copy_dynamic-update-slice_fusion.2
  207.4 1.7 constant_dynamic-slice_fusion.8
  209.0 1.3 fusion.53
  210.3 2.4 fusion.56
  212.7 3.2 fusion.54
  216.0 0.8 fusion.55
  216.7 1.2 multiply_bitcast_fusion.2
  218.0 2.6 copy_dynamic-update-slice_fusion.2
  220.6 1.7 constant_dynamic-slice_fusion.8
  222.3 1.3 fusion.53
  223.6 2.4 fusion.56
  226.0 3.2 fusion.54
  229.2 0.8 fusion.55
  230.0 1.2 multiply_bitcast_fusion.2
  231.2 2.6 copy_dynamic-update-slice_fusion.2
  233.8 0.7 multiply_convert_fusion
  234.5 0.0 all-gather.15.cloned.1.call-start
  234.6 0.7 convert_element_type.68
  235.2 0.2 reduce-scatter.2.cloned.1.call-start
  235.5 8.7 %copy.69 = f32[256,8,8,128]{3,1,2,0:T(8,128)} copy(f32[256,8,8,128]{3,2,1,0:T(8,128)} %bitcast.217) | data formatting | bytes 16777216
  244.2 0.7 dynamic-slice_bitcast_fusion
  244.9 0.1 fusion.25
  245.0 0.1 reduce_window_sum.11
  245.0 0.1 copy.38
  245.1 0.2 select_reduce_fusion
  245.3 15.6 %all-gather.13.cloned.1.call-done = bf16[512,1,1024]{0,2,1:T(8,128)(2,1)} async-done(((bf16[512,1,128]{0,2,1:T(8,128)(2,1)}), bf16[512,1,1024]{0,2,1:T(8,128)(2,1)}) %all-gather.13.cloned.1.call-update) | async-done | bytes 1048592 | tf_op jit(solution)/shard_map/all_gather | solution.py:107
  260.9 3.8 fusion.22
  264.7 23.7 %all-gather.15.cloned.1.call-done = bf16[512,1,1024]{0,2,1:T(8,128)(2,1)} async-done(((bf16[512,1,128]{0,2,1:T(8,128)(2,1)}), bf16[512,1,1024]{0,2,1:T(8,128)(2,1)}) %all-gather.15.cloned.1.call-update) | async-done | bytes 1048592 | tf_op jit(solution)/shard_map/all_gather | solution.py:108
  288.4 3.8 add_convert_fusion
  292.3 1.7 convolution_convert_fusion
  293.9 1.2 copy.41
  295.1 74.8 %all_to_all.12 = bf16[32,32,1024]{2,1,0:T(8,128)(2,1)} all-to-all(bf16[32,32,1024]{2,1,0:T(8,128)(2,1)S(1)} %bitcast.219), channel_id=1, replica_groups=mesh['vid'=32,'head'=8] {'vid'}, dimensions={0} | all-to-all | bytes 4194304 | tf_op jit(solution)/shard_map/all_to_all | solution.py:132
  369.9 166.5 %reduce-scatter.2.cloned.1.call-done = f32[64,1024]{1,0:T(8,128)} async-done(((f32[2048,1024]{1,0:T(8,128)}), f32[64,1024]{1,0:T(8,128)}) %reduce-scatter.2.cloned.1.call-update) | async-done | bytes 262160 | tf_op jit(solution)/shard_map/reduce_scatter | solution.py:101
  536.4 1.6 convert_element_type.61
  538.0 3.1 copy.98
  (63 shorter events, 1.6 us)
Async XLA Ops:
  7.2 253.7 %copy-start = (bf16[1024,1024]{1,0:T(8,128)(2,1)S(1)}, bf16[1024,1024]{1,0:T(8,128)(2,1)}, u32[]{:S(2)}) copy-start(bf16[1024,1024]{1,0:T(8,128)(2,1)} %param.19) | copy-start | bytes 6291460
  7.2 107.6 %all-gather.9.cloned.1.call-start = ((), (), s32[]{:S(2)}) async-start(), calls=%async_computation.2 | async-start | bytes 4325376 | tf_op jit(solution)/shard_map/all_gather | solution.py:65
  7.9 167.6 %all-gather.11.cloned.1.call-start = ((), (), s32[]{:S(2)}) async-start(), calls=%async_computation.3 | async-start | bytes 4325376 | tf_op jit(solution)/shard_map/all_gather | solution.py:66
  8.7 252.2 %all-gather.13.cloned.1.call-start = ((), (), s32[]{:S(2)}) async-start(), calls=%async_computation.5 | async-start | bytes 1179648 | tf_op jit(solution)/shard_map/all_gather | solution.py:107
  175.5 5.3 copy-start.1
  175.5 5.3 copy-start.2
  234.5 53.9 %all-gather.15.cloned.1.call-start = ((), (), s32[]{:S(2)}) async-start(), calls=%async_computation.6 | async-start | bytes 1179648 | tf_op jit(solution)/shard_map/all_gather | solution.py:108
  235.2 301.1 %reduce-scatter.2.cloned.1.call-start = ((), (), s32[]{:S(2)}) async-start(), calls=%async_computation.4 | async-start | bytes 8650752 | tf_op jit(solution)/shard_map/reduce_scatter | solution.py:101
Sparse Core Ops, SparseCore 0:
  10.6 83.2 all-gather.8
  96.4 79.0 all-gather.10
  234.6 26.2 all-gather.12
  262.6 25.7 all-gather.14
  292.3 244.0 reduce-scatter.1
where the time goes:
time: 552 us; the launch traced here: 548 us
  waiting for transfers between devices  263 us (48%)
  blocking collectives  155 us (28%)
  local copies, waits for them, and re-layouts  45.6 us (8%)
  matrix products  45 us (8%)
  other arithmetic  24.4 us (4%)
  between operations  13.9 us (3%)
    reduce_scatter x1, waiting for transfers between devices, on_device(): lax.psum_scatter(query_parts, 'vid', scatter_dimension=0, tiled=True)  166 us
    all_to_all x1, blocking collectives, on_device(): lax.all_to_all(outgoing, 'vid', split_axis=0, concat_axis=0, tiled=True)  74.8 us
    all_gather x1, waiting for transfers between devices, on_device(): lax.all_gather(out_grad, 'vid', axis=0, tiled=True)  55.5 us
    all_gather x1, blocking collectives, on_device(): lax.all_gather(log_totals, 'vid', axis=1, tiled=True)  42.9 us
    all_gather x1, blocking collectives, on_device(): lax.all_gather(out_dots, 'vid', axis=1, tiled=True)  37.7 us
    all_gather x1, waiting for transfers between devices, on_device(): lax.all_gather(value_grad.astype(jnp.bfloat16), 'head', axis=1, tiled=True)  23.7 us
    unnamed x10, local copies, waits for them, and re-layouts  22.3 us
    gather x27, other arithmetic, on_device(): valid_pad = in_thread < jnp.take(lengths, thread)  21.1 us
  transfers between devices with their start and end apart: 5, of which 4 were waited for; matrix products, arithmetic and copies ran while one was open for 9% of the time, Pallas kernels for 0%

commit v1 on v0

v1 whole, which is shorter than its diff:
```python
import math

import jax
import jax.numpy as jnp
from jax import lax
from jax.experimental import pallas as pl
from jax.experimental.pallas import tpu as pltpu
from jax.sharding import PartitionSpec as P

QH = 64
KVH = 8
HD = 128
TPF = 16
QLEN = 64
GROUP = QH // KVH
ROWS = GROUP * QLEN
NZ = 8
NY = 4
NX = 4
BLOCK = 512
MSG = 2 * QLEN + 16
FPD = 32
MOST = 2
N_VID = NZ * NY
SLOT_ROWS = N_VID * MOST * TPF
SCALE = HD ** (-0.5)
LOG2E = math.log2(math.e)
DEAD = 1e30
ORDER = (0, -1, 1, -2, 2, -3, 3, 4)
EVEN = (0, 2, -2, 4)
ODD = (-1, 1, -3, 3)
VMEM = 20 * 1024 * 1024
SMALL = 8 * 1024 * 1024
MIDDLE = 12 * 1024 * 1024


def shift(a, axis, k):
    n = lax.axis_size(axis)
    return lax.ppermute(a, axis, [(i, (i + k) % n) for i in range(n)])


def run_copies(pairs, sems):
    copies = [pltpu.make_async_copy(src, dst, sems.at[i]) for i, (src, dst) in enumerate(pairs)]
    for copy in copies:
        copy.start()
    return copies


def pack_kernel(
    where_ref, len_ref, q_ref, g_ref, total_ref, dot_ref, k_ref, v_ref, msg_ref, kv_ref,
    len_at, total_at, dot_at, sems,
):
    f32 = jnp.float32
    copies = run_copies(
        [
            (len_ref, len_at),
            (total_ref, total_at),
            (dot_ref, dot_at),
            (q_ref, msg_ref.at[0:QLEN, :]),
            (g_ref, msg_ref.at[QLEN : 2 * QLEN, :]),
            (k_ref, kv_ref.at[:, 0:HD]),
            (v_ref, kv_ref.at[:, HD : 2 * HD]),
        ],
        sems,
    )
    for copy in copies[:3]:
        copy.wait()
    row = lax.broadcasted_iota(jnp.int32, (GROUP, QLEN), 1)
    total = jnp.where(row < len_at[where_ref[0]], total_at[...].astype(f32), DEAD)
    dots = dot_at[...].astype(f32)
    line = [total[h : h + 1, :] for h in range(GROUP)] + [dots[h : h + 1, :] for h in range(GROUP)]
    line = jnp.concatenate(line, axis=1)
    msg_ref[2 * QLEN :, :] = jnp.broadcast_to(line, (MSG - 2 * QLEN, 2 * ROWS)).astype(jnp.bfloat16)
    for copy in copies[3:]:
        copy.wait()


def pack(where, lengths, queries, out_grad, log_totals, out_dots, vis_keys, vis_values):
    vm = pl.BlockSpec(memory_space=pltpu.VMEM)
    sm = pl.BlockSpec(memory_space=pltpu.SMEM)
    hbm = pl.BlockSpec(memory_space=pltpu.HBM)
    return pl.pallas_call(
        pack_kernel,
        out_shape=[
            jax.ShapeDtypeStruct((MSG, GROUP * HD), jnp.bfloat16),
            jax.ShapeDtypeStruct((BLOCK, 2 * HD), jnp.bfloat16),
        ],
        in_specs=[sm] + [hbm] * 7,
        out_specs=[vm, vm],
        scratch_shapes=[
            pltpu.SMEM(lengths.shape, jnp.int32),
            pltpu.VMEM((GROUP, QLEN), jnp.bfloat16),
            pltpu.VMEM((GROUP, QLEN), jnp.bfloat16),
            pltpu.SemaphoreType.DMA((7,)),
        ],
        cost_estimate=pl.CostEstimate(flops=0, bytes_accessed=1 << 20, transcendentals=0),
        name="pack",
    )(where, lengths, queries, out_grad, log_totals, out_dots, vis_keys, vis_values)


def heads_as_rows(block):
    return jnp.concatenate([block[:, h * HD : (h + 1) * HD] for h in range(GROUP)], axis=0)


NT = (((1,), (1,)), ((), ()))
NN = (((1,), (0,)), ((), ()))
TN = (((0,), (0,)), ((), ()))


def dot32(a, b, contract):
    return lax.dot_general(a, b, contract, preferred_element_type=jnp.float32)


def load_message(ref, c, q_at, g_at, stat_at):
    rows = slice(c * ROWS, (c + 1) * ROWS)
    q_at[rows, :] = heads_as_rows(ref[0:QLEN, :])
    g_at[rows, :] = heads_as_rows(ref[QLEN : 2 * QLEN, :])
    stats = ref[2 * QLEN : MSG, :].astype(jnp.float32)[0:8, :]
    stat_at[8 * c : 8 * c + 8, 0:ROWS] = stats[:, :ROWS] * LOG2E
    stat_at[8 * c : 8 * c + 8, ROWS:] = stats[:, ROWS:]


def attend_tile(c, b, q_at, g_at, stat_at, kv, kv_acc, dq_at):
    rows = pl.ds(pl.multiple_of(c * ROWS, ROWS), ROWS)
    block = pl.ds(pl.multiple_of(b * BLOCK, BLOCK), BLOCK)
    q, g = q_at[rows, :], g_at[rows, :]
    stat = pl.ds(pl.multiple_of(c * 8, 8), 8)
    total, dots = stat_at[stat, 0:ROWS][0:1, :], stat_at[stat, ROWS:][0:1, :]
    k, v = kv[block, 0:HD], kv[block, HD : 2 * HD]
    p = jnp.exp2(dot32(k, q, NT) * (SCALE * LOG2E) - total)
    ds = (p * (dot32(v, g, NT) - dots)).astype(jnp.bfloat16)
    kv_acc[block, HD : 2 * HD] += dot32(p.astype(jnp.bfloat16), g, NN)
    kv_acc[block, 0:HD] += dot32(ds, q, NN)
    dq = pl.ds(pl.multiple_of(c * HD, HD), HD)
    dq_at[dq, :] += dot32(k, ds, TN)


def message_scratch(n):
    return [
        pltpu.VMEM((n * ROWS, HD), jnp.bfloat16),
        pltpu.VMEM((n * ROWS, HD), jnp.bfloat16),
        pltpu.VMEM((8 * n, 2 * ROWS), jnp.float32),
    ]


def attend(name, messages, blocks, accs, dqs, dq_type, acc_type, final, odd=None):
    n, nb = len(messages), len(blocks)
    in_acc = [a for a in accs if a is not None]
    in_dq = [a for a in dqs if a is not None]
    in_odd = list(odd) if odd else []
    operands = list(messages) + list(blocks) + in_acc + in_dq + in_odd
    n_in = len(operands)
    n_dq = 1 if odd else n

    def body(*refs):
        ins = list(refs[:n_in])
        dq_refs = refs[n_in : n_in + n_dq]
        out_refs = refs[n_in + n_dq : n_in + n_dq + nb]
        q_at, g_at, stat_at, kv_at, acc_at, dq_at = refs[n_in + n_dq + nb :]
        take = lambda count: [ins.pop(0) for _ in range(count)]
        msg_refs, kv_refs = take(n), take(nb)
        acc_refs = [take(1)[0] if a is not None else None for a in accs]
        dq_ins = [take(1)[0] if a is not None else None for a in dqs]
        for b in range(nb):
            block = slice(b * BLOCK, (b + 1) * BLOCK)
            kv_at[block, :] = kv_refs[b][...]
            if acc_refs[b] is None:
                acc_at[block, :] = jnp.zeros((BLOCK, 2 * HD), jnp.float32)
            else:
                acc_at[block, :] = acc_refs[b][...]
        for c in range(n):
            load_message(msg_refs[c], c, q_at, g_at, stat_at)
            rows = slice(c * HD, (c + 1) * HD)
            if dq_ins[c] is None:
                dq_at[rows, :] = jnp.zeros((HD, ROWS), jnp.float32)
            else:
                dq_at[rows, :] = dq_ins[c][...]

        def step(b, carry):
            for c in range(n):
                attend_tile(c, b, q_at, g_at, stat_at, kv_at, acc_at, dq_at)
            return carry

        if n == 1 or nb == 1:
            for b in range(nb):
                step(b, 0)
        else:
            lax.fori_loop(0, nb, step, 0)
        if odd:
            for c, ref in enumerate(ins):
                dq_refs[0][c * HD : (c + 1) * HD, :] = ref[...]
            dq_refs[0][len(ins) * HD :, :] = dq_at[...].astype(dq_type)
        else:
            for c in range(n):
                dq_refs[c][...] = dq_at[c * HD : (c + 1) * HD, :].astype(dq_type[c])
        for b in range(nb):
            block = slice(b * BLOCK, (b + 1) * BLOCK)
            dk, dv = acc_at[block, 0:HD], acc_at[block, HD : 2 * HD]
            if final:
                dk = dk * SCALE
            out_refs[b][:, 0:HD] = dk.astype(acc_type)
            out_refs[b][:, HD : 2 * HD] = dv.astype(acc_type)

    if odd:
        out_shape = [jax.ShapeDtypeStruct(((len(in_odd) + n) * HD, ROWS), dq_type)]
    else:
        out_shape = [jax.ShapeDtypeStruct((HD, ROWS), t) for t in dq_type]
    out_shape += [jax.ShapeDtypeStruct((BLOCK, 2 * HD), acc_type)] * nb
    outs = pl.pallas_call(
        body,
        out_shape=out_shape,
        scratch_shapes=message_scratch(n)
        + [
            pltpu.VMEM((nb * BLOCK, 2 * HD), jnp.bfloat16),
            pltpu.VMEM((nb * BLOCK, 2 * HD), jnp.float32),
            pltpu.VMEM((n * HD, ROWS), jnp.float32),
        ],
        compiler_params=pltpu.CompilerParams(vmem_limit_bytes=VMEM),
        cost_estimate=pl.CostEstimate(
            flops=n * 20 * ROWS * nb * BLOCK * HD,
            bytes_accessed=2 << 20,
            transcendentals=n * ROWS * nb * BLOCK,
        ),
        name=name,
    )(*operands)
    return list(outs[:n_dq]), list(outs[n_dq:])


def pair_kernel(where_ref, got_ref, *refs):
    even_refs, keep_ref, send_refs = refs[: len(EVEN)], refs[len(EVEN)], refs[len(EVEN) + 1 :]
    away = 1 - 2 * ((where_ref[0] // NY) % 2)
    for i, offset in enumerate(EVEN):
        there = (offset - away + NZ) % NZ
        slot = jnp.int32(0)
        for j, odd in enumerate(ODD):
            slot = jnp.where(there == odd % NZ, j, slot)
        got = got_ref[pl.ds(pl.multiple_of(slot * HD, HD), HD), :].astype(jnp.float32)
        total = even_refs[i][...] + got
        if i == 0:
            keep_ref[...] = total
        else:
            send_refs[i - 1][...] = total.astype(jnp.bfloat16)


def pair(where, even, got):
    vm = pl.BlockSpec(memory_space=pltpu.VMEM)
    return pl.pallas_call(
        pair_kernel,
        out_shape=[jax.ShapeDtypeStruct((HD, ROWS), jnp.float32)]
        + [jax.ShapeDtypeStruct((HD, ROWS), jnp.bfloat16)] * 3,
        in_specs=[pl.BlockSpec(memory_space=pltpu.SMEM)] + [vm] * 5,
        out_specs=[vm] * 4,
        compiler_params=pltpu.CompilerParams(vmem_limit_bytes=SMALL),
        cost_estimate=pl.CostEstimate(flops=0, bytes_accessed=2 << 20, transcendentals=0),
        name="pair",
    )(where, got, *even)


def dispatch_kernel(where_ref, owner_ref, own_ref, a_ref, b_ref, c_ref, out_ref, sum_ref, count_ref):
    f32 = jnp.float32
    total = own_ref[...] + a_ref[...].astype(f32) + b_ref[...].astype(f32) + c_ref[...].astype(f32)
    sum_ref[...] = total.astype(jnp.bfloat16)
    out_ref[...] = jnp.zeros_like(out_ref)
    for j in range(N_VID):
        count_ref[j] = 0

    def place(f, carry):
        owner = owner_ref[where_ref[0] * FPD + f]
        slot = count_ref[owner]
        count_ref[owner] = slot + 1
        to = pl.multiple_of((owner * MOST + slot) * TPF, TPF)
        fr = pl.multiple_of(f * TPF, TPF)
        out_ref[pl.ds(to, TPF), :] = sum_ref[pl.ds(fr, TPF), :]
        return carry

    lax.fori_loop(0, FPD, place, 0)


def dispatch(where, owners, own, others):
    vm = pl.BlockSpec(memory_space=pltpu.VMEM)
    return pl.pallas_call(
        dispatch_kernel,
        out_shape=jax.ShapeDtypeStruct((SLOT_ROWS, 2 * HD), jnp.bfloat16),
        in_specs=[pl.BlockSpec(memory_space=pltpu.SMEM)] * 2 + [vm] * 4,
        out_specs=vm,
        scratch_shapes=[pltpu.VMEM((BLOCK, 2 * HD), jnp.bfloat16), pltpu.SMEM((N_VID,), jnp.int32)],
        compiler_params=pltpu.CompilerParams(vmem_limit_bytes=SMALL),
        cost_estimate=pl.CostEstimate(flops=0, bytes_accessed=2 << 20, transcendentals=0),
        name="dispatch",
    )(where, owners, own, *others)


PIECES = [(dx, other) for dx in (0, -1, 1, 2) for other in (False, True)]


def project_first(head, rows, key_weight, value_weight):
    cols = key_weight.shape[0]
    feats = KVH * HD
    tile = 512

    def body(head_ref, a_ref, b_ref, wk_ref, wv_ref, acc_ref, w_ref):
        x, core = head_ref[0] // 2, head_ref[0] % 2
        for p, (dx, other) in enumerate(PIECES):
            h = ((x + dx) % NX) * 2 + (1 - core if other else core)
            at = pl.ds(pl.multiple_of(h * HD, HD), HD)
            w_ref[:, 2 * p * HD : (2 * p + 1) * HD] = wk_ref[:, at]
            w_ref[:, (2 * p + 1) * HD : (2 * p + 2) * HD] = wv_ref[:, at]
        for t in range(SLOT_ROWS // tile):
            at = slice(t * tile, (t + 1) * tile)
            a = jnp.concatenate([a_ref[at, :], b_ref[at, :]], axis=1)
            acc_ref[at, :] = dot32(a, w_ref[:, 0 : 4 * HD], NT)

    vm = pl.BlockSpec(memory_space=pltpu.VMEM)
    return pl.pallas_call(
        body,
        out_shape=[
            jax.ShapeDtypeStruct((SLOT_ROWS, cols), jnp.float32),
            jax.ShapeDtypeStruct((cols, 2 * feats), jnp.bfloat16),
        ],
        in_specs=[pl.BlockSpec(memory_space=pltpu.SMEM)] + [vm] * 4,
        out_specs=[vm, vm],
        compiler_params=pltpu.CompilerParams(vmem_limit_bytes=SMALL),
        cost_estimate=pl.CostEstimate(
            flops=SLOT_ROWS * cols * feats, bytes_accessed=10 << 20, transcendentals=0
        ),
        name="project_first",
    )(head, *rows, key_weight, value_weight)


def project_rest(acc, rows, weight):
    cols = weight.shape[0]
    tile = 512

    def body(*refs):
        acc_ref, w_ref, out_ref = refs[len(rows) :]
        for t in range(SLOT_ROWS // tile):
            at = slice(t * tile, (t + 1) * tile)
            a = jnp.concatenate([ref[at, :] for ref in refs[: len(rows)]], axis=1)
            out = acc_ref[at, :] + dot32(a, w_ref[:, 4 * HD :], NT)
            out_ref[at, :] = out.astype(jnp.bfloat16)

    return pl.pallas_call(
        body,
        out_shape=jax.ShapeDtypeStruct((SLOT_ROWS, cols), jnp.bfloat16),
        compiler_params=pltpu.CompilerParams(vmem_limit_bytes=MIDDLE),
        cost_estimate=pl.CostEstimate(
            flops=3 * SLOT_ROWS * cols * KVH * HD, bytes_accessed=10 << 20, transcendentals=0
        ),
        name="project_rest",
    )(*rows, acc, weight)


def finish_kernel(keep_ref, a_ref, b_ref, c_ref, out_ref):
    total = keep_ref[...]
    for ref in (a_ref, b_ref, c_ref):
        total = total + ref[...].astype(jnp.float32)
    total = (total * SCALE).T
    for h in range(GROUP):
        out_ref[:, h * HD : (h + 1) * HD] = total[h * QLEN : (h + 1) * QLEN, :].astype(jnp.bfloat16)


def finish(keep, others):
    return pl.pallas_call(
        finish_kernel,
        out_shape=jax.ShapeDtypeStruct((QLEN, GROUP * HD), jnp.bfloat16),
        compiler_params=pltpu.CompilerParams(vmem_limit_bytes=SMALL),
        cost_estimate=pl.CostEstimate(flops=0, bytes_accessed=1 << 19, transcendentals=0),
        name="finish",
    )(keep, *others)


def on_device(
    queries,
    out_grad,
    log_totals,
    out_dots,
    lengths,
    vis_keys,
    vis_values,
    key_weight,
    value_weight,
    frame_owner,
):
    vid = lax.axis_index("z") * NY + lax.axis_index("y")
    head = lax.axis_index("x") * 2 + lax.axis_index("core")
    where, head = vid.reshape(1), head.reshape(1)

    msg, kv0 = pack(
        where, lengths, queries, out_grad, log_totals, out_dots, vis_keys, vis_values
    )

    kv_up, kv_down = shift(kv0, "y", 1), shift(kv0, "y", -1)
    up1, down1 = shift(msg, "z", 1), shift(msg, "z", -1)
    away = [kv_up, kv_down, shift(kv0, "y", 2)]
    up2, down2 = shift(up1, "z", 1), shift(down1, "z", -1)
    bf16, f32 = jnp.bfloat16, jnp.float32
    none = [None] * NY

    near = [msg, up1, down1]
    dq, (own,) = attend("home_first", near, [kv0], none[:1], none[:3], [f32] * 3, f32, False)
    up2, down2, own = lax.optimization_barrier((up2, down2, own))
    up3, down3 = shift(up2, "z", 1), shift(down2, "z", -1)
    dq, acc = attend("away_near", near, away, none[:3], dq, [f32, bf16, bf16], f32, False)
    dq_0, dq_u1, dq_d1 = dq
    up3, down3, dq_0 = lax.optimization_barrier((up3, down3, dq_0))
    far = shift(up3, "z", 1)
    two = [up2, down2]
    (dq_u2, dq_d2), acc = attend("away_two", two, away, acc, none[:2], [f32] * 2, f32, False)
    three = [up3, down3]
    (odd,), acc = attend(
        "all_three", three, away + [kv0], acc + [own], none[:2], bf16, f32, False, (dq_u1, dq_d1)
    )
    own = acc.pop()
    (dq_4,), parts = attend("away_far", [far], away, acc, none[:1], [f32], bf16, True)

    part_up, part_down, part_far = parts
    back = (shift(part_far, "y", 2), shift(part_up, "y", -1), shift(part_down, "y", 1))
    got = lax.ppermute(odd, "z", [(i, i ^ 1) for i in range(NZ)])
    dq, (own,) = attend(
        "home_last", two + [far], [kv0], [own], [dq_u2, dq_d2, dq_4], [f32] * 3, f32, True
    )
    even = [dq_0, dq[1], dq[0], dq[2]]

    keep, *sends = pair(where, even, got)
    others = [shift(rows, "z", offset) for rows, offset in zip(sends, EVEN[1:])]
    own, keep = lax.optimization_barrier((own, keep))

    outgoing = dispatch(where, frame_owner.reshape(-1), own, back)
    mine = lax.all_to_all(outgoing, ("z", "y"), split_axis=0, concat_axis=0, tiled=True)
    mine, *others = lax.optimization_barrier((mine, *others))

    right, left, across = shift(mine, "x", 1), shift(mine, "x", -1), shift(mine, "x", 2)
    here = [mine, shift(mine, "core", 1)]
    acc, weight = project_first(head, here, key_weight, value_weight)
    query_grad = finish(keep, others)
    pieces = []
    for rows in (right, left, across):
        pieces += [rows, shift(rows, "core", 1)]
    acc, query_grad = lax.optimization_barrier((acc, query_grad))
    return query_grad, project_rest(acc, pieces, weight)


def solution(mesh):
    devices = mesh.devices.reshape(NZ, NY, NX, 2)
    split = jax.sharding.Mesh(devices, ("z", "y", "x", "core"))
    vid, head = ("z", "y"), ("x", "core")
    in_specs = (
        P(vid, head),
        P(vid, head),
        P(head, vid),
        P(head, vid),
        P(),
        P(vid, head),
        P(vid, head),
        P(head, None),
        P(head, None),
        P(),
    )
    out_specs = (P(vid, head), P(vid, head))
    return jax.shard_map(
        on_device, mesh=split, in_specs=in_specs, out_specs=out_specs, check_vma=False
    )
```

time: 552 us -> 137 us (0.25)
  waiting for transfers between devices: 263 us -> 33.5 us
  blocking collectives: 155 us -> 0 us
  starting transfers between devices: 0.38 us -> 58.3 us
  matrix products: 45 us -> 0 us
  local copies, waits for them, and re-layouts: 45.6 us -> 6.63 us
  Pallas kernels: 0 us -> 37.1 us
  other arithmetic: 24.4 us -> 0 us
  between operations: 13.9 us -> 0.83 us
    reduce_scatter x1 -> x0, waiting for transfers between devices: 166 us -> none  [on_device(): lax.psum_scatter(query_parts, 'vid', scatter_dimension=0, tiled=True)]
    all_gather x4 -> x0, waiting for transfers between devices: 94.8 us -> none  [the longest x1 55.5 us: on_device(): lax.all_gather(out_grad, 'vid', axis=0, tiled=True)]
    all_gather x2 -> x0, blocking collectives: 80.6 us -> none  [the longest x1 42.9 us: on_device(): lax.all_gather(log_totals, 'vid', axis=1, tiled=True)]
    all_to_all x1 -> x0, blocking collectives: 74.8 us -> none  [on_device(): lax.all_to_all(outgoing, 'vid', split_axis=0, concat_axis=0, tiled=True)]
    ppermute x0 -> x24, starting transfers between devices: none -> 50.3 us  [the longest x23 48.7 us: shift(): return lax.ppermute(a, axis, [(i, (i + k) % n) for i in range(n)])]
    dot_general x23 -> x0, matrix products: 45 us -> none  [the longest x4 13 us: attend_block(): jnp.einsum('bhgd,vhd->hgbv', grad_blk, value_rows, preferred_element_type...]
    pallas_call x0 -> x12, Pallas kernels: none -> 37.1 us  [the longest x6 23.4 us: attend(): pl.pallas_call(body, out_shape=out_shape, scratch_shapes=message_scratch(...]
    ppermute x0 -> x24, waiting for transfers between devices: none -> 33.5 us  [the longest x23 31.9 us: shift(): return lax.ppermute(a, axis, [(i, (i + k) % n) for i in range(n)])]
  transfers between devices with their start and end apart: 5 -> 25, of which waited for: 4 -> 10; matrix products, arithmetic and copies ran while one was open for 9% -> 0% of each run, Pallas kernels for 0% -> 19%
where the time goes in v1:
time: 137 us; the launch traced here: 136 us
  starting transfers between devices  58.3 us (43%)
  Pallas kernels  37.1 us (27%)
  waiting for transfers between devices  33.5 us (24%)
  local copies, waits for them, and re-layouts  6.63 us (5%)
    ppermute x23, starting transfers between devices, shift(): return lax.ppermute(a, axis, [(i, (i + k) % n) for i in range(n)])  48.7 us
    ppermute x23, waiting for transfers between devices, shift(): return lax.ppermute(a, axis, [(i, (i + k) % n) for i in range(n)])  31.9 us
    pallas_call x6, Pallas kernels, attend(): pl.pallas_call(body, out_shape=out_shape, scratch_shapes=message_scratch(...  23.4 us
    all_to_all x1, starting transfers between devices, on_device(): lax.all_to_all(outgoing, ('z', 'y'), split_axis=0, concat_axis=0, tiled=T...  8.03 us
    pallas_call x1, Pallas kernels, project_rest(): pl.pallas_call(body, out_shape=jax.ShapeDtypeStruct((SLOT_ROWS, cols), jn...  6.65 us
    unnamed x24, local copies, waits for them, and re-layouts  6.63 us
  transfers between devices with their start and end apart: 25, of which 10 were waited for; matrix products, arithmetic and copies ran while one was open for 0% of the time, Pallas kernels for 19%

profile of v1, /device:TPU:1, one launch (start us, length us, event | category | flops | bytes accessed | tf_op | source)
XLA Modules:
  0.0 136.4 jit_solution(14199857251442155974)
XLA Ops:
  0.6 2.0 %pack.1 = (bf16[144,1024]{1,0:T(8,128)(2,1)}, bf16[512,256]{1,0:T(8,128)(2,1)}) custom-call(s32[1]{0:T(128)} %bitcast.1.where_ref, s32[32]{0:T(128)} %len_ref.1, bf16[64,1024]{1,0:T(8,128)(2,1)} %q_ref.1, bf16[64,1024]{1,0:T(8,128)(2,1)} %g_ref.1, bf16[8,64]{1,0:T(8,128)(2,1)} %total_ref.1, bf16[8,64]{1,0:T(8,128)(2,1)} %dot_ref.1, bf16[512,128]{1,0:T(8,128)(2,1)} %k_ref.1, ...), custom_call_target="tpu_custom_call" | custom-call | bytes 1048576 | tf_op jit(solution)/shard_map/pack/pallas_call | solution.py:82
  2.6 2.5 %collective-permute-start = (bf16[144,1024]{1,0:T(8,128)(2,1)}, bf16[144,1024]{1,0:T(8,128)(2,1)S(1)}, u32[]{:S(2)}, u32[]{:S(2)}) collective-permute-start(bf16[144,1024]{1,0:T(8,128)(2,1)} %get-tuple-element.52.refs_0_), channel_id=1, source_target_pairs={{0,32},{32,64},{64,96},{96,128},{128,160},{160,192},{192,224},{224... | collective-permute-start | bytes 884744 | tf_op jit(solution)/shard_map/ppermute | solution.py:39
  5.2 4.0 %collective-permute-start.2 = (bf16[144,1024]{1,0:T(8,128)(2,1)}, bf16[144,1024]{1,0:T(8,128)(2,1)S(1)}, u32[]{:S(2)}, u32[]{:S(2)}) collective-permute-start(bf16[144,1024]{1,0:T(8,128)(2,1)} %get-tuple-element.52.refs_0_), channel_id=1, source_target_pairs={{0,224},{32,0},{64,32},{96,64},{128,96},{160,128},{192,160},{224,1... | collective-permute-start | bytes 884744 | tf_op jit(solution)/shard_map/ppermute | solution.py:39
  9.2 1.3 collective-permute-start.6
  10.5 1.4 %collective-permute-start.7 = (bf16[512,256]{1,0:T(8,128)(2,1)}, bf16[512,256]{1,0:T(8,128)(2,1)S(1)}, u32[]{:S(2)}, u32[]{:S(2)}) collective-permute-start(bf16[512,256]{1,0:T(8,128)(2,1)} %get-tuple-element.53.refs_3_.refs_5_), channel_id=1, source_target_pairs={{0,24},{8,0},{16,8},{24,16},{1,25},{9,1},{17,9},{25,17},{2,26},{10... | collective-permute-start | bytes 786440 | tf_op jit(solution)/shard_map/ppermute | solution.py:39
  12.0 1.6 %collective-permute-start.8 = (bf16[512,256]{1,0:T(8,128)(2,1)}, bf16[512,256]{1,0:T(8,128)(2,1)S(1)}, u32[]{:S(2)}, u32[]{:S(2)}) collective-permute-start(bf16[512,256]{1,0:T(8,128)(2,1)} %get-tuple-element.53.refs_3_.refs_5_), channel_id=1, source_target_pairs={{0,16},{8,24},{16,0},{24,8},{1,17},{9,25},{17,1},{25,9},{2,18},{10... | collective-permute-start | bytes 786440 | tf_op jit(solution)/shard_map/ppermute | solution.py:39
  13.6 2.5 %collective-permute-done.refs_1_ = bf16[144,1024]{1,0:T(8,128)(2,1)S(1)} collective-permute-done((bf16[144,1024]{1,0:T(8,128)(2,1)}, bf16[144,1024]{1,0:T(8,128)(2,1)S(1)}, u32[]{:S(2)}, u32[]{:S(2)}) %collective-permute-start) | collective-permute-done | bytes 294944 | tf_op jit(solution)/shard_map/ppermute | solution.py:39
  16.1 0.0 collective-permute-start.1
  16.1 2.7 %collective-permute-start.3 = (bf16[144,1024]{1,0:T(8,128)(2,1)S(1)}, bf16[144,1024]{1,0:T(8,128)(2,1)S(1)}, u32[]{:S(2)}, u32[]{:S(2)}) collective-permute-start(bf16[144,1024]{1,0:T(8,128)(2,1)S(1)} %collective-permute-done.2.refs_2_), channel_id=1, source_target_pairs={{0,224},{32,0},{64,32},{96,64},{128,96},{160,128},{192,160},{224,1... | collective-permute-start | bytes 884744 | tf_op jit(solution)/shard_map/ppermute | solution.py:39
  18.8 1.0 copy-done.7
  19.7 0.9 copy-done.8
  20.7 2.1 %home_first.1 = (f32[128,512]{1,0:T(8,128)S(1)}, f32[128,512]{1,0:T(8,128)S(1)}, f32[128,512]{1,0:T(8,128)S(1)}, f32[512,256]{1,0:T(8,128)S(1)}) custom-call(bf16[144,1024]{1,0:T(8,128)(2,1)S(1)} %copy-done.7, bf16[144,1024]{1,0:T(8,128)(2,1)S(1)} %collective-permute-done.refs_1_, bf16[144,1024]{1,0:T(8,128)(2,1)S(1)} %collective-permute-done.2.refs_2_, ...), custom_call_target="tpu_custom_call" | custom-call | flops 2013265920 | bytes 2097152 | tf_op jit(solution)/shard_map/home_first/pallas_call | solution.py:209
  22.7 0.0 collective-permute-done.7.refs_4_.refs_3_.refs_2_
  22.8 1.6 %collective-permute-done.8.refs_5_.refs_4_.refs_3_ = bf16[512,256]{1,0:T(8,128)(2,1)S(1)} collective-permute-done((bf16[512,256]{1,0:T(8,128)(2,1)}, bf16[512,256]{1,0:T(8,128)(2,1)S(1)}, u32[]{:S(2)}, u32[]{:S(2)}) %collective-permute-start.8) | collective-permute-done | bytes 262176 | tf_op jit(solution)/shard_map/ppermute | solution.py:39
  24.4 6.5 %away_near.1 = (f32[128,512]{1,0:T(8,128)S(1)}, bf16[128,512]{1,0:T(8,128)(2,1)S(1)}, bf16[128,512]{1,0:T(8,128)(2,1)S(1)}, f32[512,256]{1,0:T(8,128)S(1)}, f32[...) custom-call(bf16[144,1024]{1,0:T(8,128)(2,1)S(1)} %copy-done.7, bf16[144,1024]{1,0:T(8,128)(2,1)S(1)} %collective-permute-done.refs_1_, ...), custom_call_target="tpu_custom_call" | custom-call | flops 6039797760 | bytes 2097152 | tf_op jit(solution)/shard_map/away_near/pallas_call | solution.py:209
  30.8 0.0 collective-permute-done.1.refs_0_
  30.9 0.1 collective-permute-start.4
  30.9 2.7 %collective-permute-start.5 = (bf16[144,1024]{1,0:T(8,128)(2,1)S(1)}, bf16[144,1024]{1,0:T(8,128)(2,1)S(1)}, u32[]{:S(2)}, u32[]{:S(2)}) collective-permute-start(bf16[144,1024]{1,0:T(8,128)(2,1)S(1)} %collective-permute-done.3.refs_1_), channel_id=1, source_target_pairs={{0,224},{32,0},{64,32},{96,64},{128,96},{160,128},{192,160},{224,1... | collective-permute-start | bytes 884744 | tf_op jit(solution)/shard_map/ppermute | solution.py:39
  33.6 4.6 %away_two.1 = (f32[128,512]{1,0:T(8,128)S(1)}, f32[128,512]{1,0:T(8,128)S(1)}, f32[512,256]{1,0:T(8,128)S(1)}, f32[512,256]{1,0:T(8,128)S(1)}, f32[512,256]{1,0:T(8,128)S(1)}) custom-call(bf16[144,1024]{1,0:T(8,128)(2,1)S(1)} %collective-permute-done.1.refs_0_, bf16[144,1024]{1,0:T(8,128)(2,1)S(1)} %collective-permute-done.3.refs_1_, ...), custom_call_target="tpu_custom_call" | custom-call | flops 4026531840 | bytes 2097152 | tf_op jit(solution)/shard_map/away_two/pallas_call | solution.py:209
  38.2 0.6 collective-permute-done.4.refs_0_
  38.8 0.0 collective-permute-done.5.refs_1_
  38.8 6.1 %all_three.1 = (bf16[512,512]{1,0:T(8,128)(2,1)S(1)}, f32[512,256]{1,0:T(8,128)S(1)}, f32[512,256]{1,0:T(8,128)S(1)}, f32[512,256]{1,0:T(8,128)S(1)}, f32[512,256]{1,0:T(8,128)S(1)}) custom-call(bf16[144,1024]{1,0:T(8,128)(2,1)S(1)} %collective-permute-done.4.refs_0_, bf16[144,1024]{1,0:T(8,128)(2,1)S(1)} %collective-permute-done.5.refs_1_, ...), custom_call_target="tpu_custom_call" | custom-call | flops 5368709120 | bytes 2097152 | tf_op jit(solution)/shard_map/all_three/pallas_call | solution.py:209
  44.9 1.6 %collective-permute-start.10 = (bf16[512,512]{1,0:T(8,128)(2,1)S(1)}, bf16[512,512]{1,0:T(8,128)(2,1)S(1)}, u32[]{:S(2)}, u32[]{:S(2)}) collective-permute-start(bf16[512,512]{1,0:T(8,128)(2,1)S(1)} %get-tuple-element.80), channel_id=1, source_target_pairs={{0,32},{32,0},{64,96},{96,64},{128,160},{160,128},{192,224},{224,1... | collective-permute-start | bytes 1572872 | tf_op jit(solution)/shard_map/ppermute | solution.py:418
  46.4 2.2 %away_far.1 = (f32[128,512]{1,0:T(8,128)S(1)}, bf16[512,256]{1,0:T(8,128)(2,1)S(1)}, bf16[512,256]{1,0:T(8,128)(2,1)S(1)}, bf16[512,256]{1,0:T(8,128)(2,1)S(1)}) custom-call(bf16[144,1024]{1,0:T(8,128)(2,1)S(1)} %collective-permute-done.9.refs_0_.refs_2_, bf16[512,256]{1,0:T(8,128)(2,1)S(1)} %collective-permute-done.6.refs_3_.refs_2_.refs_1_, ...), custom_call_target="tpu_custom_call" | custom-call | flops 2013265920 | bytes 2097152 | tf_op jit(solution)/shard_map/away_far/pallas_call | solution.py:209
  48.6 1.5 %collective-permute-start.11 = (bf16[512,256]{1,0:T(8,128)(2,1)S(1)}, bf16[512,256]{1,0:T(8,128)(2,1)S(1)}, u32[]{:S(2)}, u32[]{:S(2)}) collective-permute-start(bf16[512,256]{1,0:T(8,128)(2,1)S(1)} %get-tuple-element.87), channel_id=1, source_target_pairs={{0,16},{8,24},{16,0},{24,8},{1,17},{9,25},{17,1},{25,9},{2,18},{10... | collective-permute-start | bytes 786440 | tf_op jit(solution)/shard_map/ppermute | solution.py:39
  50.1 1.3 collective-permute-start.12
  51.4 0.2 collective-permute-start.13
  51.6 2.1 %home_last.1 = (f32[128,512]{1,0:T(8,128)S(1)}, f32[128,512]{1,0:T(8,128)S(1)}, f32[128,512]{1,0:T(8,128)S(1)}, f32[512,256]{1,0:T(8,128)S(1)}) custom-call(bf16[144,1024]{1,0:T(8,128)(2,1)S(1)} %collective-permute-done.1.refs_0_, bf16[144,1024]{1,0:T(8,128)(2,1)S(1)} %collective-permute-done.3.refs_1_, ...), custom_call_target="tpu_custom_call" | custom-call | flops 2013265920 | bytes 2097152 | tf_op jit(solution)/shard_map/home_last/pallas_call | solution.py:209
  53.7 1.6 %collective-permute-done.10.got_ref = bf16[512,512]{1,0:T(8,128)(2,1)S(1)} collective-permute-done((bf16[512,512]{1,0:T(8,128)(2,1)S(1)}, bf16[512,512]{1,0:T(8,128)(2,1)S(1)}, u32[]{:S(2)}, u32[]{:S(2)}) %collective-permute-start.10) | collective-permute-done | bytes 524320 | tf_op jit(solution)/shard_map/ppermute | solution.py:418
  55.3 0.1 pair.1
  55.4 0.0 copy-start.11
  55.4 0.0 copy-start
  55.4 0.0 collective-permute-done.11.a_ref
  55.4 2.7 %collective-permute-done.12.b_ref = bf16[512,256]{1,0:T(8,128)(2,1)S(1)} collective-permute-done((bf16[512,256]{1,0:T(8,128)(2,1)S(1)}, bf16[512,256]{1,0:T(8,128)(2,1)S(1)}, u32[]{:S(2)}, u32[]{:S(2)}) %collective-permute-start.12) | collective-permute-done | bytes 262176 | tf_op jit(solution)/shard_map/ppermute | solution.py:39
  58.2 1.8 %collective-permute-done.13.c_ref = bf16[512,256]{1,0:T(8,128)(2,1)S(1)} collective-permute-done((bf16[512,256]{1,0:T(8,128)(2,1)S(1)}, bf16[512,256]{1,0:T(8,128)(2,1)S(1)}, u32[]{:S(2)}, u32[]{:S(2)}) %collective-permute-start.13) | collective-permute-done | bytes 262176 | tf_op jit(solution)/shard_map/ppermute | solution.py:39
  60.0 1.9 %dispatch.1 = bf16[1024,256]{1,0:T(8,128)(2,1)} custom-call(s32[1]{0:T(128)} %bitcast.1.where_ref, s32[1024]{0:T(1024)S(1)} %bitcast.10, f32[512,256]{1,0:T(8,128)S(1)} %get-tuple-element.86.own_ref, bf16[512,256]{1,0:T(8,128)(2,1)S(1)} %collective-permute-done.11.a_ref, bf16[512,256]{1,0:T(8,128)(2,1)S(1)} %collective-permute-done.12.b_ref, ...), custom_call_target="tpu_custom_call" | custom-call | bytes 2097152 | tf_op jit(solution)/shard_map/dispatch/pallas_call | solution.py:281
  61.9 8.0 %all-to-all-start = ((bf16[32,32,256]{2,1,0:T(8,128)(2,1)}), bf16[32,32,256]{2,1,0:T(8,128)(2,1)S(1)}, u32[]{:S(2)}, u32[]{:S(2)}) async-start(bf16[32,32,256]{2,1,0:T(8,128)(2,1)} %bitcast.3), calls=%async_computation | async-start | bytes 1048576 | tf_op jit(solution)/shard_map/all_to_all | solution.py:429
  69.9 2.2 %collective-permute-start.14 = (bf16[128,512]{1,0:T(8,128)(2,1)}, bf16[128,512]{1,0:T(8,128)(2,1)S(1)}, u32[]{:S(2)}, u32[]{:S(2)}) collective-permute-start(bf16[128,512]{1,0:T(8,128)(2,1)} %copy-done.11), channel_id=1, source_target_pairs={{0,64},{32,96},{64,128},{96,160},{128,192},{160,224},{192,0},{224,... | collective-permute-start | bytes 393224 | tf_op jit(solution)/shard_map/ppermute | solution.py:39
  72.1 1.6 %collective-permute-start.15 = (bf16[128,512]{1,0:T(8,128)(2,1)}, bf16[128,512]{1,0:T(8,128)(2,1)S(1)}, u32[]{:S(2)}, u32[]{:S(2)}) collective-permute-start(bf16[128,512]{1,0:T(8,128)(2,1)} %copy-done.10), channel_id=1, source_target_pairs={{0,192},{32,224},{64,0},{96,32},{128,64},{160,96},{192,128},{224,1... | collective-permute-start | bytes 393224 | tf_op jit(solution)/shard_map/ppermute | solution.py:39
  73.7 5.0 %collective-permute-start.16 = (bf16[128,512]{1,0:T(8,128)(2,1)S(1)}, bf16[128,512]{1,0:T(8,128)(2,1)S(1)}, u32[]{:S(2)}, u32[]{:S(2)}) collective-permute-start(bf16[128,512]{1,0:T(8,128)(2,1)S(1)} %get-tuple-element.92), channel_id=1, source_target_pairs={{0,128},{32,160},{64,192},{96,224},{128,0},{160,32},{192,64},{224,... | collective-permute-start | bytes 393224 | tf_op jit(solution)/shard_map/ppermute | solution.py:39
  78.7 8.4 %collective-permute-done.14.a_ref = bf16[128,512]{1,0:T(8,128)(2,1)S(1)} collective-permute-done((bf16[128,512]{1,0:T(8,128)(2,1)}, bf16[128,512]{1,0:T(8,128)(2,1)S(1)}, u32[]{:S(2)}, u32[]{:S(2)}) %collective-permute-start.14) | collective-permute-done | bytes 131104 | tf_op jit(solution)/shard_map/ppermute | solution.py:39
  87.1 0.0 collective-permute-done.15.b_ref
  87.1 0.7 copy-done.2
  87.8 6.9 %collective-permute-done.16.c_ref = bf16[128,512]{1,0:T(8,128)(2,1)S(1)} collective-permute-done((bf16[128,512]{1,0:T(8,128)(2,1)S(1)}, bf16[128,512]{1,0:T(8,128)(2,1)S(1)}, u32[]{:S(2)}, u32[]{:S(2)}) %collective-permute-start.16) | collective-permute-done | bytes 131104 | tf_op jit(solution)/shard_map/ppermute | solution.py:39
  94.7 0.6 copy-done.4
  95.3 0.0 all-to-all-done
  95.3 1.2 collective-permute-start.18
  96.5 1.4 %collective-permute-start.20 = (bf16[1024,256]{1,0:T(8,128)(2,1)S(1)}, bf16[1024,256]{1,0:T(8,128)(2,1)}, u32[]{:S(2)}, u32[]{:S(2)}) collective-permute-start(bf16[1024,256]{1,0:T(8,128)(2,1)S(1)} %bitcast.6), channel_id=1, source_target_pairs={{0,6},{2,0},{4,2},{6,4},{1,7},{3,1},{5,3},{7,5},{8,14},{10,8},{12,... | collective-permute-start | bytes 1572872 | tf_op jit(solution)/shard_map/ppermute | solution.py:39
  98.0 1.5 %collective-permute-start.22 = (bf16[1024,256]{1,0:T(8,128)(2,1)S(1)}, bf16[1024,256]{1,0:T(8,128)(2,1)}, u32[]{:S(2)}, u32[]{:S(2)}) collective-permute-start(bf16[1024,256]{1,0:T(8,128)(2,1)S(1)} %bitcast.7), channel_id=1, source_target_pairs={{0,4},{2,6},{4,0},{6,2},{1,5},{3,7},{5,1},{7,3},{8,12},{10,14},{12... | collective-permute-start | bytes 1572872 | tf_op jit(solution)/shard_map/ppermute | solution.py:39
  99.5 4.1 %collective-permute-start.17 = (bf16[1024,256]{1,0:T(8,128)(2,1)S(1)}, bf16[1024,256]{1,0:T(8,128)(2,1)S(1)}, u32[]{:S(2)}, u32[]{:S(2)}) collective-permute-start(bf16[1024,256]{1,0:T(8,128)(2,1)S(1)} %bitcast.8), channel_id=1, source_target_pairs={{0,1},{1,0},{2,3},{3,2},{4,5},{5,4},{6,7},{7,6},{8,9},{9,8},{10,11... | collective-permute-start | bytes 1572872 | tf_op jit(solution)/shard_map/ppermute | solution.py:39
  103.6 3.2 %collective-permute-done.18.refs_0_ = bf16[1024,256]{1,0:T(8,128)(2,1)} collective-permute-done((bf16[1024,256]{1,0:T(8,128)(2,1)S(1)}, bf16[1024,256]{1,0:T(8,128)(2,1)}, u32[]{:S(2)}, u32[]{:S(2)}) %collective-permute-start.18) | collective-permute-done | bytes 524320 | tf_op jit(solution)/shard_map/ppermute | solution.py:39
  106.8 6.8 %collective-permute-start.19 = (bf16[1024,256]{1,0:T(8,128)(2,1)}, bf16[1024,256]{1,0:T(8,128)(2,1)}, u32[]{:S(2)}, u32[]{:S(2)}) collective-permute-start(bf16[1024,256]{1,0:T(8,128)(2,1)} %collective-permute-done.18.refs_0_), channel_id=1, source_target_pairs={{0,1},{1,0},{2,3},{3,2},{4,5},{5,4},{6,7},{7,6},{8,9},{9,8},{10,11... | collective-permute-start | bytes 1572872 | tf_op jit(solution)/shard_map/ppermute | solution.py:39
  113.6 0.0 collective-permute-done.20.refs_2_
  113.6 1.4 %collective-permute-start.21 = (bf16[1024,256]{1,0:T(8,128)(2,1)}, bf16[1024,256]{1,0:T(8,128)(2,1)}, u32[]{:S(2)}, u32[]{:S(2)}) collective-permute-start(bf16[1024,256]{1,0:T(8,128)(2,1)} %collective-permute-done.20.refs_2_), channel_id=1, source_target_pairs={{0,1},{1,0},{2,3},{3,2},{4,5},{5,4},{6,7},{7,6},{8,9},{9,8},{10,11... | collective-permute-start | bytes 1572872 | tf_op jit(solution)/shard_map/ppermute | solution.py:39
  115.0 4.2 %collective-permute-done.22.refs_4_ = bf16[1024,256]{1,0:T(8,128)(2,1)} collective-permute-done((bf16[1024,256]{1,0:T(8,128)(2,1)S(1)}, bf16[1024,256]{1,0:T(8,128)(2,1)}, u32[]{:S(2)}, u32[]{:S(2)}) %collective-permute-start.22) | collective-permute-done | bytes 524320 | tf_op jit(solution)/shard_map/ppermute | solution.py:39
  119.1 4.1 %collective-permute-start.23 = (bf16[1024,256]{1,0:T(8,128)(2,1)}, bf16[1024,256]{1,0:T(8,128)(2,1)}, u32[]{:S(2)}, u32[]{:S(2)}) collective-permute-start(bf16[1024,256]{1,0:T(8,128)(2,1)} %collective-permute-done.22.refs_4_), channel_id=1, source_target_pairs={{0,1},{1,0},{2,3},{3,2},{4,5},{5,4},{6,7},{7,6},{8,9},{9,8},{10,11... | collective-permute-start | bytes 1572872 | tf_op jit(solution)/shard_map/ppermute | solution.py:39
  123.3 0.9 copy-done.3
  124.2 0.9 copy-done.5
  125.1 0.8 finish.1
  125.9 1.6 %copy-done.1 = bf16[1024,1024]{1,0:T(8,128)(2,1)S(1)} copy-done((bf16[1024,1024]{1,0:T(8,128)(2,1)S(1)}, bf16[1024,1024]{1,0:T(8,128)(2,1)}, u32[]{:S(2)}) %copy-start.1) | copy-done | bytes 2097176
  127.5 2.3 %project_first.1 = (f32[1024,1024]{1,0:T(8,128)S(1)}, bf16[1024,2048]{1,0:T(8,128)(2,1)S(1)}) custom-call(s32[1]{0:T(128)} %bitcast.head_ref, bf16[1024,256]{1,0:T(8,128)(2,1)S(1)} %bitcast.9, bf16[1024,256]{1,0:T(8,128)(2,1)S(1)} %collective-permute-done.17.b_ref, bf16[1024,1024]{1,0:T(8,128)(2,1)S(1)} %copy-done, bf16[1024,1024]{1,0:T(8,128)(2,1)S(1)} %copy-done.1), custom_call_target="tpu_custom_call" | custom-call | flops 1073741824 | bytes 10485760 | tf_op jit(solution)/shard_map/project_first/pallas_call | solution.py:314
  129.7 0.0 collective-permute-done.19.refs_1_
  129.7 0.0 collective-permute-done.21.refs_3_
  129.7 6.7 %project_rest.1 = bf16[1024,1024]{1,0:T(8,128)(2,1)} custom-call(bf16[1024,256]{1,0:T(8,128)(2,1)} %collective-permute-done.18.refs_0_, bf16[1024,256]{1,0:T(8,128)(2,1)} %collective-permute-done.19.refs_1_, bf16[1024,256]{1,0:T(8,128)(2,1)} %collective-permute-done.20.refs_2_, bf16[1024,256]{1,0:T(8,128)(2,1)} %collective-permute-done.21.refs_3_, ...), custom_call_target="tpu_custom_call" | custom-call | flops 3221225472 | bytes 10485760 | tf_op jit(solution)/shard_map/project_rest/pallas_call | solution.py:342
  (22 shorter events, 0.0 us)
Async XLA Ops:
  2.6 13.4 %collective-permute-start = (bf16[144,1024]{1,0:T(8,128)(2,1)}, bf16[144,1024]{1,0:T(8,128)(2,1)S(1)}, u32[]{:S(2)}, u32[]{:S(2)}) collective-permute-start(bf16[144,1024]{1,0:T(8,128)(2,1)} %get-tuple-element.52.refs_0_), channel_id=1, source_target_pairs={{0,32},{32,64},{64,96},{96,128},{128,160},{160,192},{192,224},{224... | collective-permute-start | bytes 884744 | tf_op jit(solution)/shard_map/ppermute | solution.py:39
  5.2 10.9 %collective-permute-start.2 = (bf16[144,1024]{1,0:T(8,128)(2,1)}, bf16[144,1024]{1,0:T(8,128)(2,1)S(1)}, u32[]{:S(2)}, u32[]{:S(2)}) collective-permute-start(bf16[144,1024]{1,0:T(8,128)(2,1)} %get-tuple-element.52.refs_0_), channel_id=1, source_target_pairs={{0,224},{32,0},{64,32},{96,64},{128,96},{160,128},{192,160},{224,1... | collective-permute-start | bytes 884744 | tf_op jit(solution)/shard_map/ppermute | solution.py:39
  9.2 13.5 %collective-permute-start.6 = (bf16[512,256]{1,0:T(8,128)(2,1)}, bf16[512,256]{1,0:T(8,128)(2,1)S(1)}, u32[]{:S(2)}, u32[]{:S(2)}) collective-permute-start(bf16[512,256]{1,0:T(8,128)(2,1)} %get-tuple-element.53.refs_3_.refs_5_), channel_id=1, source_target_pairs={{0,8},{8,16},{16,24},{24,0},{1,9},{9,17},{17,25},{25,1},{2,10},{10... | collective-permute-start | bytes 786440 | tf_op jit(solution)/shard_map/ppermute | solution.py:39
  10.5 12.2 %collective-permute-start.7 = (bf16[512,256]{1,0:T(8,128)(2,1)}, bf16[512,256]{1,0:T(8,128)(2,1)S(1)}, u32[]{:S(2)}, u32[]{:S(2)}) collective-permute-start(bf16[512,256]{1,0:T(8,128)(2,1)} %get-tuple-element.53.refs_3_.refs_5_), channel_id=1, source_target_pairs={{0,24},{8,0},{16,8},{24,16},{1,25},{9,1},{17,9},{25,17},{2,26},{10... | collective-permute-start | bytes 786440 | tf_op jit(solution)/shard_map/ppermute | solution.py:39
  12.0 12.4 %collective-permute-start.8 = (bf16[512,256]{1,0:T(8,128)(2,1)}, bf16[512,256]{1,0:T(8,128)(2,1)S(1)}, u32[]{:S(2)}, u32[]{:S(2)}) collective-permute-start(bf16[512,256]{1,0:T(8,128)(2,1)} %get-tuple-element.53.refs_3_.refs_5_), channel_id=1, source_target_pairs={{0,16},{8,24},{16,0},{24,8},{1,17},{9,25},{17,1},{25,9},{2,18},{10... | collective-permute-start | bytes 786440 | tf_op jit(solution)/shard_map/ppermute | solution.py:39
  16.1 14.8 %collective-permute-start.1 = (bf16[144,1024]{1,0:T(8,128)(2,1)S(1)}, bf16[144,1024]{1,0:T(8,128)(2,1)S(1)}, u32[]{:S(2)}, u32[]{:S(2)}) collective-permute-start(bf16[144,1024]{1,0:T(8,128)(2,1)S(1)} %collective-permute-done.refs_1_), channel_id=1, source_target_pairs={{0,32},{32,64},{64,96},{96,128},{128,160},{160,192},{192,224},{224... | collective-permute-start | bytes 884744 | tf_op jit(solution)/shard_map/ppermute | solution.py:39
  16.1 14.8 %collective-permute-start.3 = (bf16[144,1024]{1,0:T(8,128)(2,1)S(1)}, bf16[144,1024]{1,0:T(8,128)(2,1)S(1)}, u32[]{:S(2)}, u32[]{:S(2)}) collective-permute-start(bf16[144,1024]{1,0:T(8,128)(2,1)S(1)} %collective-permute-done.2.refs_2_), channel_id=1, source_target_pairs={{0,224},{32,0},{64,32},{96,64},{128,96},{160,128},{192,160},{224,1... | collective-permute-start | bytes 884744 | tf_op jit(solution)/shard_map/ppermute | solution.py:39
  18.8 1.0 copy-start.7
  19.7 0.9 copy-start.8
  30.9 7.9 %collective-permute-start.4 = (bf16[144,1024]{1,0:T(8,128)(2,1)S(1)}, bf16[144,1024]{1,0:T(8,128)(2,1)S(1)}, u32[]{:S(2)}, u32[]{:S(2)}) collective-permute-start(bf16[144,1024]{1,0:T(8,128)(2,1)S(1)} %collective-permute-done.1.refs_0_), channel_id=1, source_target_pairs={{0,32},{32,64},{64,96},{96,128},{128,160},{160,192},{192,224},{224... | collective-permute-start | bytes 884744 | tf_op jit(solution)/shard_map/ppermute | solution.py:39
  30.9 7.8 %collective-permute-start.5 = (bf16[144,1024]{1,0:T(8,128)(2,1)S(1)}, bf16[144,1024]{1,0:T(8,128)(2,1)S(1)}, u32[]{:S(2)}, u32[]{:S(2)}) collective-permute-start(bf16[144,1024]{1,0:T(8,128)(2,1)S(1)} %collective-permute-done.3.refs_1_), channel_id=1, source_target_pairs={{0,224},{32,0},{64,32},{96,64},{128,96},{160,128},{192,160},{224,1... | collective-permute-start | bytes 884744 | tf_op jit(solution)/shard_map/ppermute | solution.py:39
  33.6 5.2 %copy-start.9 = (bf16[512,256]{1,0:T(8,128)(2,1)S(1)}, bf16[512,256]{1,0:T(8,128)(2,1)}, u32[]{:S(2)}) copy-start(bf16[512,256]{1,0:T(8,128)(2,1)} %get-tuple-element.53.refs_3_.refs_5_) | copy-start | bytes 786436
  38.8 7.7 %collective-permute-start.9 = (bf16[144,1024]{1,0:T(8,128)(2,1)S(1)}, bf16[144,1024]{1,0:T(8,128)(2,1)S(1)}, u32[]{:S(2)}, u32[]{:S(2)}) collective-permute-start(bf16[144,1024]{1,0:T(8,128)(2,1)S(1)} %collective-permute-done.4.refs_0_), channel_id=1, source_target_pairs={{0,32},{32,64},{64,96},{96,128},{128,160},{160,192},{192,224},{224... | collective-permute-start | bytes 884744 | tf_op jit(solution)/shard_map/ppermute | solution.py:39
  44.9 10.4 %collective-permute-start.10 = (bf16[512,512]{1,0:T(8,128)(2,1)S(1)}, bf16[512,512]{1,0:T(8,128)(2,1)S(1)}, u32[]{:S(2)}, u32[]{:S(2)}) collective-permute-start(bf16[512,512]{1,0:T(8,128)(2,1)S(1)} %get-tuple-element.80), channel_id=1, source_target_pairs={{0,32},{32,0},{64,96},{96,64},{128,160},{160,128},{192,224},{224,1... | collective-permute-start | bytes 1572872 | tf_op jit(solution)/shard_map/ppermute | solution.py:418
  48.6 6.9 %collective-permute-start.11 = (bf16[512,256]{1,0:T(8,128)(2,1)S(1)}, bf16[512,256]{1,0:T(8,128)(2,1)S(1)}, u32[]{:S(2)}, u32[]{:S(2)}) collective-permute-start(bf16[512,256]{1,0:T(8,128)(2,1)S(1)} %get-tuple-element.87), channel_id=1, source_target_pairs={{0,16},{8,24},{16,0},{24,8},{1,17},{9,25},{17,1},{25,9},{2,18},{10... | collective-permute-start | bytes 786440 | tf_op jit(solution)/shard_map/ppermute | solution.py:39
  50.1 8.1 %collective-permute-start.12 = (bf16[512,256]{1,0:T(8,128)(2,1)S(1)}, bf16[512,256]{1,0:T(8,128)(2,1)S(1)}, u32[]{:S(2)}, u32[]{:S(2)}) collective-permute-start(bf16[512,256]{1,0:T(8,128)(2,1)S(1)} %get-tuple-element.88), channel_id=1, source_target_pairs={{0,24},{8,0},{16,8},{24,16},{1,25},{9,1},{17,9},{25,17},{2,26},{10... | collective-permute-start | bytes 786440 | tf_op jit(solution)/shard_map/ppermute | solution.py:39
  51.4 8.6 %collective-permute-start.13 = (bf16[512,256]{1,0:T(8,128)(2,1)S(1)}, bf16[512,256]{1,0:T(8,128)(2,1)S(1)}, u32[]{:S(2)}, u32[]{:S(2)}) collective-permute-start(bf16[512,256]{1,0:T(8,128)(2,1)S(1)} %get-tuple-element.89), channel_id=1, source_target_pairs={{0,8},{8,16},{16,24},{24,0},{1,9},{9,17},{17,25},{25,1},{2,10},{10... | collective-permute-start | bytes 786440 | tf_op jit(solution)/shard_map/ppermute | solution.py:39
  51.6 8.4 %copy-start.6 = (s32[1024,1]{0,1:T(1,128)S(1)}, s32[1024,1]{0,1:T(1,128)}, u32[]{:S(2)}) copy-start(s32[1024,1]{0,1:T(1,128)} %param.19) | copy-start | bytes 12292
  55.4 6.5 %copy-start.10 = (bf16[128,512]{1,0:T(8,128)(2,1)}, bf16[128,512]{1,0:T(8,128)(2,1)S(1)}, u32[]{:S(2)}) copy-start(bf16[128,512]{1,0:T(8,128)(2,1)S(1)} %get-tuple-element.91) | copy-start | bytes 393220
  55.4 6.5 %copy-start.11 = (bf16[128,512]{1,0:T(8,128)(2,1)}, bf16[128,512]{1,0:T(8,128)(2,1)S(1)}, u32[]{:S(2)}) copy-start(bf16[128,512]{1,0:T(8,128)(2,1)S(1)} %get-tuple-element.90) | copy-start | bytes 393220
  55.4 70.4 %copy-start = (bf16[1024,1024]{1,0:T(8,128)(2,1)S(1)}, bf16[1024,1024]{1,0:T(8,128)(2,1)}, u32[]{:S(2)}) copy-start(bf16[1024,1024]{1,0:T(8,128)(2,1)} %wk_ref.1) | copy-start | bytes 6291460
  61.9 33.4 %all-to-all-start = ((bf16[32,32,256]{2,1,0:T(8,128)(2,1)}), bf16[32,32,256]{2,1,0:T(8,128)(2,1)S(1)}, u32[]{:S(2)}, u32[]{:S(2)}) async-start(bf16[32,32,256]{2,1,0:T(8,128)(2,1)} %bitcast.3), calls=%async_computation | async-start | bytes 1048576 | tf_op jit(solution)/shard_map/all_to_all | solution.py:429
  69.9 17.2 %collective-permute-start.14 = (bf16[128,512]{1,0:T(8,128)(2,1)}, bf16[128,512]{1,0:T(8,128)(2,1)S(1)}, u32[]{:S(2)}, u32[]{:S(2)}) collective-permute-start(bf16[128,512]{1,0:T(8,128)(2,1)} %copy-done.11), channel_id=1, source_target_pairs={{0,64},{32,96},{64,128},{96,160},{128,192},{160,224},{192,0},{224,... | collective-permute-start | bytes 393224 | tf_op jit(solution)/shard_map/ppermute | solution.py:39
  72.1 15.0 %collective-permute-start.15 = (bf16[128,512]{1,0:T(8,128)(2,1)}, bf16[128,512]{1,0:T(8,128)(2,1)S(1)}, u32[]{:S(2)}, u32[]{:S(2)}) collective-permute-start(bf16[128,512]{1,0:T(8,128)(2,1)} %copy-done.10), channel_id=1, source_target_pairs={{0,192},{32,224},{64,0},{96,32},{128,64},{160,96},{192,128},{224,1... | collective-permute-start | bytes 393224 | tf_op jit(solution)/shard_map/ppermute | solution.py:39
  73.7 20.9 %collective-permute-start.16 = (bf16[128,512]{1,0:T(8,128)(2,1)S(1)}, bf16[128,512]{1,0:T(8,128)(2,1)S(1)}, u32[]{:S(2)}, u32[]{:S(2)}) collective-permute-start(bf16[128,512]{1,0:T(8,128)(2,1)S(1)} %get-tuple-element.92), channel_id=1, source_target_pairs={{0,128},{32,160},{64,192},{96,224},{128,0},{160,32},{192,64},{224,... | collective-permute-start | bytes 393224 | tf_op jit(solution)/shard_map/ppermute | solution.py:39
  87.1 0.7 copy-start.2
  94.6 0.6 copy-start.4
  95.3 11.5 %collective-permute-start.18 = (bf16[1024,256]{1,0:T(8,128)(2,1)S(1)}, bf16[1024,256]{1,0:T(8,128)(2,1)}, u32[]{:S(2)}, u32[]{:S(2)}) collective-permute-start(bf16[1024,256]{1,0:T(8,128)(2,1)S(1)} %bitcast.5), channel_id=1, source_target_pairs={{0,2},{2,4},{4,6},{6,0},{1,3},{3,5},{5,7},{7,1},{8,10},{10,12},{12... | collective-permute-start | bytes 1572872 | tf_op jit(solution)/shard_map/ppermute | solution.py:39
  96.5 17.1 %collective-permute-start.20 = (bf16[1024,256]{1,0:T(8,128)(2,1)S(1)}, bf16[1024,256]{1,0:T(8,128)(2,1)}, u32[]{:S(2)}, u32[]{:S(2)}) collective-permute-start(bf16[1024,256]{1,0:T(8,128)(2,1)S(1)} %bitcast.6), channel_id=1, source_target_pairs={{0,6},{2,0},{4,2},{6,4},{1,7},{3,1},{5,3},{7,5},{8,14},{10,8},{12,... | collective-permute-start | bytes 1572872 | tf_op jit(solution)/shard_map/ppermute | solution.py:39
  98.0 21.2 %collective-permute-start.22 = (bf16[1024,256]{1,0:T(8,128)(2,1)S(1)}, bf16[1024,256]{1,0:T(8,128)(2,1)}, u32[]{:S(2)}, u32[]{:S(2)}) collective-permute-start(bf16[1024,256]{1,0:T(8,128)(2,1)S(1)} %bitcast.7), channel_id=1, source_target_pairs={{0,4},{2,6},{4,0},{6,2},{1,5},{3,7},{5,1},{7,3},{8,12},{10,14},{12... | collective-permute-start | bytes 1572872 | tf_op jit(solution)/shard_map/ppermute | solution.py:39
  99.5 26.3 %collective-permute-start.17 = (bf16[1024,256]{1,0:T(8,128)(2,1)S(1)}, bf16[1024,256]{1,0:T(8,128)(2,1)S(1)}, u32[]{:S(2)}, u32[]{:S(2)}) collective-permute-start(bf16[1024,256]{1,0:T(8,128)(2,1)S(1)} %bitcast.8), channel_id=1, source_target_pairs={{0,1},{1,0},{2,3},{3,2},{4,5},{5,4},{6,7},{7,6},{8,9},{9,8},{10,11... | collective-permute-start | bytes 1572872 | tf_op jit(solution)/shard_map/ppermute | solution.py:39
  106.8 22.9 %collective-permute-start.19 = (bf16[1024,256]{1,0:T(8,128)(2,1)}, bf16[1024,256]{1,0:T(8,128)(2,1)}, u32[]{:S(2)}, u32[]{:S(2)}) collective-permute-start(bf16[1024,256]{1,0:T(8,128)(2,1)} %collective-permute-done.18.refs_0_), channel_id=1, source_target_pairs={{0,1},{1,0},{2,3},{3,2},{4,5},{5,4},{6,7},{7,6},{8,9},{9,8},{10,11... | collective-permute-start | bytes 1572872 | tf_op jit(solution)/shard_map/ppermute | solution.py:39
  113.6 16.1 %collective-permute-start.21 = (bf16[1024,256]{1,0:T(8,128)(2,1)}, bf16[1024,256]{1,0:T(8,128)(2,1)}, u32[]{:S(2)}, u32[]{:S(2)}) collective-permute-start(bf16[1024,256]{1,0:T(8,128)(2,1)} %collective-permute-done.20.refs_2_), channel_id=1, source_target_pairs={{0,1},{1,0},{2,3},{3,2},{4,5},{5,4},{6,7},{7,6},{8,9},{9,8},{10,11... | collective-permute-start | bytes 1572872 | tf_op jit(solution)/shard_map/ppermute | solution.py:39
  119.1 10.6 %collective-permute-start.23 = (bf16[1024,256]{1,0:T(8,128)(2,1)}, bf16[1024,256]{1,0:T(8,128)(2,1)}, u32[]{:S(2)}, u32[]{:S(2)}) collective-permute-start(bf16[1024,256]{1,0:T(8,128)(2,1)} %collective-permute-done.22.refs_4_), channel_id=1, source_target_pairs={{0,1},{1,0},{2,3},{3,2},{4,5},{5,4},{6,7},{7,6},{8,9},{9,8},{10,11... | collective-permute-start | bytes 1572872 | tf_op jit(solution)/shard_map/ppermute | solution.py:39
  123.2 0.9 copy-start.3
  124.2 0.9 copy-start.5
  125.9 1.6 %copy-start.1 = (bf16[1024,1024]{1,0:T(8,128)(2,1)S(1)}, bf16[1024,1024]{1,0:T(8,128)(2,1)}, u32[]{:S(2)}) copy-start(bf16[1024,1024]{1,0:T(8,128)(2,1)} %wv_ref.1) | copy-start | bytes 6291460

commit v2 on v1

--- a/solution.py
+++ b/solution.py
@@ -17,6 +17,7 @@
 NZ = 8
 NY = 4
 NX = 4
+Z = ("zq", "zp")
 BLOCK = 512
 MSG = 2 * QLEN + 16
 FPD = 32
@@ -34,9 +35,20 @@
 MIDDLE = 12 * 1024 * 1024
 
 
+SIZES = {"z": NZ, "y": NY, "x": NX, "core": 2}
+
+
 def shift(a, axis, k):
-    n = lax.axis_size(axis)
-    return lax.ppermute(a, axis, [(i, (i + k) % n) for i in range(n)])
+    n = SIZES[axis]
+    return lax.ppermute(a, Z if axis == "z" else axis, [(i, (i + k) % n) for i in range(n)])
+
+
+def shift_by_core(a, k):
+    pairs = []
+    for x in range(NX):
+        for core, by in ((0, k), (1, -k)):
+            pairs.append((2 * x + core, 2 * ((x + by) % NX) + core))
+    return lax.ppermute(a, ("x", "core"), pairs)
 
 
 def run_copies(pairs, sems):
@@ -227,29 +239,27 @@
 
 
 def pair_kernel(where_ref, got_ref, *refs):
-    even_refs, keep_ref, send_refs = refs[: len(EVEN)], refs[len(EVEN)], refs[len(EVEN) + 1 :]
-    away = 1 - 2 * ((where_ref[0] // NY) % 2)
+    even_refs, out_ref = refs[: len(EVEN)], refs[len(EVEN)]
+    z = where_ref[0] // NY
+    away = 1 - 2 * (z % 2)
     for i, offset in enumerate(EVEN):
         there = (offset - away + NZ) % NZ
         slot = jnp.int32(0)
         for j, odd in enumerate(ODD):
             slot = jnp.where(there == odd % NZ, j, slot)
         got = got_ref[pl.ds(pl.multiple_of(slot * HD, HD), HD), :].astype(jnp.float32)
+        to = ((z + offset + NZ) % NZ) // 2
         total = even_refs[i][...] + got
-        if i == 0:
-            keep_ref[...] = total
-        else:
-            send_refs[i - 1][...] = total.astype(jnp.bfloat16)
+        out_ref[pl.ds(pl.multiple_of(to * HD, HD), HD), :] = total.astype(jnp.bfloat16)
 
 
 def pair(where, even, got):
     vm = pl.BlockSpec(memory_space=pltpu.VMEM)
     return pl.pallas_call(
         pair_kernel,
-        out_shape=[jax.ShapeDtypeStruct((HD, ROWS), jnp.float32)]
-        + [jax.ShapeDtypeStruct((HD, ROWS), jnp.bfloat16)] * 3,
+        out_shape=jax.ShapeDtypeStruct((len(EVEN) * HD, ROWS), jnp.bfloat16),
         in_specs=[pl.BlockSpec(memory_space=pltpu.SMEM)] + [vm] * 5,
-        out_specs=[vm] * 4,
+        out_specs=vm,
         compiler_params=pltpu.CompilerParams(vmem_limit_bytes=SMALL),
         cost_estimate=pl.CostEstimate(flops=0, bytes_accessed=2 << 20, transcendentals=0),
         name="pair",
@@ -293,80 +303,82 @@
 PIECES = [(dx, other) for dx in (0, -1, 1, 2) for other in (False, True)]
 
 
-def project_first(head, rows, key_weight, value_weight):
-    cols = key_weight.shape[0]
-    feats = KVH * HD
-    tile = 512
-
-    def body(head_ref, a_ref, b_ref, wk_ref, wv_ref, acc_ref, w_ref):
-        x, core = head_ref[0] // 2, head_ref[0] % 2
-        for p, (dx, other) in enumerate(PIECES):
-            h = ((x + dx) % NX) * 2 + (1 - core if other else core)
-            at = pl.ds(pl.multiple_of(h * HD, HD), HD)
-            w_ref[:, 2 * p * HD : (2 * p + 1) * HD] = wk_ref[:, at]
-            w_ref[:, (2 * p + 1) * HD : (2 * p + 2) * HD] = wv_ref[:, at]
-        for t in range(SLOT_ROWS // tile):
-            at = slice(t * tile, (t + 1) * tile)
-            a = jnp.concatenate([a_ref[at, :], b_ref[at, :]], axis=1)
-            acc_ref[at, :] = dot32(a, w_ref[:, 0 : 4 * HD], NT)
-
+def merge_kernel(where_ref, wk_ref, wv_ref, out_ref):
+    x, core = where_ref[1] // 2, where_ref[1] % 2
+    for p, (dx, other) in enumerate(PIECES):
+        by = 1 - core if other else core
+        h = ((x + dx * (1 - 2 * by) + NX) % NX) * 2 + by
+        at = pl.ds(pl.multiple_of(h * HD, HD), HD)
+        out_ref[:, 2 * p * HD : (2 * p + 1) * HD] = wk_ref[:, at]
+        out_ref[:, (2 * p + 1) * HD : (2 * p + 2) * HD] = wv_ref[:, at]
+
+
+def merge(where, key_weight, value_weight):
     vm = pl.BlockSpec(memory_space=pltpu.VMEM)
     return pl.pallas_call(
-        body,
-        out_shape=[
-            jax.ShapeDtypeStruct((SLOT_ROWS, cols), jnp.float32),
-            jax.ShapeDtypeStruct((cols, 2 * feats), jnp.bfloat16),
-        ],
-        in_specs=[pl.BlockSpec(memory_space=pltpu.SMEM)] + [vm] * 4,
-        out_specs=[vm, vm],
+        merge_kernel,
+        out_shape=jax.ShapeDtypeStruct((key_weight.shape[0], 2 * KVH * HD), jnp.bfloat16),
+        in_specs=[pl.BlockSpec(memory_space=pltpu.SMEM), vm, vm],
+        out_specs=vm,
         compiler_params=pltpu.CompilerParams(vmem_limit_bytes=SMALL),
-        cost_estimate=pl.CostEstimate(
-            flops=SLOT_ROWS * cols * feats, bytes_accessed=10 << 20, transcendentals=0
-        ),
-        name="project_first",
-    )(head, *rows, key_weight, value_weight)
-
-
-def project_rest(acc, rows, weight):
+        cost_estimate=pl.CostEstimate(flops=0, bytes_accessed=8 << 20, transcendentals=0),
+        name="merge",
+    )(where, key_weight, value_weight)
+
+
+def project(pieces, weight):
     cols = weight.shape[0]
     tile = 512
+    n_tile = SLOT_ROWS // tile
 
     def body(*refs):
-        acc_ref, w_ref, out_ref = refs[len(rows) :]
-        for t in range(SLOT_ROWS // tile):
-            at = slice(t * tile, (t + 1) * tile)
-            a = jnp.concatenate([ref[at, :] for ref in refs[: len(rows)]], axis=1)
-            out = acc_ref[at, :] + dot32(a, w_ref[:, 4 * HD :], NT)
-            out_ref[at, :] = out.astype(jnp.bfloat16)
-
+        w_ref, out_ref, out_at, sems = refs[KVH:]
+        copies = []
+        for t in range(n_tile):
+            rows = slice(t * tile, (t + 1) * tile)
+            a = jnp.concatenate([ref[rows, :] for ref in refs[:KVH]], axis=1)
+            out_at[rows, :] = dot32(a, w_ref[...], NT).astype(jnp.bfloat16)
+            copy = pltpu.make_async_copy(out_at.at[rows, :], out_ref.at[rows, :], sems.at[t])
+            copy.start()
+            copies.append(copy)
+        for copy in copies:
+            copy.wait()
+
+    vm = pl.BlockSpec(memory_space=pltpu.VMEM)
     return pl.pallas_call(
         body,
         out_shape=jax.ShapeDtypeStruct((SLOT_ROWS, cols), jnp.bfloat16),
+        in_specs=[vm] * (KVH + 1),
+        out_specs=pl.BlockSpec(memory_space=pltpu.HBM),
+        scratch_shapes=[
+            pltpu.VMEM((SLOT_ROWS, cols), jnp.bfloat16),
+            pltpu.SemaphoreType.DMA((n_tile,)),
+        ],
         compiler_params=pltpu.CompilerParams(vmem_limit_bytes=MIDDLE),
         cost_estimate=pl.CostEstimate(
-            flops=3 * SLOT_ROWS * cols * KVH * HD, bytes_accessed=10 << 20, transcendentals=0
+            flops=4 * SLOT_ROWS * cols * KVH * HD, bytes_accessed=10 << 20, transcendentals=0
         ),
-        name="project_rest",
-    )(*rows, acc, weight)
-
-
-def finish_kernel(keep_ref, a_ref, b_ref, c_ref, out_ref):
-    total = keep_ref[...]
-    for ref in (a_ref, b_ref, c_ref):
-        total = total + ref[...].astype(jnp.float32)
+        name="project",
+    )(*pieces, weight)
+
+
+def finish_kernel(part_ref, out_ref):
+    total = part_ref[0:HD, :].astype(jnp.float32)
+    for i in range(1, len(EVEN)):
+        total = total + part_ref[i * HD : (i + 1) * HD, :].astype(jnp.float32)
     total = (total * SCALE).T
     for h in range(GROUP):
         out_ref[:, h * HD : (h + 1) * HD] = total[h * QLEN : (h + 1) * QLEN, :].astype(jnp.bfloat16)
 
 
-def finish(keep, others):
+def finish(parts):
     return pl.pallas_call(
         finish_kernel,
         out_shape=jax.ShapeDtypeStruct((QLEN, GROUP * HD), jnp.bfloat16),
         compiler_params=pltpu.CompilerParams(vmem_limit_bytes=SMALL),
         cost_estimate=pl.CostEstimate(flops=0, bytes_accessed=1 << 19, transcendentals=0),
         name="finish",
-    )(keep, *others)
+    )(parts)
 
 
 def on_device(
@@ -381,9 +393,9 @@
     value_weight,
     frame_owner,
 ):
-    vid = lax.axis_index("z") * NY + lax.axis_index("y")
+    vid = lax.axis_index(Z) * NY + lax.axis_index("y")
     head = lax.axis_index("x") * 2 + lax.axis_index("core")
-    where, head = vid.reshape(1), head.reshape(1)
+    where = jnp.stack([vid, head])
 
     msg, kv0 = pack(
         where, lengths, queries, out_grad, log_totals, out_dots, vis_keys, vis_values
@@ -415,35 +427,38 @@
 
     part_up, part_down, part_far = parts
     back = (shift(part_far, "y", 2), shift(part_up, "y", -1), shift(part_down, "y", 1))
-    got = lax.ppermute(odd, "z", [(i, i ^ 1) for i in range(NZ)])
+    got = lax.ppermute(odd, "zp", [(0, 1), (1, 0)])
     dq, (own,) = attend(
         "home_last", two + [far], [kv0], [own], [dq_u2, dq_d2, dq_4], [f32] * 3, f32, True
     )
     even = [dq_0, dq[1], dq[0], dq[2]]
 
-    keep, *sends = pair(where, even, got)
-    others = [shift(rows, "z", offset) for rows, offset in zip(sends, EVEN[1:])]
-    own, keep = lax.optimization_barrier((own, keep))
+    paired = pair(where, even, got)
+    own, paired = lax.optimization_barrier((own, paired))
 
     outgoing = dispatch(where, frame_owner.reshape(-1), own, back)
-    mine = lax.all_to_all(outgoing, ("z", "y"), split_axis=0, concat_axis=0, tiled=True)
-    mine, *others = lax.optimization_barrier((mine, *others))
-
-    right, left, across = shift(mine, "x", 1), shift(mine, "x", -1), shift(mine, "x", 2)
-    here = [mine, shift(mine, "core", 1)]
-    acc, weight = project_first(head, here, key_weight, value_weight)
-    query_grad = finish(keep, others)
-    pieces = []
-    for rows in (right, left, across):
+    mine = lax.all_to_all(outgoing, Z + ("y",), split_axis=0, concat_axis=0, tiled=True)
+    paired, mine = lax.optimization_barrier((paired, mine))
+
+    first, second = shift_by_core(mine, 1), shift_by_core(mine, -1)
+    pieces = [mine, shift(mine, "core", 1)]
+    first, second = lax.optimization_barrier((first, second))
+    across = shift_by_core(first, 1)
+    for rows in (first, second):
         pieces += [rows, shift(rows, "core", 1)]
-    acc, query_grad = lax.optimization_barrier((acc, query_grad))
-    return query_grad, project_rest(acc, pieces, weight)
+    parts = lax.all_to_all(paired, "zq", split_axis=0, concat_axis=0, tiled=True)
+    query_grad = finish(parts)
+    where, query_grad = lax.optimization_barrier((where, query_grad))
+    weight = merge(where, key_weight, value_weight)
+    across, weight = lax.optimization_barrier((across, weight))
+    pieces += [across, shift(across, "core", 1)]
+    return query_grad, project(pieces, weight)
 
 
 def solution(mesh):
-    devices = mesh.devices.reshape(NZ, NY, NX, 2)
-    split = jax.sharding.Mesh(devices, ("z", "y", "x", "core"))
-    vid, head = ("z", "y"), ("x", "core")
+    devices = mesh.devices.reshape(NZ // 2, 2, NY, NX, 2)
+    split = jax.sharding.Mesh(devices, Z + ("y", "x", "core"))
+    vid, head = Z + ("y",), ("x", "core")
     in_specs = (
         P(vid, head),
         P(vid, head),

time: 137 us -> 128 us (0.934)
  blocking collectives: 0 us -> 22.1 us
  starting transfers between devices: 58.3 us -> 41.6 us
  waiting for transfers between devices: 33.5 us -> 20 us
  local copies, waits for them, and re-layouts: 6.63 us -> 3.52 us
  Pallas kernels: 37.1 us -> 38.5 us
    all_to_all x0 -> x1, blocking collectives: none -> 22.1 us  [on_device(): lax.all_to_all(outgoing, Z + ('y',), split_axis=0, concat_axis=0, tiled=T...]
    ppermute x24 -> x21, waiting for transfers between devices: 33.5 us -> 20 us  [the longest x17 13.5 us: shift(): lax.ppermute(a, Z if axis == 'z' else axis, [(i, (i + k) % n) for i in ra...]
    ppermute x24 -> x21, starting transfers between devices: 50.3 us -> 38.1 us  [the longest x17 32.9 us: shift(): lax.ppermute(a, Z if axis == 'z' else axis, [(i, (i + k) % n) for i in ra...]
    all_to_all x1, starting transfers between devices: 8.03 us -> 3.54 us  [on_device(): lax.all_to_all(paired, 'zq', split_axis=0, concat_axis=0, tiled=True)]
    unnamed x24 -> x14, local copies, waits for them, and re-layouts: 6.63 us -> 3.52 us
    pallas_call x3, Pallas kernels: 9 us -> 10.6 us  [the longest x1 7.35 us: project(): pl.pallas_call(body, out_shape=jax.ShapeDtypeStruct((SLOT_ROWS, cols), jn...]
  transfers between devices with their start and end apart: 25 -> 22, of which waited for: 10 -> 8; matrix products, arithmetic and copies ran while one was open for 0% -> 0% of each run, Pallas kernels for 19% -> 21%
where the time goes in v2:
time: 128 us; the launch traced here: 127 us
  starting transfers between devices  41.6 us (32%)
  Pallas kernels  38.5 us (30%)
  blocking collectives  22.1 us (17%)
  waiting for transfers between devices  20 us (16%)
  local copies, waits for them, and re-layouts  3.52 us (3%)
    ppermute x17, starting transfers between devices, shift(): lax.ppermute(a, Z if axis == 'z' else axis, [(i, (i + k) % n) for i in ra...  32.9 us
    pallas_call x6, Pallas kernels, attend(): pl.pallas_call(body, out_shape=out_shape, scratch_shapes=message_scratch(...  23.4 us
    all_to_all x1, blocking collectives, on_device(): lax.all_to_all(outgoing, Z + ('y',), split_axis=0, concat_axis=0, tiled=T...  22.1 us
    ppermute x17, waiting for transfers between devices, shift(): lax.ppermute(a, Z if axis == 'z' else axis, [(i, (i + k) % n) for i in ra...  13.5 us
    pallas_call x1, Pallas kernels, project(): pl.pallas_call(body, out_shape=jax.ShapeDtypeStruct((SLOT_ROWS, cols), jn...  7.35 us
    ppermute x3, waiting for transfers between devices, shift_by_core(): return lax.ppermute(a, ('x', 'core'), pairs)  6.53 us
    ppermute x3, starting transfers between devices, shift_by_core(): return lax.ppermute(a, ('x', 'core'), pairs)  4.31 us
    all_to_all x1, starting transfers between devices, on_device(): lax.all_to_all(paired, 'zq', split_axis=0, concat_axis=0, tiled=True)  3.54 us
  transfers between devices with their start and end apart: 22, of which 8 were waited for; matrix products, arithmetic and copies ran while one was open for 0% of the time, Pallas kernels for 21%

profile of v2, /device:TPU:1, one launch (start us, length us, event | category | flops | bytes accessed | tf_op | source)
XLA Modules:
  0.0 127.4 jit_solution(11550083863319312309)
XLA Ops:
  0.6 0.6 pad_add_fusion.where_ref
  1.3 2.6 %pack.1 = (bf16[144,1024]{1,0:T(8,128)(2,1)}, bf16[512,256]{1,0:T(8,128)(2,1)}) custom-call(s32[2]{0:T(128)} %pad_add_fusion.where_ref, s32[32]{0:T(128)} %len_ref.1, bf16[64,1024]{1,0:T(8,128)(2,1)} %q_ref.1, bf16[64,1024]{1,0:T(8,128)(2,1)} %g_ref.1, bf16[8,64]{1,0:T(8,128)(2,1)} %total_ref.1, bf16[8,64]{1,0:T(8,128)(2,1)} %dot_ref.1, ...), custom_call_target="tpu_custom_call" | custom-call | bytes 1048576 | tf_op jit(solution)/shard_map/pack/pallas_call | solution.py:94
  3.9 6.5 %collective-permute-start.2 = (bf16[144,1024]{1,0:T(8,128)(2,1)}, bf16[144,1024]{1,0:T(8,128)(2,1)S(1)}, u32[]{:S(2)}, u32[]{:S(2)}) collective-permute-start(bf16[144,1024]{1,0:T(8,128)(2,1)} %get-tuple-element.48.refs_0_), channel_id=1, source_target_pairs={{0,224},{32,0},{64,32},{96,64},{128,96},{160,128},{192,160},{224,1... | collective-permute-start | bytes 884744 | tf_op jit(solution)/shard_map/ppermute | solution.py:43
  10.4 0.0 collective-permute-start
  10.4 2.9 %collective-permute-start.8 = (bf16[512,256]{1,0:T(8,128)(2,1)}, bf16[512,256]{1,0:T(8,128)(2,1)S(1)}, u32[]{:S(2)}, u32[]{:S(2)}) collective-permute-start(bf16[512,256]{1,0:T(8,128)(2,1)} %get-tuple-element.49.refs_3_.refs_5_), channel_id=1, source_target_pairs={{0,16},{8,24},{16,0},{24,8},{1,17},{9,25},{17,1},{25,9},{2,18},{10... | collective-permute-start | bytes 786440 | tf_op jit(solution)/shard_map/ppermute | solution.py:43
  13.3 0.8 collective-permute-start.7
  14.1 0.7 collective-permute-start.6
  14.8 1.6 %collective-permute-done.2.refs_2_ = bf16[144,1024]{1,0:T(8,128)(2,1)S(1)} collective-permute-done((bf16[144,1024]{1,0:T(8,128)(2,1)}, bf16[144,1024]{1,0:T(8,128)(2,1)S(1)}, u32[]{:S(2)}, u32[]{:S(2)}) %collective-permute-start.2) | collective-permute-done | bytes 294944 | tf_op jit(solution)/shard_map/ppermute | solution.py:43
  16.4 3.3 %collective-permute-start.3 = (bf16[144,1024]{1,0:T(8,128)(2,1)S(1)}, bf16[144,1024]{1,0:T(8,128)(2,1)S(1)}, u32[]{:S(2)}, u32[]{:S(2)}) collective-permute-start(bf16[144,1024]{1,0:T(8,128)(2,1)S(1)} %collective-permute-done.2.refs_2_), channel_id=1, source_target_pairs={{0,224},{32,0},{64,32},{96,64},{128,96},{160,128},{192,160},{224,1... | collective-permute-start | bytes 884744 | tf_op jit(solution)/shard_map/ppermute | solution.py:43
  19.7 0.0 collective-permute-done.refs_1_
  19.7 0.0 collective-permute-start.1
  19.7 1.0 copy-done.4
  20.7 0.9 copy-done.5
  21.6 2.1 %home_first.1 = (f32[128,512]{1,0:T(8,128)S(1)}, f32[128,512]{1,0:T(8,128)S(1)}, f32[128,512]{1,0:T(8,128)S(1)}, f32[512,256]{1,0:T(8,128)S(1)}) custom-call(bf16[144,1024]{1,0:T(8,128)(2,1)S(1)} %copy-done.4, bf16[144,1024]{1,0:T(8,128)(2,1)S(1)} %collective-permute-done.refs_1_, bf16[144,1024]{1,0:T(8,128)(2,1)S(1)} %collective-permute-done.2.refs_2_, ...), custom_call_target="tpu_custom_call" | custom-call | flops 2013265920 | bytes 2097152 | tf_op jit(solution)/shard_map/home_first/pallas_call | solution.py:221
  23.7 0.0 collective-permute-done.8.refs_5_.refs_4_.refs_3_
  23.7 1.7 %collective-permute-done.7.refs_4_.refs_3_.refs_2_ = bf16[512,256]{1,0:T(8,128)(2,1)S(1)} collective-permute-done((bf16[512,256]{1,0:T(8,128)(2,1)}, bf16[512,256]{1,0:T(8,128)(2,1)S(1)}, u32[]{:S(2)}, u32[]{:S(2)}) %collective-permute-start.7) | collective-permute-done | bytes 262176 | tf_op jit(solution)/shard_map/ppermute | solution.py:43
  25.4 0.0 collective-permute-done.6.refs_3_.refs_2_.refs_1_
  25.4 6.5 %away_near.1 = (f32[128,512]{1,0:T(8,128)S(1)}, bf16[128,512]{1,0:T(8,128)(2,1)S(1)}, bf16[128,512]{1,0:T(8,128)(2,1)S(1)}, f32[512,256]{1,0:T(8,128)S(1)}, f32[...) custom-call(bf16[144,1024]{1,0:T(8,128)(2,1)S(1)} %copy-done.4, bf16[144,1024]{1,0:T(8,128)(2,1)S(1)} %collective-permute-done.refs_1_, ...), custom_call_target="tpu_custom_call" | custom-call | flops 6039797760 | bytes 2097152 | tf_op jit(solution)/shard_map/away_near/pallas_call | solution.py:221
  31.9 0.0 collective-permute-done.3.refs_1_
  31.9 0.0 collective-permute-done.1.refs_0_
  31.9 0.1 collective-permute-start.4
  32.0 2.9 %collective-permute-start.5 = (bf16[144,1024]{1,0:T(8,128)(2,1)S(1)}, bf16[144,1024]{1,0:T(8,128)(2,1)S(1)}, u32[]{:S(2)}, u32[]{:S(2)}) collective-permute-start(bf16[144,1024]{1,0:T(8,128)(2,1)S(1)} %collective-permute-done.3.refs_1_), channel_id=1, source_target_pairs={{0,224},{32,0},{64,32},{96,64},{128,96},{160,128},{192,160},{224,1... | collective-permute-start | bytes 884744 | tf_op jit(solution)/shard_map/ppermute | solution.py:43
  34.9 4.6 %away_two.1 = (f32[128,512]{1,0:T(8,128)S(1)}, f32[128,512]{1,0:T(8,128)S(1)}, f32[512,256]{1,0:T(8,128)S(1)}, f32[512,256]{1,0:T(8,128)S(1)}, f32[512,256]{1,0:T(8,128)S(1)}) custom-call(bf16[144,1024]{1,0:T(8,128)(2,1)S(1)} %collective-permute-done.1.refs_0_, bf16[144,1024]{1,0:T(8,128)(2,1)S(1)} %collective-permute-done.3.refs_1_, ...), custom_call_target="tpu_custom_call" | custom-call | flops 4026531840 | bytes 2097152 | tf_op jit(solution)/shard_map/away_two/pallas_call | solution.py:221
  39.5 0.7 collective-permute-done.4.refs_0_
  40.3 0.0 collective-permute-done.5.refs_1_
  40.3 0.0 collective-permute-start.9
  40.3 0.0 copy-done.6
  40.3 6.1 %all_three.1 = (bf16[512,512]{1,0:T(8,128)(2,1)S(1)}, f32[512,256]{1,0:T(8,128)S(1)}, f32[512,256]{1,0:T(8,128)S(1)}, f32[512,256]{1,0:T(8,128)S(1)}, f32[512,256]{1,0:T(8,128)S(1)}) custom-call(bf16[144,1024]{1,0:T(8,128)(2,1)S(1)} %collective-permute-done.4.refs_0_, bf16[144,1024]{1,0:T(8,128)(2,1)S(1)} %collective-permute-done.5.refs_1_, ...), custom_call_target="tpu_custom_call" | custom-call | flops 5368709120 | bytes 2097152 | tf_op jit(solution)/shard_map/all_three/pallas_call | solution.py:221
  46.3 0.8 collective-permute-start.10
  47.2 0.9 collective-permute-done.9.refs_0_.refs_2_
  48.1 2.2 %away_far.1 = (f32[128,512]{1,0:T(8,128)S(1)}, bf16[512,256]{1,0:T(8,128)(2,1)S(1)}, bf16[512,256]{1,0:T(8,128)(2,1)S(1)}, bf16[512,256]{1,0:T(8,128)(2,1)S(1)}) custom-call(bf16[144,1024]{1,0:T(8,128)(2,1)S(1)} %collective-permute-done.9.refs_0_.refs_2_, bf16[512,256]{1,0:T(8,128)(2,1)S(1)} %collective-permute-done.6.refs_3_.refs_2_.refs_1_, ...), custom_call_target="tpu_custom_call" | custom-call | flops 2013265920 | bytes 2097152 | tf_op jit(solution)/shard_map/away_far/pallas_call | solution.py:221
  50.2 5.6 %collective-permute-start.11 = (bf16[512,256]{1,0:T(8,128)(2,1)S(1)}, bf16[512,256]{1,0:T(8,128)(2,1)S(1)}, u32[]{:S(2)}, u32[]{:S(2)}) collective-permute-start(bf16[512,256]{1,0:T(8,128)(2,1)S(1)} %get-tuple-element.83), channel_id=1, source_target_pairs={{0,16},{8,24},{16,0},{24,8},{1,17},{9,25},{17,1},{25,9},{2,18},{10... | collective-permute-start | bytes 786440 | tf_op jit(solution)/shard_map/ppermute | solution.py:43
  55.9 0.4 collective-permute-start.12
  56.3 1.0 collective-permute-start.13
  57.3 2.1 %home_last.1 = (f32[128,512]{1,0:T(8,128)S(1)}, f32[128,512]{1,0:T(8,128)S(1)}, f32[128,512]{1,0:T(8,128)S(1)}, f32[512,256]{1,0:T(8,128)S(1)}) custom-call(bf16[144,1024]{1,0:T(8,128)(2,1)S(1)} %collective-permute-done.1.refs_0_, bf16[144,1024]{1,0:T(8,128)(2,1)S(1)} %collective-permute-done.3.refs_1_, ...), custom_call_target="tpu_custom_call" | custom-call | flops 2013265920 | bytes 2097152 | tf_op jit(solution)/shard_map/home_last/pallas_call | solution.py:221
  59.4 0.0 copy-start.3
  59.4 0.0 collective-permute-done.10.got_ref
  59.4 0.0 copy-done.2
  59.4 1.5 %pair.1 = bf16[512,512]{1,0:T(8,128)(2,1)} custom-call(s32[2]{0:T(128)S(1)} %copy-done.2, bf16[512,512]{1,0:T(8,128)(2,1)S(1)} %collective-permute-done.10.got_ref, f32[128,512]{1,0:T(8,128)S(1)} %get-tuple-element.77.refs_0_, f32[128,512]{1,0:T(8,128)S(1)} %get-tuple-element.78.refs_1_, f32[128,512]{1,0:T(8,128)S(1)} %get-tuple-element.79.refs_2_, ...), custom_call_target="tpu_custom_call" | custom-call | bytes 2097152 | tf_op jit(solution)/shard_map/pair/pallas_call | solution.py:258
  60.9 0.0 collective-permute-done.11.a_ref
  60.9 6.8 %collective-permute-done.12.b_ref = bf16[512,256]{1,0:T(8,128)(2,1)S(1)} collective-permute-done((bf16[512,256]{1,0:T(8,128)(2,1)S(1)}, bf16[512,256]{1,0:T(8,128)(2,1)S(1)}, u32[]{:S(2)}, u32[]{:S(2)}) %collective-permute-start.12) | collective-permute-done | bytes 262176 | tf_op jit(solution)/shard_map/ppermute | solution.py:43
  67.7 0.0 collective-permute-done.13.c_ref
  67.7 1.2 dispatch.1
  68.8 22.1 %all_to_all.23 = bf16[32,32,256]{2,1,0:T(8,128)(2,1)S(1)} all-to-all(bf16[32,32,256]{2,1,0:T(8,128)(2,1)S(1)} %bitcast.8), channel_id=1, replica_groups=mesh['zq'=4,'zp'=2,'y'=4,'x'=4,'core'=2] {'zq','zp','y'}, dimensions={0} | all-to-all | bytes 1048576 | tf_op jit(solution)/shard_map/all_to_all | solution.py:440
  90.9 1.3 %collective-permute-start.16 = (bf16[1024,256]{1,0:T(8,128)(2,1)S(1)}, bf16[1024,256]{1,0:T(8,128)(2,1)}, u32[]{:S(2)}, u32[]{:S(2)}) collective-permute-start(bf16[1024,256]{1,0:T(8,128)(2,1)S(1)} %bitcast.9), channel_id=1, source_target_pairs={{0,6},{1,3},{2,0},{3,5},{4,2},{5,7},{6,4},{7,1},{8,14},{9,11},{10,... | collective-permute-start | bytes 1572872 | tf_op jit(solution)/shard_map/ppermute | solution.py:51
  92.2 1.4 %collective-permute-start.15 = (bf16[1024,256]{1,0:T(8,128)(2,1)S(1)}, bf16[1024,256]{1,0:T(8,128)(2,1)}, u32[]{:S(2)}, u32[]{:S(2)}) collective-permute-start(bf16[1024,256]{1,0:T(8,128)(2,1)S(1)} %bitcast.10), channel_id=1, source_target_pairs={{0,2},{1,7},{2,4},{3,1},{4,6},{5,3},{6,0},{7,5},{8,10},{9,15},{10,... | collective-permute-start | bytes 1572872 | tf_op jit(solution)/shard_map/ppermute | solution.py:51
  93.6 3.5 %all-to-all-start.1 = ((bf16[4,128,512]{2,1,0:T(8,128)(2,1)}), bf16[4,128,512]{2,1,0:T(8,128)(2,1)S(1)}, u32[]{:S(2)}, u32[]{:S(2)}) async-start(bf16[4,128,512]{2,1,0:T(8,128)(2,1)} %bitcast.5), calls=%async_computation.1 | async-start | bytes 1048576 | tf_op jit(solution)/shard_map/all_to_all | solution.py:449
  97.1 3.1 %collective-permute-done.16.refs_4_ = bf16[1024,256]{1,0:T(8,128)(2,1)} collective-permute-done((bf16[1024,256]{1,0:T(8,128)(2,1)S(1)}, bf16[1024,256]{1,0:T(8,128)(2,1)}, u32[]{:S(2)}, u32[]{:S(2)}) %collective-permute-start.16) | collective-permute-done | bytes 524320 | tf_op jit(solution)/shard_map/ppermute | solution.py:51
  100.3 3.4 %collective-permute-done.15.refs_2_ = bf16[1024,256]{1,0:T(8,128)(2,1)} collective-permute-done((bf16[1024,256]{1,0:T(8,128)(2,1)S(1)}, bf16[1024,256]{1,0:T(8,128)(2,1)}, u32[]{:S(2)}, u32[]{:S(2)}) %collective-permute-start.15) | collective-permute-done | bytes 524320 | tf_op jit(solution)/shard_map/ppermute | solution.py:51
  103.7 1.6 %collective-permute-start.19 = (bf16[1024,256]{1,0:T(8,128)(2,1)}, bf16[1024,256]{1,0:T(8,128)(2,1)}, u32[]{:S(2)}, u32[]{:S(2)}) collective-permute-start(bf16[1024,256]{1,0:T(8,128)(2,1)} %collective-permute-done.15.refs_2_), channel_id=1, source_target_pairs={{0,2},{1,7},{2,4},{3,1},{4,6},{5,3},{6,0},{7,5},{8,10},{9,15},{10,... | collective-permute-start | bytes 1572872 | tf_op jit(solution)/shard_map/ppermute | solution.py:51
  105.3 2.8 %collective-permute-start.14 = (bf16[1024,256]{1,0:T(8,128)(2,1)S(1)}, bf16[1024,256]{1,0:T(8,128)(2,1)}, u32[]{:S(2)}, u32[]{:S(2)}) collective-permute-start(bf16[1024,256]{1,0:T(8,128)(2,1)S(1)} %bitcast.11), channel_id=1, source_target_pairs={{0,1},{1,0},{2,3},{3,2},{4,5},{5,4},{6,7},{7,6},{8,9},{9,8},{10,11... | collective-permute-start | bytes 1572872 | tf_op jit(solution)/shard_map/ppermute | solution.py:43
  108.1 0.0 collective-permute-start.17
  108.1 0.5 collective-permute-start.18
  108.7 0.0 all-to-all-done.1
  108.7 0.8 finish.1
  109.5 1.6 %copy-done.1 = bf16[1024,1024]{1,0:T(8,128)(2,1)S(1)} copy-done((bf16[1024,1024]{1,0:T(8,128)(2,1)S(1)}, bf16[1024,1024]{1,0:T(8,128)(2,1)}, u32[]{:S(2)}) %copy-start.1) | copy-done | bytes 2097176
  111.1 1.8 %merge.1.refs_8_ = bf16[1024,2048]{1,0:T(8,128)(2,1)S(1)} custom-call(s32[2]{0:T(128)S(1)} %copy-done.2, bf16[1024,1024]{1,0:T(8,128)(2,1)S(1)} %copy-done, bf16[1024,1024]{1,0:T(8,128)(2,1)S(1)} %copy-done.1), custom_call_target="tpu_custom_call" | custom-call | bytes 8388608 | tf_op jit(solution)/shard_map/merge/pallas_call | solution.py:318
  112.8 0.0 collective-permute-done.19.refs_6_
  112.8 5.3 %collective-permute-start.20 = (bf16[1024,256]{1,0:T(8,128)(2,1)}, bf16[1024,256]{1,0:T(8,128)(2,1)S(1)}, u32[]{:S(2)}, u32[]{:S(2)}) collective-permute-start(bf16[1024,256]{1,0:T(8,128)(2,1)} %collective-permute-done.19.refs_6_), channel_id=1, source_target_pairs={{0,1},{1,0},{2,3},{3,2},{4,5},{5,4},{6,7},{7,6},{8,9},{9,8},{10,11... | collective-permute-start | bytes 1572872 | tf_op jit(solution)/shard_map/ppermute | solution.py:43
  118.1 0.0 collective-permute-done.14.refs_1_
  118.1 0.0 collective-permute-done.18.refs_5_
  118.1 0.0 collective-permute-done.17.refs_3_
  118.1 1.7 %collective-permute-done.20.refs_7_ = bf16[1024,256]{1,0:T(8,128)(2,1)S(1)} collective-permute-done((bf16[1024,256]{1,0:T(8,128)(2,1)}, bf16[1024,256]{1,0:T(8,128)(2,1)S(1)}, u32[]{:S(2)}, u32[]{:S(2)}) %collective-permute-start.20) | collective-permute-done | bytes 524320 | tf_op jit(solution)/shard_map/ppermute | solution.py:43
  119.8 7.3 %project.1 = bf16[1024,1024]{1,0:T(8,128)(2,1)} custom-call(bf16[1024,256]{1,0:T(8,128)(2,1)S(1)} %bitcast.12, bf16[1024,256]{1,0:T(8,128)(2,1)} %collective-permute-done.14.refs_1_, bf16[1024,256]{1,0:T(8,128)(2,1)} %collective-permute-done.15.refs_2_, bf16[1024,256]{1,0:T(8,128)(2,1)} %collective-permute-done.17.refs_3_, ...), custom_call_target="tpu_custom_call" | custom-call | flops 4294967296 | bytes 10485760 | tf_op jit(solution)/shard_map/project/pallas_call | solution.py:348
  (8 shorter events, 0.0 us)
Async XLA Ops:
  3.9 12.5 %collective-permute-start.2 = (bf16[144,1024]{1,0:T(8,128)(2,1)}, bf16[144,1024]{1,0:T(8,128)(2,1)S(1)}, u32[]{:S(2)}, u32[]{:S(2)}) collective-permute-start(bf16[144,1024]{1,0:T(8,128)(2,1)} %get-tuple-element.48.refs_0_), channel_id=1, source_target_pairs={{0,224},{32,0},{64,32},{96,64},{128,96},{160,128},{192,160},{224,1... | collective-permute-start | bytes 884744 | tf_op jit(solution)/shard_map/ppermute | solution.py:43
  10.4 9.3 %collective-permute-start = (bf16[144,1024]{1,0:T(8,128)(2,1)}, bf16[144,1024]{1,0:T(8,128)(2,1)S(1)}, u32[]{:S(2)}, u32[]{:S(2)}) collective-permute-start(bf16[144,1024]{1,0:T(8,128)(2,1)} %get-tuple-element.48.refs_0_), channel_id=1, source_target_pairs={{0,32},{32,64},{64,96},{96,128},{128,160},{160,192},{192,224},{224... | collective-permute-start | bytes 884744 | tf_op jit(solution)/shard_map/ppermute | solution.py:43
  10.4 13.3 %collective-permute-start.8 = (bf16[512,256]{1,0:T(8,128)(2,1)}, bf16[512,256]{1,0:T(8,128)(2,1)S(1)}, u32[]{:S(2)}, u32[]{:S(2)}) collective-permute-start(bf16[512,256]{1,0:T(8,128)(2,1)} %get-tuple-element.49.refs_3_.refs_5_), channel_id=1, source_target_pairs={{0,16},{8,24},{16,0},{24,8},{1,17},{9,25},{17,1},{25,9},{2,18},{10... | collective-permute-start | bytes 786440 | tf_op jit(solution)/shard_map/ppermute | solution.py:43
  13.3 12.1 %collective-permute-start.7 = (bf16[512,256]{1,0:T(8,128)(2,1)}, bf16[512,256]{1,0:T(8,128)(2,1)S(1)}, u32[]{:S(2)}, u32[]{:S(2)}) collective-permute-start(bf16[512,256]{1,0:T(8,128)(2,1)} %get-tuple-element.49.refs_3_.refs_5_), channel_id=1, source_target_pairs={{0,24},{8,0},{16,8},{24,16},{1,25},{9,1},{17,9},{25,17},{2,26},{10... | collective-permute-start | bytes 786440 | tf_op jit(solution)/shard_map/ppermute | solution.py:43
  14.1 11.3 %collective-permute-start.6 = (bf16[512,256]{1,0:T(8,128)(2,1)}, bf16[512,256]{1,0:T(8,128)(2,1)S(1)}, u32[]{:S(2)}, u32[]{:S(2)}) collective-permute-start(bf16[512,256]{1,0:T(8,128)(2,1)} %get-tuple-element.49.refs_3_.refs_5_), channel_id=1, source_target_pairs={{0,8},{8,16},{16,24},{24,0},{1,9},{9,17},{17,25},{25,1},{2,10},{10... | collective-permute-start | bytes 786440 | tf_op jit(solution)/shard_map/ppermute | solution.py:43
  16.4 15.5 %collective-permute-start.3 = (bf16[144,1024]{1,0:T(8,128)(2,1)S(1)}, bf16[144,1024]{1,0:T(8,128)(2,1)S(1)}, u32[]{:S(2)}, u32[]{:S(2)}) collective-permute-start(bf16[144,1024]{1,0:T(8,128)(2,1)S(1)} %collective-permute-done.2.refs_2_), channel_id=1, source_target_pairs={{0,224},{32,0},{64,32},{96,64},{128,96},{160,128},{192,160},{224,1... | collective-permute-start | bytes 884744 | tf_op jit(solution)/shard_map/ppermute | solution.py:43
  19.7 12.2 %collective-permute-start.1 = (bf16[144,1024]{1,0:T(8,128)(2,1)S(1)}, bf16[144,1024]{1,0:T(8,128)(2,1)S(1)}, u32[]{:S(2)}, u32[]{:S(2)}) collective-permute-start(bf16[144,1024]{1,0:T(8,128)(2,1)S(1)} %collective-permute-done.refs_1_), channel_id=1, source_target_pairs={{0,32},{32,64},{64,96},{96,128},{128,160},{160,192},{192,224},{224... | collective-permute-start | bytes 884744 | tf_op jit(solution)/shard_map/ppermute | solution.py:43
  19.7 1.0 copy-start.4
  20.7 0.9 copy-start.5
  31.9 8.3 %collective-permute-start.4 = (bf16[144,1024]{1,0:T(8,128)(2,1)S(1)}, bf16[144,1024]{1,0:T(8,128)(2,1)S(1)}, u32[]{:S(2)}, u32[]{:S(2)}) collective-permute-start(bf16[144,1024]{1,0:T(8,128)(2,1)S(1)} %collective-permute-done.1.refs_0_), channel_id=1, source_target_pairs={{0,32},{32,64},{64,96},{96,128},{128,160},{160,192},{192,224},{224... | collective-permute-start | bytes 884744 | tf_op jit(solution)/shard_map/ppermute | solution.py:43
  32.0 8.2 %collective-permute-start.5 = (bf16[144,1024]{1,0:T(8,128)(2,1)S(1)}, bf16[144,1024]{1,0:T(8,128)(2,1)S(1)}, u32[]{:S(2)}, u32[]{:S(2)}) collective-permute-start(bf16[144,1024]{1,0:T(8,128)(2,1)S(1)} %collective-permute-done.3.refs_1_), channel_id=1, source_target_pairs={{0,224},{32,0},{64,32},{96,64},{128,96},{160,128},{192,160},{224,1... | collective-permute-start | bytes 884744 | tf_op jit(solution)/shard_map/ppermute | solution.py:43
  34.9 5.3 %copy-start.6 = (bf16[512,256]{1,0:T(8,128)(2,1)S(1)}, bf16[512,256]{1,0:T(8,128)(2,1)}, u32[]{:S(2)}) copy-start(bf16[512,256]{1,0:T(8,128)(2,1)} %get-tuple-element.49.refs_3_.refs_5_) | copy-start | bytes 786436
  40.3 7.8 %collective-permute-start.9 = (bf16[144,1024]{1,0:T(8,128)(2,1)S(1)}, bf16[144,1024]{1,0:T(8,128)(2,1)S(1)}, u32[]{:S(2)}, u32[]{:S(2)}) collective-permute-start(bf16[144,1024]{1,0:T(8,128)(2,1)S(1)} %collective-permute-done.4.refs_0_), channel_id=1, source_target_pairs={{0,32},{32,64},{64,96},{96,128},{128,160},{160,192},{192,224},{224... | collective-permute-start | bytes 884744 | tf_op jit(solution)/shard_map/ppermute | solution.py:43
  46.3 13.1 %collective-permute-start.10 = (bf16[512,512]{1,0:T(8,128)(2,1)S(1)}, bf16[512,512]{1,0:T(8,128)(2,1)S(1)}, u32[]{:S(2)}, u32[]{:S(2)}) collective-permute-start(bf16[512,512]{1,0:T(8,128)(2,1)S(1)} %get-tuple-element.76), channel_id=1, source_target_pairs={{0,32},{32,0},{1,33},{33,1},{2,34},{34,2},{3,35},{35,3},{4,36},{36... | collective-permute-start | bytes 1572872 | tf_op jit(solution)/shard_map/ppermute | solution.py:430
  50.2 10.7 %collective-permute-start.11 = (bf16[512,256]{1,0:T(8,128)(2,1)S(1)}, bf16[512,256]{1,0:T(8,128)(2,1)S(1)}, u32[]{:S(2)}, u32[]{:S(2)}) collective-permute-start(bf16[512,256]{1,0:T(8,128)(2,1)S(1)} %get-tuple-element.83), channel_id=1, source_target_pairs={{0,16},{8,24},{16,0},{24,8},{1,17},{9,25},{17,1},{25,9},{2,18},{10... | collective-permute-start | bytes 786440 | tf_op jit(solution)/shard_map/ppermute | solution.py:43
  55.9 11.8 %collective-permute-start.12 = (bf16[512,256]{1,0:T(8,128)(2,1)S(1)}, bf16[512,256]{1,0:T(8,128)(2,1)S(1)}, u32[]{:S(2)}, u32[]{:S(2)}) collective-permute-start(bf16[512,256]{1,0:T(8,128)(2,1)S(1)} %get-tuple-element.84), channel_id=1, source_target_pairs={{0,24},{8,0},{16,8},{24,16},{1,25},{9,1},{17,9},{25,17},{2,26},{10... | collective-permute-start | bytes 786440 | tf_op jit(solution)/shard_map/ppermute | solution.py:43
  56.3 11.4 %collective-permute-start.13 = (bf16[512,256]{1,0:T(8,128)(2,1)S(1)}, bf16[512,256]{1,0:T(8,128)(2,1)S(1)}, u32[]{:S(2)}, u32[]{:S(2)}) collective-permute-start(bf16[512,256]{1,0:T(8,128)(2,1)S(1)} %get-tuple-element.85), channel_id=1, source_target_pairs={{0,8},{8,16},{16,24},{24,0},{1,9},{9,17},{17,25},{25,1},{2,10},{10... | collective-permute-start | bytes 786440 | tf_op jit(solution)/shard_map/ppermute | solution.py:43
  57.3 2.1 %copy-start.2 = (s32[2]{0:T(128)S(1)}, s32[2]{0:T(128)}, u32[]{:S(2)}) copy-start(s32[2]{0:T(128)} %pad_add_fusion.where_ref) | copy-start | bytes 28
  59.4 8.3 %copy-start.3 = (s32[1024,1]{0,1:T(1,128)S(1)}, s32[1024,1]{0,1:T(1,128)}, u32[]{:S(2)}) copy-start(s32[1024,1]{0,1:T(1,128)} %param.19) | copy-start | bytes 12292
  67.7 41.8 %copy-start = (bf16[1024,1024]{1,0:T(8,128)(2,1)S(1)}, bf16[1024,1024]{1,0:T(8,128)(2,1)}, u32[]{:S(2)}) copy-start(bf16[1024,1024]{1,0:T(8,128)(2,1)} %wk_ref.1) | copy-start | bytes 6291460
  90.9 9.3 %collective-permute-start.16 = (bf16[1024,256]{1,0:T(8,128)(2,1)S(1)}, bf16[1024,256]{1,0:T(8,128)(2,1)}, u32[]{:S(2)}, u32[]{:S(2)}) collective-permute-start(bf16[1024,256]{1,0:T(8,128)(2,1)S(1)} %bitcast.9), channel_id=1, source_target_pairs={{0,6},{1,3},{2,0},{3,5},{4,2},{5,7},{6,4},{7,1},{8,14},{9,11},{10,... | collective-permute-start | bytes 1572872 | tf_op jit(solution)/shard_map/ppermute | solution.py:51
  92.2 11.5 %collective-permute-start.15 = (bf16[1024,256]{1,0:T(8,128)(2,1)S(1)}, bf16[1024,256]{1,0:T(8,128)(2,1)}, u32[]{:S(2)}, u32[]{:S(2)}) collective-permute-start(bf16[1024,256]{1,0:T(8,128)(2,1)S(1)} %bitcast.10), channel_id=1, source_target_pairs={{0,2},{1,7},{2,4},{3,1},{4,6},{5,3},{6,0},{7,5},{8,10},{9,15},{10,... | collective-permute-start | bytes 1572872 | tf_op jit(solution)/shard_map/ppermute | solution.py:51
  93.6 15.1 %all-to-all-start.1 = ((bf16[4,128,512]{2,1,0:T(8,128)(2,1)}), bf16[4,128,512]{2,1,0:T(8,128)(2,1)S(1)}, u32[]{:S(2)}, u32[]{:S(2)}) async-start(bf16[4,128,512]{2,1,0:T(8,128)(2,1)} %bitcast.5), calls=%async_computation.1 | async-start | bytes 1048576 | tf_op jit(solution)/shard_map/all_to_all | solution.py:449
  103.7 9.2 %collective-permute-start.19 = (bf16[1024,256]{1,0:T(8,128)(2,1)}, bf16[1024,256]{1,0:T(8,128)(2,1)}, u32[]{:S(2)}, u32[]{:S(2)}) collective-permute-start(bf16[1024,256]{1,0:T(8,128)(2,1)} %collective-permute-done.15.refs_2_), channel_id=1, source_target_pairs={{0,2},{1,7},{2,4},{3,1},{4,6},{5,3},{6,0},{7,5},{8,10},{9,15},{10,... | collective-permute-start | bytes 1572872 | tf_op jit(solution)/shard_map/ppermute | solution.py:51
  105.3 12.8 %collective-permute-start.14 = (bf16[1024,256]{1,0:T(8,128)(2,1)S(1)}, bf16[1024,256]{1,0:T(8,128)(2,1)}, u32[]{:S(2)}, u32[]{:S(2)}) collective-permute-start(bf16[1024,256]{1,0:T(8,128)(2,1)S(1)} %bitcast.11), channel_id=1, source_target_pairs={{0,1},{1,0},{2,3},{3,2},{4,5},{5,4},{6,7},{7,6},{8,9},{9,8},{10,11... | collective-permute-start | bytes 1572872 | tf_op jit(solution)/shard_map/ppermute | solution.py:43
  108.1 10.0 %collective-permute-start.17 = (bf16[1024,256]{1,0:T(8,128)(2,1)}, bf16[1024,256]{1,0:T(8,128)(2,1)}, u32[]{:S(2)}, u32[]{:S(2)}) collective-permute-start(bf16[1024,256]{1,0:T(8,128)(2,1)} %collective-permute-done.15.refs_2_), channel_id=1, source_target_pairs={{0,1},{1,0},{2,3},{3,2},{4,5},{5,4},{6,7},{7,6},{8,9},{9,8},{10,11... | collective-permute-start | bytes 1572872 | tf_op jit(solution)/shard_map/ppermute | solution.py:43
  108.1 9.9 %collective-permute-start.18 = (bf16[1024,256]{1,0:T(8,128)(2,1)}, bf16[1024,256]{1,0:T(8,128)(2,1)}, u32[]{:S(2)}, u32[]{:S(2)}) collective-permute-start(bf16[1024,256]{1,0:T(8,128)(2,1)} %collective-permute-done.16.refs_4_), channel_id=1, source_target_pairs={{0,1},{1,0},{2,3},{3,2},{4,5},{5,4},{6,7},{7,6},{8,9},{9,8},{10,11... | collective-permute-start | bytes 1572872 | tf_op jit(solution)/shard_map/ppermute | solution.py:43
  109.5 1.6 %copy-start.1 = (bf16[1024,1024]{1,0:T(8,128)(2,1)S(1)}, bf16[1024,1024]{1,0:T(8,128)(2,1)}, u32[]{:S(2)}) copy-start(bf16[1024,1024]{1,0:T(8,128)(2,1)} %wv_ref.1) | copy-start | bytes 6291460
  112.8 7.0 %collective-permute-start.20 = (bf16[1024,256]{1,0:T(8,128)(2,1)}, bf16[1024,256]{1,0:T(8,128)(2,1)S(1)}, u32[]{:S(2)}, u32[]{:S(2)}) collective-permute-start(bf16[1024,256]{1,0:T(8,128)(2,1)} %collective-permute-done.19.refs_6_), channel_id=1, source_target_pairs={{0,1},{1,0},{2,3},{3,2},{4,5},{5,4},{6,7},{7,6},{8,9},{9,8},{10,11... | collective-permute-start | bytes 1572872 | tf_op jit(solution)/shard_map/ppermute | solution.py:43

commit v3 on v2

--- a/solution.py
+++ b/solution.py
@@ -51,6 +51,10 @@
     return lax.ppermute(a, ("x", "core"), pairs)
 
 
+def vid_index():
+    return (lax.axis_index("zq") * 2 + lax.axis_index("zp")) * NY + lax.axis_index("y")
+
+
 def run_copies(pairs, sems):
     copies = [pltpu.make_async_copy(src, dst, sems.at[i]) for i, (src, dst) in enumerate(pairs)]
     for copy in copies:
@@ -59,7 +63,7 @@
 
 
 def pack_kernel(
-    where_ref, len_ref, q_ref, g_ref, total_ref, dot_ref, k_ref, v_ref, msg_ref, kv_ref,
+    len_ref, q_ref, g_ref, total_ref, dot_ref, k_ref, v_ref, msg_ref, kv_ref,
     len_at, total_at, dot_at, sems,
 ):
     f32 = jnp.float32
@@ -78,7 +82,7 @@
     for copy in copies[:3]:
         copy.wait()
     row = lax.broadcasted_iota(jnp.int32, (GROUP, QLEN), 1)
-    total = jnp.where(row < len_at[where_ref[0]], total_at[...].astype(f32), DEAD)
+    total = jnp.where(row < len_at[vid_index()], total_at[...].astype(f32), DEAD)
     dots = dot_at[...].astype(f32)
     line = [total[h : h + 1, :] for h in range(GROUP)] + [dots[h : h + 1, :] for h in range(GROUP)]
     line = jnp.concatenate(line, axis=1)
@@ -87,9 +91,8 @@
         copy.wait()
 
 
-def pack(where, lengths, queries, out_grad, log_totals, out_dots, vis_keys, vis_values):
+def pack(lengths, queries, out_grad, log_totals, out_dots, vis_keys, vis_values):
     vm = pl.BlockSpec(memory_space=pltpu.VMEM)
-    sm = pl.BlockSpec(memory_space=pltpu.SMEM)
     hbm = pl.BlockSpec(memory_space=pltpu.HBM)
     return pl.pallas_call(
         pack_kernel,
@@ -97,7 +100,7 @@
             jax.ShapeDtypeStruct((MSG, GROUP * HD), jnp.bfloat16),
             jax.ShapeDtypeStruct((BLOCK, 2 * HD), jnp.bfloat16),
         ],
-        in_specs=[sm] + [hbm] * 7,
+        in_specs=[hbm] * 7,
         out_specs=[vm, vm],
         scratch_shapes=[
             pltpu.SMEM(lengths.shape, jnp.int32),
@@ -107,7 +110,7 @@
         ],
         cost_estimate=pl.CostEstimate(flops=0, bytes_accessed=1 << 20, transcendentals=0),
         name="pack",
-    )(where, lengths, queries, out_grad, log_totals, out_dots, vis_keys, vis_values)
+    )(lengths, queries, out_grad, log_totals, out_dots, vis_keys, vis_values)
 
 
 def heads_as_rows(block):
@@ -238,35 +241,37 @@
     return list(outs[:n_dq]), list(outs[n_dq:])
 
 
-def pair_kernel(where_ref, got_ref, *refs):
-    even_refs, out_ref = refs[: len(EVEN)], refs[len(EVEN)]
-    z = where_ref[0] // NY
-    away = 1 - 2 * (z % 2)
+def pair_kernel(got_ref, *refs):
+    even_refs, keep_ref, send_refs = refs[: len(EVEN)], refs[len(EVEN)], refs[len(EVEN) + 1 :]
+    away = 1 - 2 * (lax.axis_index("zp"))
     for i, offset in enumerate(EVEN):
         there = (offset - away + NZ) % NZ
         slot = jnp.int32(0)
         for j, odd in enumerate(ODD):
             slot = jnp.where(there == odd % NZ, j, slot)
         got = got_ref[pl.ds(pl.multiple_of(slot * HD, HD), HD), :].astype(jnp.float32)
-        to = ((z + offset + NZ) % NZ) // 2
         total = even_refs[i][...] + got
-        out_ref[pl.ds(pl.multiple_of(to * HD, HD), HD), :] = total.astype(jnp.bfloat16)
-
-
-def pair(where, even, got):
+        if i == 0:
+            keep_ref[...] = total
+        else:
+            send_refs[i - 1][...] = total.astype(jnp.bfloat16)
+
+
+def pair(even, got):
     vm = pl.BlockSpec(memory_space=pltpu.VMEM)
     return pl.pallas_call(
         pair_kernel,
-        out_shape=jax.ShapeDtypeStruct((len(EVEN) * HD, ROWS), jnp.bfloat16),
-        in_specs=[pl.BlockSpec(memory_space=pltpu.SMEM)] + [vm] * 5,
-        out_specs=vm,
+        out_shape=[jax.ShapeDtypeStruct((HD, ROWS), jnp.float32)]
+        + [jax.ShapeDtypeStruct((HD, ROWS), jnp.bfloat16)] * 3,
+        in_specs=[vm] * 5,
+        out_specs=[vm] * 4,
         compiler_params=pltpu.CompilerParams(vmem_limit_bytes=SMALL),
         cost_estimate=pl.CostEstimate(flops=0, bytes_accessed=2 << 20, transcendentals=0),
         name="pair",
-    )(where, got, *even)
-
-
-def dispatch_kernel(where_ref, owner_ref, own_ref, a_ref, b_ref, c_ref, out_ref, sum_ref, count_ref):
+    )(got, *even)
+
+
+def dispatch_kernel(owner_ref, own_ref, a_ref, b_ref, c_ref, out_ref, sum_ref, count_ref):
     f32 = jnp.float32
     total = own_ref[...] + a_ref[...].astype(f32) + b_ref[...].astype(f32) + c_ref[...].astype(f32)
     sum_ref[...] = total.astype(jnp.bfloat16)
@@ -274,8 +279,10 @@
     for j in range(N_VID):
         count_ref[j] = 0
 
+    first = vid_index() * FPD
+
     def place(f, carry):
-        owner = owner_ref[where_ref[0] * FPD + f]
+        owner = owner_ref[first + f]
         slot = count_ref[owner]
         count_ref[owner] = slot + 1
         to = pl.multiple_of((owner * MOST + slot) * TPF, TPF)
@@ -286,25 +293,25 @@
     lax.fori_loop(0, FPD, place, 0)
 
 
-def dispatch(where, owners, own, others):
+def dispatch(owners, own, others):
     vm = pl.BlockSpec(memory_space=pltpu.VMEM)
     return pl.pallas_call(
         dispatch_kernel,
         out_shape=jax.ShapeDtypeStruct((SLOT_ROWS, 2 * HD), jnp.bfloat16),
-        in_specs=[pl.BlockSpec(memory_space=pltpu.SMEM)] * 2 + [vm] * 4,
+        in_specs=[pl.BlockSpec(memory_space=pltpu.SMEM)] + [vm] * 4,
         out_specs=vm,
         scratch_shapes=[pltpu.VMEM((BLOCK, 2 * HD), jnp.bfloat16), pltpu.SMEM((N_VID,), jnp.int32)],
         compiler_params=pltpu.CompilerParams(vmem_limit_bytes=SMALL),
         cost_estimate=pl.CostEstimate(flops=0, bytes_accessed=2 << 20, transcendentals=0),
         name="dispatch",
-    )(where, owners, own, *others)
+    )(owners, own, *others)
 
 
 PIECES = [(dx, other) for dx in (0, -1, 1, 2) for other in (False, True)]
 
 
-def merge_kernel(where_ref, wk_ref, wv_ref, out_ref):
-    x, core = where_ref[1] // 2, where_ref[1] % 2
+def merge_kernel(_, wk_ref, wv_ref, out_ref):
+    x, core = lax.axis_index("x"), lax.axis_index("core")
     for p, (dx, other) in enumerate(PIECES):
         by = 1 - core if other else core
         h = ((x + dx * (1 - 2 * by) + NX) % NX) * 2 + by
@@ -313,31 +320,43 @@
         out_ref[:, (2 * p + 1) * HD : (2 * p + 2) * HD] = wv_ref[:, at]
 
 
-def merge(where, key_weight, value_weight):
+def merge(after, key_weight, value_weight):
     vm = pl.BlockSpec(memory_space=pltpu.VMEM)
     return pl.pallas_call(
         merge_kernel,
         out_shape=jax.ShapeDtypeStruct((key_weight.shape[0], 2 * KVH * HD), jnp.bfloat16),
-        in_specs=[pl.BlockSpec(memory_space=pltpu.SMEM), vm, vm],
+        in_specs=[pl.BlockSpec(memory_space=pl.ANY), vm, vm],
         out_specs=vm,
         compiler_params=pltpu.CompilerParams(vmem_limit_bytes=SMALL),
         cost_estimate=pl.CostEstimate(flops=0, bytes_accessed=8 << 20, transcendentals=0),
         name="merge",
-    )(where, key_weight, value_weight)
-
-
-def project(pieces, weight):
+    )(after, key_weight, value_weight)
+
+
+def project(name, pieces, first, weight, total=None):
     cols = weight.shape[0]
+    n = len(pieces)
     tile = 512
     n_tile = SLOT_ROWS // tile
-
-    def body(*refs):
-        w_ref, out_ref, out_at, sems = refs[KVH:]
+    final = total is not None
+    feats = slice(2 * HD * first, 2 * HD * (first + n))
+
+    def product(refs, w_ref, rows):
+        a = jnp.concatenate([ref[rows, :] for ref in refs[:n]], axis=1)
+        return dot32(a, w_ref[:, feats], NT)
+
+    def body_first(*refs):
+        w_ref, out_ref = refs[n:]
+        for t in range(n_tile):
+            rows = slice(t * tile, (t + 1) * tile)
+            out_ref[rows, :] = product(refs, w_ref, rows)
+
+    def body_final(*refs):
+        w_ref, total_ref, out_ref, out_at, sems = refs[n:]
         copies = []
         for t in range(n_tile):
             rows = slice(t * tile, (t + 1) * tile)
-            a = jnp.concatenate([ref[rows, :] for ref in refs[:KVH]], axis=1)
-            out_at[rows, :] = dot32(a, w_ref[...], NT).astype(jnp.bfloat16)
+            out_at[rows, :] = (total_ref[rows, :] + product(refs, w_ref, rows)).astype(jnp.bfloat16)
             copy = pltpu.make_async_copy(out_at.at[rows, :], out_ref.at[rows, :], sems.at[t])
             copy.start()
             copies.append(copy)
@@ -345,40 +364,38 @@
             copy.wait()
 
     vm = pl.BlockSpec(memory_space=pltpu.VMEM)
-    return pl.pallas_call(
-        body,
-        out_shape=jax.ShapeDtypeStruct((SLOT_ROWS, cols), jnp.bfloat16),
-        in_specs=[vm] * (KVH + 1),
-        out_specs=pl.BlockSpec(memory_space=pltpu.HBM),
-        scratch_shapes=[
-            pltpu.VMEM((SLOT_ROWS, cols), jnp.bfloat16),
-            pltpu.SemaphoreType.DMA((n_tile,)),
-        ],
+    scratch = [pltpu.VMEM((SLOT_ROWS, cols), jnp.bfloat16), pltpu.SemaphoreType.DMA((n_tile,))]
+    return pl.pallas_call(
+        body_final if final else body_first,
+        out_shape=jax.ShapeDtypeStruct((SLOT_ROWS, cols), jnp.bfloat16 if final else jnp.float32),
+        in_specs=[vm] * (n + 1 + final),
+        out_specs=pl.BlockSpec(memory_space=pltpu.HBM) if final else vm,
+        scratch_shapes=scratch if final else [],
         compiler_params=pltpu.CompilerParams(vmem_limit_bytes=MIDDLE),
         cost_estimate=pl.CostEstimate(
-            flops=4 * SLOT_ROWS * cols * KVH * HD, bytes_accessed=10 << 20, transcendentals=0
+            flops=4 * SLOT_ROWS * cols * n * HD, bytes_accessed=6 << 20, transcendentals=0
         ),
-        name="project",
-    )(*pieces, weight)
-
-
-def finish_kernel(part_ref, out_ref):
-    total = part_ref[0:HD, :].astype(jnp.float32)
-    for i in range(1, len(EVEN)):
-        total = total + part_ref[i * HD : (i + 1) * HD, :].astype(jnp.float32)
+        name=name,
+    )(*pieces, weight, *([total] if final else []))
+
+
+def finish_kernel(keep_ref, a_ref, b_ref, c_ref, out_ref):
+    total = keep_ref[...]
+    for ref in (a_ref, b_ref, c_ref):
+        total = total + ref[...].astype(jnp.float32)
     total = (total * SCALE).T
     for h in range(GROUP):
         out_ref[:, h * HD : (h + 1) * HD] = total[h * QLEN : (h + 1) * QLEN, :].astype(jnp.bfloat16)
 
 
-def finish(parts):
+def finish(keep, others):
     return pl.pallas_call(
         finish_kernel,
         out_shape=jax.ShapeDtypeStruct((QLEN, GROUP * HD), jnp.bfloat16),
         compiler_params=pltpu.CompilerParams(vmem_limit_bytes=SMALL),
         cost_estimate=pl.CostEstimate(flops=0, bytes_accessed=1 << 19, transcendentals=0),
         name="finish",
-    )(parts)
+    )(keep, *others)
 
 
 def on_device(
@@ -393,12 +410,8 @@
     value_weight,
     frame_owner,
 ):
-    vid = lax.axis_index(Z) * NY + lax.axis_index("y")
-    head = lax.axis_index("x") * 2 + lax.axis_index("core")
-    where = jnp.stack([vid, head])
-
     msg, kv0 = pack(
-        where, lengths, queries, out_grad, log_totals, out_dots, vis_keys, vis_values
+        lengths, queries, out_grad, log_totals, out_dots, vis_keys, vis_values
     )
 
     kv_up, kv_down = shift(kv0, "y", 1), shift(kv0, "y", -1)
@@ -433,26 +446,26 @@
     )
     even = [dq_0, dq[1], dq[0], dq[2]]
 
-    paired = pair(where, even, got)
-    own, paired = lax.optimization_barrier((own, paired))
-
-    outgoing = dispatch(where, frame_owner.reshape(-1), own, back)
+    keep, *sends = pair(even, got)
+    own, keep = lax.optimization_barrier((own, keep))
+
+    outgoing = dispatch(frame_owner.reshape(-1), own, back)
     mine = lax.all_to_all(outgoing, Z + ("y",), split_axis=0, concat_axis=0, tiled=True)
-    paired, mine = lax.optimization_barrier((paired, mine))
+    mine, *sends = lax.optimization_barrier((mine, *sends))
 
     first, second = shift_by_core(mine, 1), shift_by_core(mine, -1)
+    others = [shift(rows, "z", offset) for rows, offset in zip(sends, EVEN[1:])]
     pieces = [mine, shift(mine, "core", 1)]
-    first, second = lax.optimization_barrier((first, second))
+    first, second, *others = lax.optimization_barrier((first, second, *others))
     across = shift_by_core(first, 1)
     for rows in (first, second):
         pieces += [rows, shift(rows, "core", 1)]
-    parts = lax.all_to_all(paired, "zq", split_axis=0, concat_axis=0, tiled=True)
-    query_grad = finish(parts)
-    where, query_grad = lax.optimization_barrier((where, query_grad))
-    weight = merge(where, key_weight, value_weight)
-    across, weight = lax.optimization_barrier((across, weight))
-    pieces += [across, shift(across, "core", 1)]
-    return query_grad, project(pieces, weight)
+    query_grad = finish(keep, others)
+    weight = merge(first, key_weight, value_weight)
+    total = project("project_near", pieces, 0, weight)
+    across, total, query_grad = lax.optimization_barrier((across, total, query_grad))
+    pieces = [across, shift(across, "core", 1)]
+    return query_grad, project("project_across", pieces, 6, weight, total)
 
 
 def solution(mesh):

time: 128 us -> 119 us (0.930)
  waiting for transfers between devices: 20 us -> 13.3 us
  starting transfers between devices: 41.6 us -> 46.8 us
  Pallas kernels: 38.5 us -> 34.2 us
  local copies, waits for them, and re-layouts: 3.52 us -> 1.93 us
    ppermute x17 -> x20, starting transfers between devices: 32.9 us -> 40.5 us  [shift(): lax.ppermute(a, Z if axis == 'z' else axis, [(i, (i + k) % n) for i in ra...]
    ppermute x3, waiting for transfers between devices: 6.53 us -> 0.64 us  [shift_by_core(): return lax.ppermute(a, ('x', 'core'), pairs)]
    all_to_all x1 -> x0, starting transfers between devices: 3.54 us -> none  [on_device(): lax.all_to_all(paired, 'zq', split_axis=0, concat_axis=0, tiled=True)]
    pallas_call x2 -> x3, Pallas kernels: 8.8 us -> 5.84 us  [the longest x2 5.74 us: project(): pl.pallas_call(body_final if final else body_first, out_shape=jax.ShapeDt...]
    ppermute x17 -> x20, waiting for transfers between devices: 13.5 us -> 11.1 us  [shift(): lax.ppermute(a, Z if axis == 'z' else axis, [(i, (i + k) % n) for i in ra...]
    ppermute x1, waiting for transfers between devices: 0.01 us -> 1.62 us  [on_device(): got = lax.ppermute(odd, 'zp', [(0, 1), (1, 0)])]
    unnamed x14 -> x12, local copies, waits for them, and re-layouts: 3.52 us -> 1.93 us
  transfers between devices with their start and end apart: 22 -> 24, of which waited for: 8 -> 9; matrix products, arithmetic and copies ran while one was open for 0% -> 0% of each run, Pallas kernels for 21% -> 24%
where the time goes in v3:
time: 119 us
  starting transfers between devices  46.8 us (39%)
  Pallas kernels  34.2 us (29%)
  blocking collectives  21.8 us (18%)
  waiting for transfers between devices  13.3 us (11%)
  local copies, waits for them, and re-layouts  1.93 us (2%)
    ppermute x20, starting transfers between devices, shift(): lax.ppermute(a, Z if axis == 'z' else axis, [(i, (i + k) % n) for i in ra...  40.5 us
    pallas_call x6, Pallas kernels, attend(): pl.pallas_call(body, out_shape=out_shape, scratch_shapes=message_scratch(...  23.4 us
    all_to_all x1, blocking collectives, on_device(): lax.all_to_all(outgoing, Z + ('y',), split_axis=0, concat_axis=0, tiled=T...  21.8 us
    ppermute x20, waiting for transfers between devices, shift(): lax.ppermute(a, Z if axis == 'z' else axis, [(i, (i + k) % n) for i in ra...  11.1 us
    pallas_call x2, Pallas kernels, project(): pl.pallas_call(body_final if final else body_first, out_shape=jax.ShapeDt...  5.74 us
    ppermute x3, starting transfers between devices, shift_by_core(): return lax.ppermute(a, ('x', 'core'), pairs)  4.68 us
  transfers between devices with their start and end apart: 24, of which 9 were waited for; matrix products, arithmetic and copies ran while one was open for 0% of the time, Pallas kernels for 24%

profile of v3, /device:TPU:1, one launch (start us, length us, event | category | flops | bytes accessed | tf_op | source)
XLA Modules:
  0.0 119.0 jit_solution(16022222428994907071)
XLA Ops:
  0.6 2.0 %pack.1 = (bf16[144,1024]{1,0:T(8,128)(2,1)}, bf16[512,256]{1,0:T(8,128)(2,1)}) custom-call(s32[32]{0:T(128)} %len_ref.1, bf16[64,1024]{1,0:T(8,128)(2,1)} %q_ref.1, bf16[64,1024]{1,0:T(8,128)(2,1)} %g_ref.1, bf16[8,64]{1,0:T(8,128)(2,1)} %total_ref.1, bf16[8,64]{1,0:T(8,128)(2,1)} %dot_ref.1, bf16[512,128]{1,0:T(8,128)(2,1)} %k_ref.1, bf16[512,128]{1,0:T(8,128)(2,1)} %v_ref.1), custom_call_target="tpu_custom_call" | custom-call | bytes 1048576 | tf_op jit(solution)/shard_map/pack/pallas_call | solution.py:97
  2.6 2.5 %collective-permute-start = (bf16[144,1024]{1,0:T(8,128)(2,1)}, bf16[144,1024]{1,0:T(8,128)(2,1)S(1)}, u32[]{:S(2)}, u32[]{:S(2)}) collective-permute-start(bf16[144,1024]{1,0:T(8,128)(2,1)} %get-tuple-element.56.refs_0_), channel_id=1, source_target_pairs={{0,32},{32,64},{64,96},{96,128},{128,160},{160,192},{192,224},{224... | collective-permute-start | bytes 884744 | tf_op jit(solution)/shard_map/ppermute | solution.py:43
  5.2 4.0 %collective-permute-start.2 = (bf16[144,1024]{1,0:T(8,128)(2,1)}, bf16[144,1024]{1,0:T(8,128)(2,1)S(1)}, u32[]{:S(2)}, u32[]{:S(2)}) collective-permute-start(bf16[144,1024]{1,0:T(8,128)(2,1)} %get-tuple-element.56.refs_0_), channel_id=1, source_target_pairs={{0,224},{32,0},{64,32},{96,64},{128,96},{160,128},{192,160},{224,1... | collective-permute-start | bytes 884744 | tf_op jit(solution)/shard_map/ppermute | solution.py:43
  9.2 1.3 %collective-permute-start.6 = (bf16[512,256]{1,0:T(8,128)(2,1)}, bf16[512,256]{1,0:T(8,128)(2,1)S(1)}, u32[]{:S(2)}, u32[]{:S(2)}) collective-permute-start(bf16[512,256]{1,0:T(8,128)(2,1)} %get-tuple-element.57.refs_3_.refs_5_), channel_id=1, source_target_pairs={{0,8},{8,16},{16,24},{24,0},{1,9},{9,17},{17,25},{25,1},{2,10},{10... | collective-permute-start | bytes 786440 | tf_op jit(solution)/shard_map/ppermute | solution.py:43
  10.5 1.4 %collective-permute-start.7 = (bf16[512,256]{1,0:T(8,128)(2,1)}, bf16[512,256]{1,0:T(8,128)(2,1)S(1)}, u32[]{:S(2)}, u32[]{:S(2)}) collective-permute-start(bf16[512,256]{1,0:T(8,128)(2,1)} %get-tuple-element.57.refs_3_.refs_5_), channel_id=1, source_target_pairs={{0,24},{8,0},{16,8},{24,16},{1,25},{9,1},{17,9},{25,17},{2,26},{10... | collective-permute-start | bytes 786440 | tf_op jit(solution)/shard_map/ppermute | solution.py:43
  11.9 1.6 %collective-permute-start.8 = (bf16[512,256]{1,0:T(8,128)(2,1)}, bf16[512,256]{1,0:T(8,128)(2,1)S(1)}, u32[]{:S(2)}, u32[]{:S(2)}) collective-permute-start(bf16[512,256]{1,0:T(8,128)(2,1)} %get-tuple-element.57.refs_3_.refs_5_), channel_id=1, source_target_pairs={{0,16},{8,24},{16,0},{24,8},{1,17},{9,25},{17,1},{25,9},{2,18},{10... | collective-permute-start | bytes 786440 | tf_op jit(solution)/shard_map/ppermute | solution.py:43
  13.6 2.5 %collective-permute-done.refs_1_ = bf16[144,1024]{1,0:T(8,128)(2,1)S(1)} collective-permute-done((bf16[144,1024]{1,0:T(8,128)(2,1)}, bf16[144,1024]{1,0:T(8,128)(2,1)S(1)}, u32[]{:S(2)}, u32[]{:S(2)}) %collective-permute-start) | collective-permute-done | bytes 294944 | tf_op jit(solution)/shard_map/ppermute | solution.py:43
  16.0 0.0 collective-permute-start.1
  16.0 0.0 collective-permute-done.2.refs_2_
  16.0 2.7 %collective-permute-start.3 = (bf16[144,1024]{1,0:T(8,128)(2,1)S(1)}, bf16[144,1024]{1,0:T(8,128)(2,1)S(1)}, u32[]{:S(2)}, u32[]{:S(2)}) collective-permute-start(bf16[144,1024]{1,0:T(8,128)(2,1)S(1)} %collective-permute-done.2.refs_2_), channel_id=1, source_target_pairs={{0,224},{32,0},{64,32},{96,64},{128,96},{160,128},{192,160},{224,1... | collective-permute-start | bytes 884744 | tf_op jit(solution)/shard_map/ppermute | solution.py:43
  18.7 1.0 copy-done.3
  19.7 0.9 copy-done.4
  20.6 2.1 %home_first.1 = (f32[128,512]{1,0:T(8,128)S(1)}, f32[128,512]{1,0:T(8,128)S(1)}, f32[128,512]{1,0:T(8,128)S(1)}, f32[512,256]{1,0:T(8,128)S(1)}) custom-call(bf16[144,1024]{1,0:T(8,128)(2,1)S(1)} %copy-done.3, bf16[144,1024]{1,0:T(8,128)(2,1)S(1)} %collective-permute-done.refs_1_, bf16[144,1024]{1,0:T(8,128)(2,1)S(1)} %collective-permute-done.2.refs_2_, ...), custom_call_target="tpu_custom_call" | custom-call | flops 2013265920 | bytes 2097152 | tf_op jit(solution)/shard_map/home_first/pallas_call | solution.py:224
  22.7 0.0 collective-permute-done.6.refs_3_.refs_2_.refs_1_
  22.7 0.0 collective-permute-done.7.refs_4_.refs_3_.refs_2_
  22.7 1.6 %collective-permute-done.8.refs_5_.refs_4_.refs_3_ = bf16[512,256]{1,0:T(8,128)(2,1)S(1)} collective-permute-done((bf16[512,256]{1,0:T(8,128)(2,1)}, bf16[512,256]{1,0:T(8,128)(2,1)S(1)}, u32[]{:S(2)}, u32[]{:S(2)}) %collective-permute-start.8) | collective-permute-done | bytes 262176 | tf_op jit(solution)/shard_map/ppermute | solution.py:43
  24.3 6.5 %away_near.1 = (f32[128,512]{1,0:T(8,128)S(1)}, bf16[128,512]{1,0:T(8,128)(2,1)S(1)}, bf16[128,512]{1,0:T(8,128)(2,1)S(1)}, f32[512,256]{1,0:T(8,128)S(1)}, f32[...) custom-call(bf16[144,1024]{1,0:T(8,128)(2,1)S(1)} %copy-done.3, bf16[144,1024]{1,0:T(8,128)(2,1)S(1)} %collective-permute-done.refs_1_, ...), custom_call_target="tpu_custom_call" | custom-call | flops 6039797760 | bytes 2097152 | tf_op jit(solution)/shard_map/away_near/pallas_call | solution.py:224
  30.8 0.0 collective-permute-done.1.refs_0_
  30.8 0.0 collective-permute-done.3.refs_1_
  30.8 0.1 collective-permute-start.4
  30.9 2.7 %collective-permute-start.5 = (bf16[144,1024]{1,0:T(8,128)(2,1)S(1)}, bf16[144,1024]{1,0:T(8,128)(2,1)S(1)}, u32[]{:S(2)}, u32[]{:S(2)}) collective-permute-start(bf16[144,1024]{1,0:T(8,128)(2,1)S(1)} %collective-permute-done.3.refs_1_), channel_id=1, source_target_pairs={{0,224},{32,0},{64,32},{96,64},{128,96},{160,128},{192,160},{224,1... | collective-permute-start | bytes 884744 | tf_op jit(solution)/shard_map/ppermute | solution.py:43
  33.6 4.6 %away_two.1 = (f32[128,512]{1,0:T(8,128)S(1)}, f32[128,512]{1,0:T(8,128)S(1)}, f32[512,256]{1,0:T(8,128)S(1)}, f32[512,256]{1,0:T(8,128)S(1)}, f32[512,256]{1,0:T(8,128)S(1)}) custom-call(bf16[144,1024]{1,0:T(8,128)(2,1)S(1)} %collective-permute-done.1.refs_0_, bf16[144,1024]{1,0:T(8,128)(2,1)S(1)} %collective-permute-done.3.refs_1_, ...), custom_call_target="tpu_custom_call" | custom-call | flops 4026531840 | bytes 2097152 | tf_op jit(solution)/shard_map/away_two/pallas_call | solution.py:224
  38.2 0.6 collective-permute-done.4.refs_0_
  38.7 0.0 collective-permute-done.5.refs_1_
  38.8 0.0 collective-permute-start.9
  38.8 6.1 %all_three.1 = (bf16[512,512]{1,0:T(8,128)(2,1)S(1)}, f32[512,256]{1,0:T(8,128)S(1)}, f32[512,256]{1,0:T(8,128)S(1)}, f32[512,256]{1,0:T(8,128)S(1)}, f32[512,256]{1,0:T(8,128)S(1)}) custom-call(bf16[144,1024]{1,0:T(8,128)(2,1)S(1)} %collective-permute-done.4.refs_0_, bf16[144,1024]{1,0:T(8,128)(2,1)S(1)} %collective-permute-done.5.refs_1_, ...), custom_call_target="tpu_custom_call" | custom-call | flops 5368709120 | bytes 2097152 | tf_op jit(solution)/shard_map/all_three/pallas_call | solution.py:224
  44.8 1.6 %collective-permute-start.10 = (bf16[512,512]{1,0:T(8,128)(2,1)S(1)}, bf16[512,512]{1,0:T(8,128)(2,1)S(1)}, u32[]{:S(2)}, u32[]{:S(2)}) collective-permute-start(bf16[512,512]{1,0:T(8,128)(2,1)S(1)} %get-tuple-element.84), channel_id=1, source_target_pairs={{0,32},{32,0},{1,33},{33,1},{2,34},{34,2},{3,35},{35,3},{4,36},{36... | collective-permute-start | bytes 1572872 | tf_op jit(solution)/shard_map/ppermute | solution.py:443
  46.4 0.0 collective-permute-done.9.refs_0_.refs_2_
  46.4 2.2 %away_far.1 = (f32[128,512]{1,0:T(8,128)S(1)}, bf16[512,256]{1,0:T(8,128)(2,1)S(1)}, bf16[512,256]{1,0:T(8,128)(2,1)S(1)}, bf16[512,256]{1,0:T(8,128)(2,1)S(1)}) custom-call(bf16[144,1024]{1,0:T(8,128)(2,1)S(1)} %collective-permute-done.9.refs_0_.refs_2_, bf16[512,256]{1,0:T(8,128)(2,1)S(1)} %collective-permute-done.6.refs_3_.refs_2_.refs_1_, ...), custom_call_target="tpu_custom_call" | custom-call | flops 2013265920 | bytes 2097152 | tf_op jit(solution)/shard_map/away_far/pallas_call | solution.py:224
  48.6 1.5 %collective-permute-start.11 = (bf16[512,256]{1,0:T(8,128)(2,1)S(1)}, bf16[512,256]{1,0:T(8,128)(2,1)S(1)}, u32[]{:S(2)}, u32[]{:S(2)}) collective-permute-start(bf16[512,256]{1,0:T(8,128)(2,1)S(1)} %get-tuple-element.91), channel_id=1, source_target_pairs={{0,16},{8,24},{16,0},{24,8},{1,17},{9,25},{17,1},{25,9},{2,18},{10... | collective-permute-start | bytes 786440 | tf_op jit(solution)/shard_map/ppermute | solution.py:43
  50.1 1.3 %collective-permute-start.12 = (bf16[512,256]{1,0:T(8,128)(2,1)S(1)}, bf16[512,256]{1,0:T(8,128)(2,1)S(1)}, u32[]{:S(2)}, u32[]{:S(2)}) collective-permute-start(bf16[512,256]{1,0:T(8,128)(2,1)S(1)} %get-tuple-element.92), channel_id=1, source_target_pairs={{0,24},{8,0},{16,8},{24,16},{1,25},{9,1},{17,9},{25,17},{2,26},{10... | collective-permute-start | bytes 786440 | tf_op jit(solution)/shard_map/ppermute | solution.py:43
  51.4 0.2 collective-permute-start.13
  51.6 2.1 %home_last.1 = (f32[128,512]{1,0:T(8,128)S(1)}, f32[128,512]{1,0:T(8,128)S(1)}, f32[128,512]{1,0:T(8,128)S(1)}, f32[512,256]{1,0:T(8,128)S(1)}) custom-call(bf16[144,1024]{1,0:T(8,128)(2,1)S(1)} %collective-permute-done.1.refs_0_, bf16[144,1024]{1,0:T(8,128)(2,1)S(1)} %collective-permute-done.3.refs_1_, ...), custom_call_target="tpu_custom_call" | custom-call | flops 2013265920 | bytes 2097152 | tf_op jit(solution)/shard_map/home_last/pallas_call | solution.py:224
  53.6 1.6 %collective-permute-done.10.got_ref = bf16[512,512]{1,0:T(8,128)(2,1)S(1)} collective-permute-done((bf16[512,512]{1,0:T(8,128)(2,1)S(1)}, bf16[512,512]{1,0:T(8,128)(2,1)S(1)}, u32[]{:S(2)}, u32[]{:S(2)}) %collective-permute-start.10) | collective-permute-done | bytes 524320 | tf_op jit(solution)/shard_map/ppermute | solution.py:443
  55.3 0.1 pair.1
  55.4 0.0 collective-permute-done.11.a_ref
  55.4 2.7 %collective-permute-done.12.b_ref = bf16[512,256]{1,0:T(8,128)(2,1)S(1)} collective-permute-done((bf16[512,256]{1,0:T(8,128)(2,1)S(1)}, bf16[512,256]{1,0:T(8,128)(2,1)S(1)}, u32[]{:S(2)}, u32[]{:S(2)}) %collective-permute-start.12) | collective-permute-done | bytes 262176 | tf_op jit(solution)/shard_map/ppermute | solution.py:43
  58.2 1.7 %collective-permute-done.13.c_ref = bf16[512,256]{1,0:T(8,128)(2,1)S(1)} collective-permute-done((bf16[512,256]{1,0:T(8,128)(2,1)S(1)}, bf16[512,256]{1,0:T(8,128)(2,1)S(1)}, u32[]{:S(2)}, u32[]{:S(2)}) %collective-permute-start.13) | collective-permute-done | bytes 262176 | tf_op jit(solution)/shard_map/ppermute | solution.py:43
  59.9 1.0 dispatch.1
  60.9 21.8 %all_to_all.12 = bf16[32,32,256]{2,1,0:T(8,128)(2,1)S(1)} all-to-all(bf16[32,32,256]{2,1,0:T(8,128)(2,1)S(1)} %bitcast.3), channel_id=1, replica_groups=mesh['zq'=4,'zp'=2,'y'=4,'x'=4,'core'=2] {'zq','zp','y'}, dimensions={0} | all-to-all | bytes 1048576 | tf_op jit(solution)/shard_map/all_to_all | solution.py:453
  82.7 2.5 %collective-permute-start.14 = (bf16[1024,256]{1,0:T(8,128)(2,1)S(1)}, bf16[1024,256]{1,0:T(8,128)(2,1)S(1)}, u32[]{:S(2)}, u32[]{:S(2)}) collective-permute-start(bf16[1024,256]{1,0:T(8,128)(2,1)S(1)} %bitcast.4), channel_id=1, source_target_pairs={{0,2},{1,7},{2,4},{3,1},{4,6},{5,3},{6,0},{7,5},{8,10},{9,15},{10,... | collective-permute-start | bytes 1572872 | tf_op jit(solution)/shard_map/ppermute | solution.py:51
  85.2 0.0 collective-permute-start.15
  85.2 1.9 %collective-permute-start.16 = (bf16[128,512]{1,0:T(8,128)(2,1)S(1)}, bf16[128,512]{1,0:T(8,128)(2,1)S(1)}, u32[]{:S(2)}, u32[]{:S(2)}) collective-permute-start(bf16[128,512]{1,0:T(8,128)(2,1)S(1)} %get-tuple-element.98), channel_id=1, source_target_pairs={{0,64},{32,96},{64,128},{96,160},{128,192},{160,224},{192,0},{224,... | collective-permute-start | bytes 393224 | tf_op jit(solution)/shard_map/ppermute | solution.py:43
  87.1 1.7 %collective-permute-start.17 = (bf16[128,512]{1,0:T(8,128)(2,1)S(1)}, bf16[128,512]{1,0:T(8,128)(2,1)S(1)}, u32[]{:S(2)}, u32[]{:S(2)}) collective-permute-start(bf16[128,512]{1,0:T(8,128)(2,1)S(1)} %get-tuple-element.99), channel_id=1, source_target_pairs={{0,192},{32,224},{64,0},{96,32},{128,64},{160,96},{192,128},{224,1... | collective-permute-start | bytes 393224 | tf_op jit(solution)/shard_map/ppermute | solution.py:43
  88.8 2.5 %collective-permute-start.18 = (bf16[128,512]{1,0:T(8,128)(2,1)S(1)}, bf16[128,512]{1,0:T(8,128)(2,1)S(1)}, u32[]{:S(2)}, u32[]{:S(2)}) collective-permute-start(bf16[128,512]{1,0:T(8,128)(2,1)S(1)} %get-tuple-element.100), channel_id=1, source_target_pairs={{0,128},{32,160},{64,192},{96,224},{128,0},{160,32},{192,64},{224,... | collective-permute-start | bytes 393224 | tf_op jit(solution)/shard_map/ppermute | solution.py:43
  91.2 0.0 collective-permute-done.16.a_ref
  91.3 7.6 %collective-permute-start.20 = (bf16[1024,256]{1,0:T(8,128)(2,1)S(1)}, bf16[1024,256]{1,0:T(8,128)(2,1)S(1)}, u32[]{:S(2)}, u32[]{:S(2)}) collective-permute-start(bf16[1024,256]{1,0:T(8,128)(2,1)S(1)} %bitcast.6), channel_id=1, source_target_pairs={{0,1},{1,0},{2,3},{3,2},{4,5},{5,4},{6,7},{7,6},{8,9},{9,8},{10,11... | collective-permute-start | bytes 1572872 | tf_op jit(solution)/shard_map/ppermute | solution.py:43
  98.9 0.0 collective-permute-done.17.b_ref
  98.9 0.3 collective-permute-done.18.c_ref
  99.2 0.0 collective-permute-done.14._.refs_2_
  99.2 0.0 collective-permute-done.15.refs_4_
  99.2 4.9 %collective-permute-start.21 = (bf16[1024,256]{1,0:T(8,128)(2,1)S(1)}, bf16[1024,256]{1,0:T(8,128)(2,1)S(1)}, u32[]{:S(2)}, u32[]{:S(2)}) collective-permute-start(bf16[1024,256]{1,0:T(8,128)(2,1)S(1)} %collective-permute-done.14._.refs_2_), channel_id=1, source_target_pairs={{0,1},{1,0},{2,3},{3,2},{4,5},{5,4},{6,7},{7,6},{8,9},{9,8},{10,11... | collective-permute-start | bytes 1572872 | tf_op jit(solution)/shard_map/ppermute | solution.py:43
  104.1 0.1 collective-permute-start.22
  104.2 2.2 %collective-permute-start.19 = (bf16[1024,256]{1,0:T(8,128)(2,1)S(1)}, bf16[1024,256]{1,0:T(8,128)(2,1)S(1)}, u32[]{:S(2)}, u32[]{:S(2)}) collective-permute-start(bf16[1024,256]{1,0:T(8,128)(2,1)S(1)} %collective-permute-done.14._.refs_2_), channel_id=1, source_target_pairs={{0,2},{1,7},{2,4},{3,1},{4,6},{5,3},{6,0},{7,5},{8,10},{9,15},{10,... | collective-permute-start | bytes 1572872 | tf_op jit(solution)/shard_map/ppermute | solution.py:51
  106.4 1.2 %merge.1.refs_6_.refs_2_ = bf16[1024,2048]{1,0:T(8,128)(2,1)S(1)} custom-call(bf16[1024,256]{1,0:T(8,128)(2,1)S(1)} %collective-permute-done.14._.refs_2_, bf16[1024,1024]{1,0:T(8,128)(2,1)S(1)} %copy-done, bf16[1024,1024]{1,0:T(8,128)(2,1)S(1)} %copy-done.1), custom_call_target="tpu_custom_call" | custom-call | bytes 8388608 | tf_op jit(solution)/shard_map/merge/pallas_call | solution.py:325
  107.6 0.8 finish.1
  108.4 0.0 collective-permute-done.20.refs_1_
  108.4 0.0 collective-permute-done.21.refs_3_
  108.4 0.0 collective-permute-done.22.refs_5_
  108.4 3.5 %project_near.1.refs_3_ = f32[1024,1024]{1,0:T(8,128)S(1)} custom-call(bf16[1024,256]{1,0:T(8,128)(2,1)S(1)} %bitcast.7, bf16[1024,256]{1,0:T(8,128)(2,1)S(1)} %collective-permute-done.20.refs_1_, bf16[1024,256]{1,0:T(8,128)(2,1)S(1)} %collective-permute-done.14._.refs_2_, bf16[1024,256]{1,0:T(8,128)(2,1)S(1)} %collective-permute-done.21.refs_3_, ...), custom_call_target="tpu_custom_call" | custom-call | flops 3221225472 | bytes 6291456 | tf_op jit(solution)/shard_map/project_near/pallas_call | solution.py:368
  111.9 0.6 collective-permute-done.19.refs_0_
  112.5 2.5 %collective-permute-start.23 = (bf16[1024,256]{1,0:T(8,128)(2,1)S(1)}, bf16[1024,256]{1,0:T(8,128)(2,1)S(1)}, u32[]{:S(2)}, u32[]{:S(2)}) collective-permute-start(bf16[1024,256]{1,0:T(8,128)(2,1)S(1)} %collective-permute-done.19.refs_0_), channel_id=1, source_target_pairs={{0,1},{1,0},{2,3},{3,2},{4,5},{5,4},{6,7},{7,6},{8,9},{9,8},{10,11... | collective-permute-start | bytes 1572872 | tf_op jit(solution)/shard_map/ppermute | solution.py:43
  115.0 1.5 %collective-permute-done.23.refs_1_ = bf16[1024,256]{1,0:T(8,128)(2,1)S(1)} collective-permute-done((bf16[1024,256]{1,0:T(8,128)(2,1)S(1)}, bf16[1024,256]{1,0:T(8,128)(2,1)S(1)}, u32[]{:S(2)}, u32[]{:S(2)}) %collective-permute-start.23) | collective-permute-done | bytes 524320 | tf_op jit(solution)/shard_map/ppermute | solution.py:43
  116.5 2.3 %project_across.1 = bf16[1024,1024]{1,0:T(8,128)(2,1)} custom-call(bf16[1024,256]{1,0:T(8,128)(2,1)S(1)} %collective-permute-done.19.refs_0_, bf16[1024,256]{1,0:T(8,128)(2,1)S(1)} %collective-permute-done.23.refs_1_, bf16[1024,2048]{1,0:T(8,128)(2,1)S(1)} %merge.1.refs_6_.refs_2_, f32[1024,1024]{1,0:T(8,128)S(1)} %project_near.1.refs_3_), custom_call_target="tpu_custom_call" | custom-call | flops 1073741824 | bytes 6291456 | tf_op jit(solution)/shard_map/project_across/pallas_call | solution.py:368
  (10 shorter events, 0.0 us)
Async XLA Ops:
  2.6 13.4 %collective-permute-start = (bf16[144,1024]{1,0:T(8,128)(2,1)}, bf16[144,1024]{1,0:T(8,128)(2,1)S(1)}, u32[]{:S(2)}, u32[]{:S(2)}) collective-permute-start(bf16[144,1024]{1,0:T(8,128)(2,1)} %get-tuple-element.56.refs_0_), channel_id=1, source_target_pairs={{0,32},{32,64},{64,96},{96,128},{128,160},{160,192},{192,224},{224... | collective-permute-start | bytes 884744 | tf_op jit(solution)/shard_map/ppermute | solution.py:43
  5.2 10.9 %collective-permute-start.2 = (bf16[144,1024]{1,0:T(8,128)(2,1)}, bf16[144,1024]{1,0:T(8,128)(2,1)S(1)}, u32[]{:S(2)}, u32[]{:S(2)}) collective-permute-start(bf16[144,1024]{1,0:T(8,128)(2,1)} %get-tuple-element.56.refs_0_), channel_id=1, source_target_pairs={{0,224},{32,0},{64,32},{96,64},{128,96},{160,128},{192,160},{224,1... | collective-permute-start | bytes 884744 | tf_op jit(solution)/shard_map/ppermute | solution.py:43
  9.2 13.5 %collective-permute-start.6 = (bf16[512,256]{1,0:T(8,128)(2,1)}, bf16[512,256]{1,0:T(8,128)(2,1)S(1)}, u32[]{:S(2)}, u32[]{:S(2)}) collective-permute-start(bf16[512,256]{1,0:T(8,128)(2,1)} %get-tuple-element.57.refs_3_.refs_5_), channel_id=1, source_target_pairs={{0,8},{8,16},{16,24},{24,0},{1,9},{9,17},{17,25},{25,1},{2,10},{10... | collective-permute-start | bytes 786440 | tf_op jit(solution)/shard_map/ppermute | solution.py:43
  10.5 12.2 %collective-permute-start.7 = (bf16[512,256]{1,0:T(8,128)(2,1)}, bf16[512,256]{1,0:T(8,128)(2,1)S(1)}, u32[]{:S(2)}, u32[]{:S(2)}) collective-permute-start(bf16[512,256]{1,0:T(8,128)(2,1)} %get-tuple-element.57.refs_3_.refs_5_), channel_id=1, source_target_pairs={{0,24},{8,0},{16,8},{24,16},{1,25},{9,1},{17,9},{25,17},{2,26},{10... | collective-permute-start | bytes 786440 | tf_op jit(solution)/shard_map/ppermute | solution.py:43
  11.9 12.4 %collective-permute-start.8 = (bf16[512,256]{1,0:T(8,128)(2,1)}, bf16[512,256]{1,0:T(8,128)(2,1)S(1)}, u32[]{:S(2)}, u32[]{:S(2)}) collective-permute-start(bf16[512,256]{1,0:T(8,128)(2,1)} %get-tuple-element.57.refs_3_.refs_5_), channel_id=1, source_target_pairs={{0,16},{8,24},{16,0},{24,8},{1,17},{9,25},{17,1},{25,9},{2,18},{10... | collective-permute-start | bytes 786440 | tf_op jit(solution)/shard_map/ppermute | solution.py:43
  16.0 14.8 %collective-permute-start.1 = (bf16[144,1024]{1,0:T(8,128)(2,1)S(1)}, bf16[144,1024]{1,0:T(8,128)(2,1)S(1)}, u32[]{:S(2)}, u32[]{:S(2)}) collective-permute-start(bf16[144,1024]{1,0:T(8,128)(2,1)S(1)} %collective-permute-done.refs_1_), channel_id=1, source_target_pairs={{0,32},{32,64},{64,96},{96,128},{128,160},{160,192},{192,224},{224... | collective-permute-start | bytes 884744 | tf_op jit(solution)/shard_map/ppermute | solution.py:43
  16.0 14.8 %collective-permute-start.3 = (bf16[144,1024]{1,0:T(8,128)(2,1)S(1)}, bf16[144,1024]{1,0:T(8,128)(2,1)S(1)}, u32[]{:S(2)}, u32[]{:S(2)}) collective-permute-start(bf16[144,1024]{1,0:T(8,128)(2,1)S(1)} %collective-permute-done.2.refs_2_), channel_id=1, source_target_pairs={{0,224},{32,0},{64,32},{96,64},{128,96},{160,128},{192,160},{224,1... | collective-permute-start | bytes 884744 | tf_op jit(solution)/shard_map/ppermute | solution.py:43
  18.7 1.0 copy-start.3
  19.7 0.9 copy-start.4
  30.8 7.9 %collective-permute-start.4 = (bf16[144,1024]{1,0:T(8,128)(2,1)S(1)}, bf16[144,1024]{1,0:T(8,128)(2,1)S(1)}, u32[]{:S(2)}, u32[]{:S(2)}) collective-permute-start(bf16[144,1024]{1,0:T(8,128)(2,1)S(1)} %collective-permute-done.1.refs_0_), channel_id=1, source_target_pairs={{0,32},{32,64},{64,96},{96,128},{128,160},{160,192},{192,224},{224... | collective-permute-start | bytes 884744 | tf_op jit(solution)/shard_map/ppermute | solution.py:43
  30.9 7.8 %collective-permute-start.5 = (bf16[144,1024]{1,0:T(8,128)(2,1)S(1)}, bf16[144,1024]{1,0:T(8,128)(2,1)S(1)}, u32[]{:S(2)}, u32[]{:S(2)}) collective-permute-start(bf16[144,1024]{1,0:T(8,128)(2,1)S(1)} %collective-permute-done.3.refs_1_), channel_id=1, source_target_pairs={{0,224},{32,0},{64,32},{96,64},{128,96},{160,128},{192,160},{224,1... | collective-permute-start | bytes 884744 | tf_op jit(solution)/shard_map/ppermute | solution.py:43
  33.6 5.2 %copy-start.5 = (bf16[512,256]{1,0:T(8,128)(2,1)S(1)}, bf16[512,256]{1,0:T(8,128)(2,1)}, u32[]{:S(2)}) copy-start(bf16[512,256]{1,0:T(8,128)(2,1)} %get-tuple-element.57.refs_3_.refs_5_) | copy-start | bytes 786436
  38.8 7.6 %collective-permute-start.9 = (bf16[144,1024]{1,0:T(8,128)(2,1)S(1)}, bf16[144,1024]{1,0:T(8,128)(2,1)S(1)}, u32[]{:S(2)}, u32[]{:S(2)}) collective-permute-start(bf16[144,1024]{1,0:T(8,128)(2,1)S(1)} %collective-permute-done.4.refs_0_), channel_id=1, source_target_pairs={{0,32},{32,64},{64,96},{96,128},{128,160},{160,192},{192,224},{224... | collective-permute-start | bytes 884744 | tf_op jit(solution)/shard_map/ppermute | solution.py:43
  44.8 10.4 %collective-permute-start.10 = (bf16[512,512]{1,0:T(8,128)(2,1)S(1)}, bf16[512,512]{1,0:T(8,128)(2,1)S(1)}, u32[]{:S(2)}, u32[]{:S(2)}) collective-permute-start(bf16[512,512]{1,0:T(8,128)(2,1)S(1)} %get-tuple-element.84), channel_id=1, source_target_pairs={{0,32},{32,0},{1,33},{33,1},{2,34},{34,2},{3,35},{35,3},{4,36},{36... | collective-permute-start | bytes 1572872 | tf_op jit(solution)/shard_map/ppermute | solution.py:443
  48.6 6.9 %collective-permute-start.11 = (bf16[512,256]{1,0:T(8,128)(2,1)S(1)}, bf16[512,256]{1,0:T(8,128)(2,1)S(1)}, u32[]{:S(2)}, u32[]{:S(2)}) collective-permute-start(bf16[512,256]{1,0:T(8,128)(2,1)S(1)} %get-tuple-element.91), channel_id=1, source_target_pairs={{0,16},{8,24},{16,0},{24,8},{1,17},{9,25},{17,1},{25,9},{2,18},{10... | collective-permute-start | bytes 786440 | tf_op jit(solution)/shard_map/ppermute | solution.py:43
  50.1 8.1 %collective-permute-start.12 = (bf16[512,256]{1,0:T(8,128)(2,1)S(1)}, bf16[512,256]{1,0:T(8,128)(2,1)S(1)}, u32[]{:S(2)}, u32[]{:S(2)}) collective-permute-start(bf16[512,256]{1,0:T(8,128)(2,1)S(1)} %get-tuple-element.92), channel_id=1, source_target_pairs={{0,24},{8,0},{16,8},{24,16},{1,25},{9,1},{17,9},{25,17},{2,26},{10... | collective-permute-start | bytes 786440 | tf_op jit(solution)/shard_map/ppermute | solution.py:43
  51.4 8.6 %collective-permute-start.13 = (bf16[512,256]{1,0:T(8,128)(2,1)S(1)}, bf16[512,256]{1,0:T(8,128)(2,1)S(1)}, u32[]{:S(2)}, u32[]{:S(2)}) collective-permute-start(bf16[512,256]{1,0:T(8,128)(2,1)S(1)} %get-tuple-element.93), channel_id=1, source_target_pairs={{0,8},{8,16},{16,24},{24,0},{1,9},{9,17},{17,25},{25,1},{2,10},{10... | collective-permute-start | bytes 786440 | tf_op jit(solution)/shard_map/ppermute | solution.py:43
  51.6 8.3 %copy-start.2 = (s32[1024,1]{0,1:T(1,128)S(1)}, s32[1024,1]{0,1:T(1,128)}, u32[]{:S(2)}) copy-start(s32[1024,1]{0,1:T(1,128)} %param.19) | copy-start | bytes 12292
  55.3 51.1 %copy-start = (bf16[1024,1024]{1,0:T(8,128)(2,1)S(1)}, bf16[1024,1024]{1,0:T(8,128)(2,1)}, u32[]{:S(2)}) copy-start(bf16[1024,1024]{1,0:T(8,128)(2,1)} %wk_ref.1) | copy-start | bytes 6291460
  55.3 51.1 %copy-start.1 = (bf16[1024,1024]{1,0:T(8,128)(2,1)S(1)}, bf16[1024,1024]{1,0:T(8,128)(2,1)}, u32[]{:S(2)}) copy-start(bf16[1024,1024]{1,0:T(8,128)(2,1)} %wv_ref.1) | copy-start | bytes 6291460
  82.7 16.4 %collective-permute-start.14 = (bf16[1024,256]{1,0:T(8,128)(2,1)S(1)}, bf16[1024,256]{1,0:T(8,128)(2,1)S(1)}, u32[]{:S(2)}, u32[]{:S(2)}) collective-permute-start(bf16[1024,256]{1,0:T(8,128)(2,1)S(1)} %bitcast.4), channel_id=1, source_target_pairs={{0,2},{1,7},{2,4},{3,1},{4,6},{5,3},{6,0},{7,5},{8,10},{9,15},{10,... | collective-permute-start | bytes 1572872 | tf_op jit(solution)/shard_map/ppermute | solution.py:51
  85.2 14.0 %collective-permute-start.15 = (bf16[1024,256]{1,0:T(8,128)(2,1)S(1)}, bf16[1024,256]{1,0:T(8,128)(2,1)S(1)}, u32[]{:S(2)}, u32[]{:S(2)}) collective-permute-start(bf16[1024,256]{1,0:T(8,128)(2,1)S(1)} %bitcast.5), channel_id=1, source_target_pairs={{0,6},{1,3},{2,0},{3,5},{4,2},{5,7},{6,4},{7,1},{8,14},{9,11},{10,... | collective-permute-start | bytes 1572872 | tf_op jit(solution)/shard_map/ppermute | solution.py:51
  85.2 6.0 %collective-permute-start.16 = (bf16[128,512]{1,0:T(8,128)(2,1)S(1)}, bf16[128,512]{1,0:T(8,128)(2,1)S(1)}, u32[]{:S(2)}, u32[]{:S(2)}) collective-permute-start(bf16[128,512]{1,0:T(8,128)(2,1)S(1)} %get-tuple-element.98), channel_id=1, source_target_pairs={{0,64},{32,96},{64,128},{96,160},{128,192},{160,224},{192,0},{224,... | collective-permute-start | bytes 393224 | tf_op jit(solution)/shard_map/ppermute | solution.py:43
  87.1 11.8 %collective-permute-start.17 = (bf16[128,512]{1,0:T(8,128)(2,1)S(1)}, bf16[128,512]{1,0:T(8,128)(2,1)S(1)}, u32[]{:S(2)}, u32[]{:S(2)}) collective-permute-start(bf16[128,512]{1,0:T(8,128)(2,1)S(1)} %get-tuple-element.99), channel_id=1, source_target_pairs={{0,192},{32,224},{64,0},{96,32},{128,64},{160,96},{192,128},{224,1... | collective-permute-start | bytes 393224 | tf_op jit(solution)/shard_map/ppermute | solution.py:43
  88.8 10.4 %collective-permute-start.18 = (bf16[128,512]{1,0:T(8,128)(2,1)S(1)}, bf16[128,512]{1,0:T(8,128)(2,1)S(1)}, u32[]{:S(2)}, u32[]{:S(2)}) collective-permute-start(bf16[128,512]{1,0:T(8,128)(2,1)S(1)} %get-tuple-element.100), channel_id=1, source_target_pairs={{0,128},{32,160},{64,192},{96,224},{128,0},{160,32},{192,64},{224,... | collective-permute-start | bytes 393224 | tf_op jit(solution)/shard_map/ppermute | solution.py:43
  91.3 17.2 %collective-permute-start.20 = (bf16[1024,256]{1,0:T(8,128)(2,1)S(1)}, bf16[1024,256]{1,0:T(8,128)(2,1)S(1)}, u32[]{:S(2)}, u32[]{:S(2)}) collective-permute-start(bf16[1024,256]{1,0:T(8,128)(2,1)S(1)} %bitcast.6), channel_id=1, source_target_pairs={{0,1},{1,0},{2,3},{3,2},{4,5},{5,4},{6,7},{7,6},{8,9},{9,8},{10,11... | collective-permute-start | bytes 1572872 | tf_op jit(solution)/shard_map/ppermute | solution.py:43
  99.2 9.3 %collective-permute-start.21 = (bf16[1024,256]{1,0:T(8,128)(2,1)S(1)}, bf16[1024,256]{1,0:T(8,128)(2,1)S(1)}, u32[]{:S(2)}, u32[]{:S(2)}) collective-permute-start(bf16[1024,256]{1,0:T(8,128)(2,1)S(1)} %collective-permute-done.14._.refs_2_), channel_id=1, source_target_pairs={{0,1},{1,0},{2,3},{3,2},{4,5},{5,4},{6,7},{7,6},{8,9},{9,8},{10,11... | collective-permute-start | bytes 1572872 | tf_op jit(solution)/shard_map/ppermute | solution.py:43
  104.1 4.3 %collective-permute-start.22 = (bf16[1024,256]{1,0:T(8,128)(2,1)S(1)}, bf16[1024,256]{1,0:T(8,128)(2,1)S(1)}, u32[]{:S(2)}, u32[]{:S(2)}) collective-permute-start(bf16[1024,256]{1,0:T(8,128)(2,1)S(1)} %collective-permute-done.15.refs_4_), channel_id=1, source_target_pairs={{0,1},{1,0},{2,3},{3,2},{4,5},{5,4},{6,7},{7,6},{8,9},{9,8},{10,11... | collective-permute-start | bytes 1572872 | tf_op jit(solution)/shard_map/ppermute | solution.py:43
  104.2 8.3 %collective-permute-start.19 = (bf16[1024,256]{1,0:T(8,128)(2,1)S(1)}, bf16[1024,256]{1,0:T(8,128)(2,1)S(1)}, u32[]{:S(2)}, u32[]{:S(2)}) collective-permute-start(bf16[1024,256]{1,0:T(8,128)(2,1)S(1)} %collective-permute-done.14._.refs_2_), channel_id=1, source_target_pairs={{0,2},{1,7},{2,4},{3,1},{4,6},{5,3},{6,0},{7,5},{8,10},{9,15},{10,... | collective-permute-start | bytes 1572872 | tf_op jit(solution)/shard_map/ppermute | solution.py:51
  112.5 4.0 %collective-permute-start.23 = (bf16[1024,256]{1,0:T(8,128)(2,1)S(1)}, bf16[1024,256]{1,0:T(8,128)(2,1)S(1)}, u32[]{:S(2)}, u32[]{:S(2)}) collective-permute-start(bf16[1024,256]{1,0:T(8,128)(2,1)S(1)} %collective-permute-done.19.refs_0_), channel_id=1, source_target_pairs={{0,1},{1,0},{2,3},{3,2},{4,5},{5,4},{6,7},{7,6},{8,9},{9,8},{10,11... | collective-permute-start | bytes 1572872 | tf_op jit(solution)/shard_map/ppermute | solution.py:43

commit v4 on v3

--- a/solution.py
+++ b/solution.py
@@ -135,19 +135,16 @@
     stat_at[8 * c : 8 * c + 8, ROWS:] = stats[:, ROWS:]
 
 
-def attend_tile(c, b, q_at, g_at, stat_at, kv, kv_acc, dq_at):
+def attend_tile(c, kv_ref, q_at, g_at, stat_at):
     rows = pl.ds(pl.multiple_of(c * ROWS, ROWS), ROWS)
-    block = pl.ds(pl.multiple_of(b * BLOCK, BLOCK), BLOCK)
     q, g = q_at[rows, :], g_at[rows, :]
     stat = pl.ds(pl.multiple_of(c * 8, 8), 8)
     total, dots = stat_at[stat, 0:ROWS][0:1, :], stat_at[stat, ROWS:][0:1, :]
-    k, v = kv[block, 0:HD], kv[block, HD : 2 * HD]
+    k, v = kv_ref[:, 0:HD], kv_ref[:, HD : 2 * HD]
     p = jnp.exp2(dot32(k, q, NT) * (SCALE * LOG2E) - total)
     ds = (p * (dot32(v, g, NT) - dots)).astype(jnp.bfloat16)
-    kv_acc[block, HD : 2 * HD] += dot32(p.astype(jnp.bfloat16), g, NN)
-    kv_acc[block, 0:HD] += dot32(ds, q, NN)
-    dq = pl.ds(pl.multiple_of(c * HD, HD), HD)
-    dq_at[dq, :] += dot32(k, ds, TN)
+    dv = dot32(p.astype(jnp.bfloat16), g, NN)
+    return dot32(ds, q, NN), dv, dot32(k, ds, TN)
 
 
 def message_scratch(n):
@@ -166,41 +163,54 @@
     operands = list(messages) + list(blocks) + in_acc + in_dq + in_odd
     n_in = len(operands)
     n_dq = 1 if odd else n
+    in_place = acc_type == jnp.float32 and len(in_acc) == nb
+    aliases = {n + nb + b: n_dq + b for b in range(nb)} if in_place else {}
 
     def body(*refs):
         ins = list(refs[:n_in])
         dq_refs = refs[n_in : n_in + n_dq]
         out_refs = refs[n_in + n_dq : n_in + n_dq + nb]
-        q_at, g_at, stat_at, kv_at, acc_at, dq_at = refs[n_in + n_dq + nb :]
+        q_at, g_at, stat_at, dq_at = refs[n_in + n_dq + nb :]
         take = lambda count: [ins.pop(0) for _ in range(count)]
         msg_refs, kv_refs = take(n), take(nb)
         acc_refs = [take(1)[0] if a is not None else None for a in accs]
         dq_ins = [take(1)[0] if a is not None else None for a in dqs]
-        for b in range(nb):
-            block = slice(b * BLOCK, (b + 1) * BLOCK)
-            kv_at[block, :] = kv_refs[b][...]
-            if acc_refs[b] is None:
-                acc_at[block, :] = jnp.zeros((BLOCK, 2 * HD), jnp.float32)
-            else:
-                acc_at[block, :] = acc_refs[b][...]
         for c in range(n):
             load_message(msg_refs[c], c, q_at, g_at, stat_at)
-            rows = slice(c * HD, (c + 1) * HD)
-            if dq_ins[c] is None:
-                dq_at[rows, :] = jnp.zeros((HD, ROWS), jnp.float32)
-            else:
-                dq_at[rows, :] = dq_ins[c][...]
-
-        def step(b, carry):
+            if dq_ins[c] is not None:
+                dq_at[c * HD : (c + 1) * HD, :] = dq_ins[c][...]
+        if not in_place and n > 1:
+            for b in range(nb):
+                out_refs[b][...] = jnp.zeros_like(out_refs[b])
+
+        def step(c, carry):
+            dq = 0.0
+            for b in range(nb):
+                dk, dv, dq_b = attend_tile(c, kv_refs[b], q_at, g_at, stat_at)
+                dq = dq + dq_b
+                if n == 1:
+                    if acc_refs[b] is not None:
+                        dk = dk + acc_refs[b][:, 0:HD]
+                        dv = dv + acc_refs[b][:, HD : 2 * HD]
+                    if final:
+                        dk = dk * SCALE
+                    out_refs[b][:, 0:HD] = dk.astype(acc_type)
+                    out_refs[b][:, HD : 2 * HD] = dv.astype(acc_type)
+                else:
+                    out_refs[b][:, 0:HD] += dk
+                    out_refs[b][:, HD : 2 * HD] += dv
+            rows = pl.ds(pl.multiple_of(c * HD, HD), HD)
+            dq_at[rows, :] = dq_at[rows, :] + dq if in_dq else dq
+            return carry
+
+        if n == 1 or nb == 1:
             for c in range(n):
-                attend_tile(c, b, q_at, g_at, stat_at, kv_at, acc_at, dq_at)
-            return carry
-
-        if n == 1 or nb == 1:
+                step(c, 0)
+        else:
+            lax.fori_loop(0, n, step, 0)
+        if final and n > 1:
             for b in range(nb):
-                step(b, 0)
-        else:
-            lax.fori_loop(0, nb, step, 0)
+                out_refs[b][:, 0:HD] = out_refs[b][:, 0:HD] * SCALE
         if odd:
             for c, ref in enumerate(ins):
                 dq_refs[0][c * HD : (c + 1) * HD, :] = ref[...]
@@ -208,13 +218,6 @@
         else:
             for c in range(n):
                 dq_refs[c][...] = dq_at[c * HD : (c + 1) * HD, :].astype(dq_type[c])
-        for b in range(nb):
-            block = slice(b * BLOCK, (b + 1) * BLOCK)
-            dk, dv = acc_at[block, 0:HD], acc_at[block, HD : 2 * HD]
-            if final:
-                dk = dk * SCALE
-            out_refs[b][:, 0:HD] = dk.astype(acc_type)
-            out_refs[b][:, HD : 2 * HD] = dv.astype(acc_type)
 
     if odd:
         out_shape = [jax.ShapeDtypeStruct(((len(in_odd) + n) * HD, ROWS), dq_type)]
@@ -224,12 +227,8 @@
     outs = pl.pallas_call(
         body,
         out_shape=out_shape,
-        scratch_shapes=message_scratch(n)
-        + [
-            pltpu.VMEM((nb * BLOCK, 2 * HD), jnp.bfloat16),
-            pltpu.VMEM((nb * BLOCK, 2 * HD), jnp.float32),
-            pltpu.VMEM((n * HD, ROWS), jnp.float32),
-        ],
+        scratch_shapes=message_scratch(n) + [pltpu.VMEM((n * HD, ROWS), jnp.float32)],
+        input_output_aliases=aliases,
         compiler_params=pltpu.CompilerParams(vmem_limit_bytes=VMEM),
         cost_estimate=pl.CostEstimate(
             flops=n * 20 * ROWS * nb * BLOCK * HD,
@@ -336,9 +335,9 @@
 def project(name, pieces, first, weight, total=None):
     cols = weight.shape[0]
     n = len(pieces)
-    tile = 512
+    final = total is not None
+    tile = 256 if final else 512
     n_tile = SLOT_ROWS // tile
-    final = total is not None
     feats = slice(2 * HD * first, 2 * HD * (first + n))
 
     def product(refs, w_ref, rows):
@@ -456,15 +455,19 @@
     first, second = shift_by_core(mine, 1), shift_by_core(mine, -1)
     others = [shift(rows, "z", offset) for rows, offset in zip(sends, EVEN[1:])]
     pieces = [mine, shift(mine, "core", 1)]
-    first, second, *others = lax.optimization_barrier((first, second, *others))
+    first, second, others[0], others[1] = lax.optimization_barrier(
+        (first, second, others[0], others[1])
+    )
     across = shift_by_core(first, 1)
     for rows in (first, second):
         pieces += [rows, shift(rows, "core", 1)]
-    query_grad = finish(keep, others)
     weight = merge(first, key_weight, value_weight)
     total = project("project_near", pieces, 0, weight)
-    across, total, query_grad = lax.optimization_barrier((across, total, query_grad))
+    others[2], total = lax.optimization_barrier((others[2], total))
+    across, total = lax.optimization_barrier((across, total))
     pieces = [across, shift(across, "core", 1)]
+    query_grad = finish(keep, others)
+    total, query_grad = lax.optimization_barrier((total, query_grad))
     return query_grad, project("project_across", pieces, 6, weight, total)
 
 

time: 119 us -> 115 us (0.966)
  starting transfers between devices: 46.8 us -> 41.3 us
  waiting for transfers between devices: 13.3 us -> 15.8 us
    ppermute x20, starting transfers between devices: 40.5 us -> 36.4 us  [shift(): lax.ppermute(a, Z if axis == 'z' else axis, [(i, (i + k) % n) for i in ra...]
    ppermute x20, waiting for transfers between devices: 11.1 us -> 13.1 us  [shift(): lax.ppermute(a, Z if axis == 'z' else axis, [(i, (i + k) % n) for i in ra...]
    ppermute x3, starting transfers between devices: 4.68 us -> 3.32 us  [shift_by_core(): return lax.ppermute(a, ('x', 'core'), pairs)]
  transfers between devices with their start and end apart: 24 -> 24, of which waited for: 9 -> 10; matrix products, arithmetic and copies ran while one was open for 0% -> 0% of each run, Pallas kernels for 24% -> 25%
where the time goes in v4:
time: 115 us; the launch traced here: 114 us
  starting transfers between devices  41.3 us (36%)
  Pallas kernels  33.3 us (29%)
  blocking collectives  21 us (18%)
  waiting for transfers between devices  15.8 us (14%)
  local copies, waits for them, and re-layouts  1.93 us (2%)
    ppermute x20, starting transfers between devices, shift(): lax.ppermute(a, Z if axis == 'z' else axis, [(i, (i + k) % n) for i in ra...  36.4 us
    pallas_call x6, Pallas kernels, attend(): pl.pallas_call(body, out_shape=out_shape, scratch_shapes=message_scratch(...  22.6 us
    all_to_all x1, blocking collectives, on_device(): lax.all_to_all(outgoing, Z + ('y',), split_axis=0, concat_axis=0, tiled=T...  21 us
    ppermute x20, waiting for transfers between devices, shift(): lax.ppermute(a, Z if axis == 'z' else axis, [(i, (i + k) % n) for i in ra...  13.1 us
    pallas_call x2, Pallas kernels, project(): pl.pallas_call(body_final if final else body_first, out_shape=jax.ShapeDt...  5.57 us
    ppermute x3, starting transfers between devices, shift_by_core(): return lax.ppermute(a, ('x', 'core'), pairs)  3.32 us
  transfers between devices with their start and end apart: 24, of which 10 were waited for; matrix products, arithmetic and copies ran while one was open for 0% of the time, Pallas kernels for 25%

profile of v4, /device:TPU:1, one launch (start us, length us, event | category | flops | bytes accessed | tf_op | source)
XLA Modules:
  0.0 114.4 jit_solution(8030808784197685434)
XLA Ops:
  0.6 2.0 %pack.1 = (bf16[144,1024]{1,0:T(8,128)(2,1)}, bf16[512,256]{1,0:T(8,128)(2,1)}) custom-call(s32[32]{0:T(128)} %len_ref.1, bf16[64,1024]{1,0:T(8,128)(2,1)} %q_ref.1, bf16[64,1024]{1,0:T(8,128)(2,1)} %g_ref.1, bf16[8,64]{1,0:T(8,128)(2,1)} %total_ref.1, bf16[8,64]{1,0:T(8,128)(2,1)} %dot_ref.1, bf16[512,128]{1,0:T(8,128)(2,1)} %k_ref.1, bf16[512,128]{1,0:T(8,128)(2,1)} %v_ref.1), custom_call_target="tpu_custom_call" | custom-call | bytes 1048576 | tf_op jit(solution)/shard_map/pack/pallas_call | solution.py:97
  2.6 2.5 %collective-permute-start = (bf16[144,1024]{1,0:T(8,128)(2,1)}, bf16[144,1024]{1,0:T(8,128)(2,1)S(1)}, u32[]{:S(2)}, u32[]{:S(2)}) collective-permute-start(bf16[144,1024]{1,0:T(8,128)(2,1)} %get-tuple-element.58.refs_0_), channel_id=1, source_target_pairs={{0,32},{32,64},{64,96},{96,128},{128,160},{160,192},{192,224},{224... | collective-permute-start | bytes 884744 | tf_op jit(solution)/shard_map/ppermute | solution.py:43
  5.2 4.0 %collective-permute-start.2 = (bf16[144,1024]{1,0:T(8,128)(2,1)}, bf16[144,1024]{1,0:T(8,128)(2,1)S(1)}, u32[]{:S(2)}, u32[]{:S(2)}) collective-permute-start(bf16[144,1024]{1,0:T(8,128)(2,1)} %get-tuple-element.58.refs_0_), channel_id=1, source_target_pairs={{0,224},{32,0},{64,32},{96,64},{128,96},{160,128},{192,160},{224,1... | collective-permute-start | bytes 884744 | tf_op jit(solution)/shard_map/ppermute | solution.py:43
  9.2 1.3 %collective-permute-start.6 = (bf16[512,256]{1,0:T(8,128)(2,1)}, bf16[512,256]{1,0:T(8,128)(2,1)S(1)}, u32[]{:S(2)}, u32[]{:S(2)}) collective-permute-start(bf16[512,256]{1,0:T(8,128)(2,1)} %get-tuple-element.59.refs_3_.refs_5_), channel_id=1, source_target_pairs={{0,8},{8,16},{16,24},{24,0},{1,9},{9,17},{17,25},{25,1},{2,10},{10... | collective-permute-start | bytes 786440 | tf_op jit(solution)/shard_map/ppermute | solution.py:43
  10.5 1.4 %collective-permute-start.7 = (bf16[512,256]{1,0:T(8,128)(2,1)}, bf16[512,256]{1,0:T(8,128)(2,1)S(1)}, u32[]{:S(2)}, u32[]{:S(2)}) collective-permute-start(bf16[512,256]{1,0:T(8,128)(2,1)} %get-tuple-element.59.refs_3_.refs_5_), channel_id=1, source_target_pairs={{0,24},{8,0},{16,8},{24,16},{1,25},{9,1},{17,9},{25,17},{2,26},{10... | collective-permute-start | bytes 786440 | tf_op jit(solution)/shard_map/ppermute | solution.py:43
  11.9 1.6 %collective-permute-start.8 = (bf16[512,256]{1,0:T(8,128)(2,1)}, bf16[512,256]{1,0:T(8,128)(2,1)S(1)}, u32[]{:S(2)}, u32[]{:S(2)}) collective-permute-start(bf16[512,256]{1,0:T(8,128)(2,1)} %get-tuple-element.59.refs_3_.refs_5_), channel_id=1, source_target_pairs={{0,16},{8,24},{16,0},{24,8},{1,17},{9,25},{17,1},{25,9},{2,18},{10... | collective-permute-start | bytes 786440 | tf_op jit(solution)/shard_map/ppermute | solution.py:43
  13.6 2.5 %collective-permute-done.refs_1_ = bf16[144,1024]{1,0:T(8,128)(2,1)S(1)} collective-permute-done((bf16[144,1024]{1,0:T(8,128)(2,1)}, bf16[144,1024]{1,0:T(8,128)(2,1)S(1)}, u32[]{:S(2)}, u32[]{:S(2)}) %collective-permute-start) | collective-permute-done | bytes 294944 | tf_op jit(solution)/shard_map/ppermute | solution.py:43
  16.0 0.0 collective-permute-start.1
  16.0 0.0 collective-permute-done.2.refs_2_
  16.0 2.7 %collective-permute-start.3 = (bf16[144,1024]{1,0:T(8,128)(2,1)S(1)}, bf16[144,1024]{1,0:T(8,128)(2,1)S(1)}, u32[]{:S(2)}, u32[]{:S(2)}) collective-permute-start(bf16[144,1024]{1,0:T(8,128)(2,1)S(1)} %collective-permute-done.2.refs_2_), channel_id=1, source_target_pairs={{0,224},{32,0},{64,32},{96,64},{128,96},{160,128},{192,160},{224,1... | collective-permute-start | bytes 884744 | tf_op jit(solution)/shard_map/ppermute | solution.py:43
  18.7 1.0 copy-done.3
  19.7 0.9 copy-done.4
  20.6 2.0 %home_first.1 = (f32[128,512]{1,0:T(8,128)S(1)}, f32[128,512]{1,0:T(8,128)S(1)}, f32[128,512]{1,0:T(8,128)S(1)}, f32[512,256]{1,0:T(8,128)S(1)}) custom-call(bf16[144,1024]{1,0:T(8,128)(2,1)S(1)} %copy-done.3, bf16[144,1024]{1,0:T(8,128)(2,1)S(1)} %collective-permute-done.refs_1_, bf16[144,1024]{1,0:T(8,128)(2,1)S(1)} %collective-permute-done.2.refs_2_, ...), custom_call_target="tpu_custom_call" | custom-call | flops 2013265920 | bytes 2097152 | tf_op jit(solution)/shard_map/home_first/pallas_call | solution.py:227
  22.7 0.0 collective-permute-done.6.refs_3_.refs_2_.refs_1_
  22.7 0.0 collective-permute-done.7.refs_4_.refs_3_.refs_2_
  22.7 1.6 %collective-permute-done.8.refs_5_.refs_4_.refs_3_ = bf16[512,256]{1,0:T(8,128)(2,1)S(1)} collective-permute-done((bf16[512,256]{1,0:T(8,128)(2,1)}, bf16[512,256]{1,0:T(8,128)(2,1)S(1)}, u32[]{:S(2)}, u32[]{:S(2)}) %collective-permute-start.8) | collective-permute-done | bytes 262176 | tf_op jit(solution)/shard_map/ppermute | solution.py:43
  24.3 6.5 %away_near.1 = (f32[128,512]{1,0:T(8,128)S(1)}, bf16[128,512]{1,0:T(8,128)(2,1)S(1)}, bf16[128,512]{1,0:T(8,128)(2,1)S(1)}, f32[512,256]{1,0:T(8,128)S(1)}, f32[...) custom-call(bf16[144,1024]{1,0:T(8,128)(2,1)S(1)} %copy-done.3, bf16[144,1024]{1,0:T(8,128)(2,1)S(1)} %collective-permute-done.refs_1_, ...), custom_call_target="tpu_custom_call" | custom-call | flops 6039797760 | bytes 2097152 | tf_op jit(solution)/shard_map/away_near/pallas_call | solution.py:227
  30.8 0.0 collective-permute-done.1.refs_0_
  30.8 0.0 collective-permute-done.3.refs_1_
  30.8 0.1 collective-permute-start.4
  30.9 2.7 %collective-permute-start.5 = (bf16[144,1024]{1,0:T(8,128)(2,1)S(1)}, bf16[144,1024]{1,0:T(8,128)(2,1)S(1)}, u32[]{:S(2)}, u32[]{:S(2)}) collective-permute-start(bf16[144,1024]{1,0:T(8,128)(2,1)S(1)} %collective-permute-done.3.refs_1_), channel_id=1, source_target_pairs={{0,224},{32,0},{64,32},{96,64},{128,96},{160,128},{192,160},{224,1... | collective-permute-start | bytes 884744 | tf_op jit(solution)/shard_map/ppermute | solution.py:43
  33.6 4.2 %away_two.1 = (f32[128,512]{1,0:T(8,128)S(1)}, f32[128,512]{1,0:T(8,128)S(1)}, f32[512,256]{1,0:T(8,128)S(1)}, f32[512,256]{1,0:T(8,128)S(1)}, f32[512,256]{1,0:T(8,128)S(1)}) custom-call(bf16[144,1024]{1,0:T(8,128)(2,1)S(1)} %collective-permute-done.1.refs_0_, ...), custom_call_target="tpu_custom_call", output_to_operand_aliasing={{2}: (5, {}), {3}: (6, {}), {4}: (7, {})} | custom-call | flops 4026531840 | bytes 2097152 | tf_op jit(solution)/shard_map/away_two/pallas_call | solution.py:227
  37.8 0.9 collective-permute-done.4.refs_0_
  38.8 0.0 collective-permute-done.5.refs_1_
  38.8 0.0 collective-permute-start.9
  38.8 5.5 %all_three.1 = (bf16[512,512]{1,0:T(8,128)(2,1)S(1)}, f32[512,256]{1,0:T(8,128)S(1)}, f32[512,256]{1,0:T(8,128)S(1)}, f32[512,256]{1,0:T(8,128)S(1)}, f32[512,256]{1,0:T(8,128)S(1)}) custom-call(bf16[144,1024]{1,0:T(8,128)(2,1)S(1)} %collective-permute-done.4.refs_0_, ...), custom_call_target="tpu_custom_call", output_to_operand_aliasing={{1}: (6, {}), {2}: (7, {}), {3}: (8, {}), {4}: (9, {})} | custom-call | flops 5368709120 | bytes 2097152 | tf_op jit(solution)/shard_map/all_three/pallas_call | solution.py:227
  44.3 1.6 %collective-permute-start.10 = (bf16[512,512]{1,0:T(8,128)(2,1)S(1)}, bf16[512,512]{1,0:T(8,128)(2,1)S(1)}, u32[]{:S(2)}, u32[]{:S(2)}) collective-permute-start(bf16[512,512]{1,0:T(8,128)(2,1)S(1)} %get-tuple-element.86), channel_id=1, source_target_pairs={{0,32},{32,0},{1,33},{33,1},{2,34},{34,2},{3,35},{35,3},{4,36},{36... | collective-permute-start | bytes 1572872 | tf_op jit(solution)/shard_map/ppermute | solution.py:442
  45.9 0.0 collective-permute-done.9.refs_0_.refs_2_
  45.9 2.3 %away_far.1 = (f32[128,512]{1,0:T(8,128)S(1)}, bf16[512,256]{1,0:T(8,128)(2,1)S(1)}, bf16[512,256]{1,0:T(8,128)(2,1)S(1)}, bf16[512,256]{1,0:T(8,128)(2,1)S(1)}) custom-call(bf16[144,1024]{1,0:T(8,128)(2,1)S(1)} %collective-permute-done.9.refs_0_.refs_2_, bf16[512,256]{1,0:T(8,128)(2,1)S(1)} %collective-permute-done.6.refs_3_.refs_2_.refs_1_, ...), custom_call_target="tpu_custom_call" | custom-call | flops 2013265920 | bytes 2097152 | tf_op jit(solution)/shard_map/away_far/pallas_call | solution.py:227
  48.2 1.5 %collective-permute-start.11 = (bf16[512,256]{1,0:T(8,128)(2,1)S(1)}, bf16[512,256]{1,0:T(8,128)(2,1)S(1)}, u32[]{:S(2)}, u32[]{:S(2)}) collective-permute-start(bf16[512,256]{1,0:T(8,128)(2,1)S(1)} %get-tuple-element.93), channel_id=1, source_target_pairs={{0,16},{8,24},{16,0},{24,8},{1,17},{9,25},{17,1},{25,9},{2,18},{10... | collective-permute-start | bytes 786440 | tf_op jit(solution)/shard_map/ppermute | solution.py:43
  49.7 1.3 %collective-permute-start.12 = (bf16[512,256]{1,0:T(8,128)(2,1)S(1)}, bf16[512,256]{1,0:T(8,128)(2,1)S(1)}, u32[]{:S(2)}, u32[]{:S(2)}) collective-permute-start(bf16[512,256]{1,0:T(8,128)(2,1)S(1)} %get-tuple-element.94), channel_id=1, source_target_pairs={{0,24},{8,0},{16,8},{24,16},{1,25},{9,1},{17,9},{25,17},{2,26},{10... | collective-permute-start | bytes 786440 | tf_op jit(solution)/shard_map/ppermute | solution.py:43
  51.0 0.2 collective-permute-start.13
  51.2 2.0 %home_last.1 = (f32[128,512]{1,0:T(8,128)S(1)}, f32[128,512]{1,0:T(8,128)S(1)}, f32[128,512]{1,0:T(8,128)S(1)}, f32[512,256]{1,0:T(8,128)S(1)}) custom-call(bf16[144,1024]{1,0:T(8,128)(2,1)S(1)} %collective-permute-done.1.refs_0_, bf16[144,1024]{1,0:T(8,128)(2,1)S(1)} %collective-permute-done.3.refs_1_, ...), custom_call_target="tpu_custom_call", output_to_operand_aliasing={{3}: (4, {})} | custom-call | flops 2013265920 | bytes 2097152 | tf_op jit(solution)/shard_map/home_last/pallas_call | solution.py:227
  53.2 1.5 %collective-permute-done.10.got_ref = bf16[512,512]{1,0:T(8,128)(2,1)S(1)} collective-permute-done((bf16[512,512]{1,0:T(8,128)(2,1)S(1)}, bf16[512,512]{1,0:T(8,128)(2,1)S(1)}, u32[]{:S(2)}, u32[]{:S(2)}) %collective-permute-start.10) | collective-permute-done | bytes 524320 | tf_op jit(solution)/shard_map/ppermute | solution.py:442
  54.7 0.1 pair.1
  54.8 0.2 collective-permute-done.11.a_ref
  55.0 2.7 %collective-permute-done.12.b_ref = bf16[512,256]{1,0:T(8,128)(2,1)S(1)} collective-permute-done((bf16[512,256]{1,0:T(8,128)(2,1)S(1)}, bf16[512,256]{1,0:T(8,128)(2,1)S(1)}, u32[]{:S(2)}, u32[]{:S(2)}) %collective-permute-start.12) | collective-permute-done | bytes 262176 | tf_op jit(solution)/shard_map/ppermute | solution.py:43
  57.7 1.8 %collective-permute-done.13.c_ref = bf16[512,256]{1,0:T(8,128)(2,1)S(1)} collective-permute-done((bf16[512,256]{1,0:T(8,128)(2,1)S(1)}, bf16[512,256]{1,0:T(8,128)(2,1)S(1)}, u32[]{:S(2)}, u32[]{:S(2)}) %collective-permute-start.13) | collective-permute-done | bytes 262176 | tf_op jit(solution)/shard_map/ppermute | solution.py:43
  59.5 1.0 dispatch.1
  60.6 21.0 %all_to_all.12 = bf16[32,32,256]{2,1,0:T(8,128)(2,1)S(1)} all-to-all(bf16[32,32,256]{2,1,0:T(8,128)(2,1)S(1)} %bitcast.3), channel_id=1, replica_groups=mesh['zq'=4,'zp'=2,'y'=4,'x'=4,'core'=2] {'zq','zp','y'}, dimensions={0} | all-to-all | bytes 1048576 | tf_op jit(solution)/shard_map/all_to_all | solution.py:452
  81.5 2.5 %collective-permute-start.14 = (bf16[1024,256]{1,0:T(8,128)(2,1)S(1)}, bf16[1024,256]{1,0:T(8,128)(2,1)S(1)}, u32[]{:S(2)}, u32[]{:S(2)}) collective-permute-start(bf16[1024,256]{1,0:T(8,128)(2,1)S(1)} %bitcast.4), channel_id=1, source_target_pairs={{0,2},{1,7},{2,4},{3,1},{4,6},{5,3},{6,0},{7,5},{8,10},{9,15},{10,... | collective-permute-start | bytes 1572872 | tf_op jit(solution)/shard_map/ppermute | solution.py:51
  84.0 0.0 collective-permute-start.15
  84.0 2.2 %collective-permute-start.16 = (bf16[128,512]{1,0:T(8,128)(2,1)S(1)}, bf16[128,512]{1,0:T(8,128)(2,1)S(1)}, u32[]{:S(2)}, u32[]{:S(2)}) collective-permute-start(bf16[128,512]{1,0:T(8,128)(2,1)S(1)} %get-tuple-element.100), channel_id=1, source_target_pairs={{0,64},{32,96},{64,128},{96,160},{128,192},{160,224},{192,0},{224,... | collective-permute-start | bytes 393224 | tf_op jit(solution)/shard_map/ppermute | solution.py:43
  86.2 1.4 %collective-permute-start.17 = (bf16[128,512]{1,0:T(8,128)(2,1)S(1)}, bf16[128,512]{1,0:T(8,128)(2,1)S(1)}, u32[]{:S(2)}, u32[]{:S(2)}) collective-permute-start(bf16[128,512]{1,0:T(8,128)(2,1)S(1)} %get-tuple-element.101), channel_id=1, source_target_pairs={{0,192},{32,224},{64,0},{96,32},{128,64},{160,96},{192,128},{224,1... | collective-permute-start | bytes 393224 | tf_op jit(solution)/shard_map/ppermute | solution.py:43
  87.6 6.8 %collective-permute-start.20 = (bf16[1024,256]{1,0:T(8,128)(2,1)S(1)}, bf16[1024,256]{1,0:T(8,128)(2,1)S(1)}, u32[]{:S(2)}, u32[]{:S(2)}) collective-permute-start(bf16[1024,256]{1,0:T(8,128)(2,1)S(1)} %bitcast.6), channel_id=1, source_target_pairs={{0,1},{1,0},{2,3},{3,2},{4,5},{5,4},{6,7},{7,6},{8,9},{9,8},{10,11... | collective-permute-start | bytes 1572872 | tf_op jit(solution)/shard_map/ppermute | solution.py:43
  94.4 0.0 collective-permute-done.16.a_ref
  94.4 0.0 collective-permute-done.17.b_ref
  94.5 0.0 collective-permute-done.14._.refs_2_
  94.5 1.2 %collective-permute-done.15.refs_4_ = bf16[1024,256]{1,0:T(8,128)(2,1)S(1)} collective-permute-done((bf16[1024,256]{1,0:T(8,128)(2,1)S(1)}, bf16[1024,256]{1,0:T(8,128)(2,1)S(1)}, u32[]{:S(2)}, u32[]{:S(2)}) %collective-permute-start.15) | collective-permute-done | bytes 524320 | tf_op jit(solution)/shard_map/ppermute | solution.py:51
  95.6 4.0 %collective-permute-start.21 = (bf16[1024,256]{1,0:T(8,128)(2,1)S(1)}, bf16[1024,256]{1,0:T(8,128)(2,1)S(1)}, u32[]{:S(2)}, u32[]{:S(2)}) collective-permute-start(bf16[1024,256]{1,0:T(8,128)(2,1)S(1)} %collective-permute-done.14._.refs_2_), channel_id=1, source_target_pairs={{0,1},{1,0},{2,3},{3,2},{4,5},{5,4},{6,7},{7,6},{8,9},{9,8},{10,11... | collective-permute-start | bytes 1572872 | tf_op jit(solution)/shard_map/ppermute | solution.py:43
  99.6 0.0 collective-permute-start.22
  99.6 0.8 collective-permute-start.18
  100.4 1.9 %collective-permute-start.19 = (bf16[128,512]{1,0:T(8,128)(2,1)S(1)}, bf16[128,512]{1,0:T(8,128)(2,1)S(1)}, u32[]{:S(2)}, u32[]{:S(2)}) collective-permute-start(bf16[128,512]{1,0:T(8,128)(2,1)S(1)} %get-tuple-element.103), channel_id=1, source_target_pairs={{0,128},{32,160},{64,192},{96,224},{128,0},{160,32},{192,64},{224,... | collective-permute-start | bytes 393224 | tf_op jit(solution)/shard_map/ppermute | solution.py:43
  102.4 1.2 %merge.1.refs_6_.refs_2_ = bf16[1024,2048]{1,0:T(8,128)(2,1)S(1)} custom-call(bf16[1024,256]{1,0:T(8,128)(2,1)S(1)} %collective-permute-done.14._.refs_2_, bf16[1024,1024]{1,0:T(8,128)(2,1)S(1)} %copy-done, bf16[1024,1024]{1,0:T(8,128)(2,1)S(1)} %copy-done.1), custom_call_target="tpu_custom_call" | custom-call | bytes 8388608 | tf_op jit(solution)/shard_map/merge/pallas_call | solution.py:324
  103.6 0.0 collective-permute-done.20.refs_1_
  103.6 0.0 collective-permute-done.21.refs_3_
  103.6 0.0 collective-permute-done.22.refs_5_
  103.6 3.5 %project_near.1.refs_3_ = f32[1024,1024]{1,0:T(8,128)S(1)} custom-call(bf16[1024,256]{1,0:T(8,128)(2,1)S(1)} %bitcast.7, bf16[1024,256]{1,0:T(8,128)(2,1)S(1)} %collective-permute-done.20.refs_1_, bf16[1024,256]{1,0:T(8,128)(2,1)S(1)} %collective-permute-done.14._.refs_2_, bf16[1024,256]{1,0:T(8,128)(2,1)S(1)} %collective-permute-done.21.refs_3_, ...), custom_call_target="tpu_custom_call" | custom-call | flops 3221225472 | bytes 6291456 | tf_op jit(solution)/shard_map/project_near/pallas_call | solution.py:367
  107.1 2.6 %collective-permute-done.19.c_ref = bf16[128,512]{1,0:T(8,128)(2,1)S(1)} collective-permute-done((bf16[128,512]{1,0:T(8,128)(2,1)S(1)}, bf16[128,512]{1,0:T(8,128)(2,1)S(1)}, u32[]{:S(2)}, u32[]{:S(2)}) %collective-permute-start.19) | collective-permute-done | bytes 131104 | tf_op jit(solution)/shard_map/ppermute | solution.py:43
  109.7 0.0 collective-permute-done.18.refs_0_
  109.7 0.8 collective-permute-start.23
  110.5 0.8 finish.1
  111.3 0.7 collective-permute-done.23.refs_1_
  112.0 2.1 %project_across.1 = bf16[1024,1024]{1,0:T(8,128)(2,1)} custom-call(bf16[1024,256]{1,0:T(8,128)(2,1)S(1)} %collective-permute-done.18.refs_0_, bf16[1024,256]{1,0:T(8,128)(2,1)S(1)} %collective-permute-done.23.refs_1_, bf16[1024,2048]{1,0:T(8,128)(2,1)S(1)} %merge.1.refs_6_.refs_2_, f32[1024,1024]{1,0:T(8,128)S(1)} %project_near.1.refs_3_), custom_call_target="tpu_custom_call" | custom-call | flops 1073741824 | bytes 6291456 | tf_op jit(solution)/shard_map/project_across/pallas_call | solution.py:367
  (10 shorter events, 0.0 us)
Async XLA Ops:
  2.6 13.4 %collective-permute-start = (bf16[144,1024]{1,0:T(8,128)(2,1)}, bf16[144,1024]{1,0:T(8,128)(2,1)S(1)}, u32[]{:S(2)}, u32[]{:S(2)}) collective-permute-start(bf16[144,1024]{1,0:T(8,128)(2,1)} %get-tuple-element.58.refs_0_), channel_id=1, source_target_pairs={{0,32},{32,64},{64,96},{96,128},{128,160},{160,192},{192,224},{224... | collective-permute-start | bytes 884744 | tf_op jit(solution)/shard_map/ppermute | solution.py:43
  5.2 10.9 %collective-permute-start.2 = (bf16[144,1024]{1,0:T(8,128)(2,1)}, bf16[144,1024]{1,0:T(8,128)(2,1)S(1)}, u32[]{:S(2)}, u32[]{:S(2)}) collective-permute-start(bf16[144,1024]{1,0:T(8,128)(2,1)} %get-tuple-element.58.refs_0_), channel_id=1, source_target_pairs={{0,224},{32,0},{64,32},{96,64},{128,96},{160,128},{192,160},{224,1... | collective-permute-start | bytes 884744 | tf_op jit(solution)/shard_map/ppermute | solution.py:43
  9.2 13.5 %collective-permute-start.6 = (bf16[512,256]{1,0:T(8,128)(2,1)}, bf16[512,256]{1,0:T(8,128)(2,1)S(1)}, u32[]{:S(2)}, u32[]{:S(2)}) collective-permute-start(bf16[512,256]{1,0:T(8,128)(2,1)} %get-tuple-element.59.refs_3_.refs_5_), channel_id=1, source_target_pairs={{0,8},{8,16},{16,24},{24,0},{1,9},{9,17},{17,25},{25,1},{2,10},{10... | collective-permute-start | bytes 786440 | tf_op jit(solution)/shard_map/ppermute | solution.py:43
  10.5 12.2 %collective-permute-start.7 = (bf16[512,256]{1,0:T(8,128)(2,1)}, bf16[512,256]{1,0:T(8,128)(2,1)S(1)}, u32[]{:S(2)}, u32[]{:S(2)}) collective-permute-start(bf16[512,256]{1,0:T(8,128)(2,1)} %get-tuple-element.59.refs_3_.refs_5_), channel_id=1, source_target_pairs={{0,24},{8,0},{16,8},{24,16},{1,25},{9,1},{17,9},{25,17},{2,26},{10... | collective-permute-start | bytes 786440 | tf_op jit(solution)/shard_map/ppermute | solution.py:43
  11.9 12.4 %collective-permute-start.8 = (bf16[512,256]{1,0:T(8,128)(2,1)}, bf16[512,256]{1,0:T(8,128)(2,1)S(1)}, u32[]{:S(2)}, u32[]{:S(2)}) collective-permute-start(bf16[512,256]{1,0:T(8,128)(2,1)} %get-tuple-element.59.refs_3_.refs_5_), channel_id=1, source_target_pairs={{0,16},{8,24},{16,0},{24,8},{1,17},{9,25},{17,1},{25,9},{2,18},{10... | collective-permute-start | bytes 786440 | tf_op jit(solution)/shard_map/ppermute | solution.py:43
  16.0 14.8 %collective-permute-start.1 = (bf16[144,1024]{1,0:T(8,128)(2,1)S(1)}, bf16[144,1024]{1,0:T(8,128)(2,1)S(1)}, u32[]{:S(2)}, u32[]{:S(2)}) collective-permute-start(bf16[144,1024]{1,0:T(8,128)(2,1)S(1)} %collective-permute-done.refs_1_), channel_id=1, source_target_pairs={{0,32},{32,64},{64,96},{96,128},{128,160},{160,192},{192,224},{224... | collective-permute-start | bytes 884744 | tf_op jit(solution)/shard_map/ppermute | solution.py:43
  16.0 14.8 %collective-permute-start.3 = (bf16[144,1024]{1,0:T(8,128)(2,1)S(1)}, bf16[144,1024]{1,0:T(8,128)(2,1)S(1)}, u32[]{:S(2)}, u32[]{:S(2)}) collective-permute-start(bf16[144,1024]{1,0:T(8,128)(2,1)S(1)} %collective-permute-done.2.refs_2_), channel_id=1, source_target_pairs={{0,224},{32,0},{64,32},{96,64},{128,96},{160,128},{192,160},{224,1... | collective-permute-start | bytes 884744 | tf_op jit(solution)/shard_map/ppermute | solution.py:43
  18.7 1.0 copy-start.3
  19.7 0.9 copy-start.4
  30.8 7.9 %collective-permute-start.4 = (bf16[144,1024]{1,0:T(8,128)(2,1)S(1)}, bf16[144,1024]{1,0:T(8,128)(2,1)S(1)}, u32[]{:S(2)}, u32[]{:S(2)}) collective-permute-start(bf16[144,1024]{1,0:T(8,128)(2,1)S(1)} %collective-permute-done.1.refs_0_), channel_id=1, source_target_pairs={{0,32},{32,64},{64,96},{96,128},{128,160},{160,192},{192,224},{224... | collective-permute-start | bytes 884744 | tf_op jit(solution)/shard_map/ppermute | solution.py:43
  30.9 7.8 %collective-permute-start.5 = (bf16[144,1024]{1,0:T(8,128)(2,1)S(1)}, bf16[144,1024]{1,0:T(8,128)(2,1)S(1)}, u32[]{:S(2)}, u32[]{:S(2)}) collective-permute-start(bf16[144,1024]{1,0:T(8,128)(2,1)S(1)} %collective-permute-done.3.refs_1_), channel_id=1, source_target_pairs={{0,224},{32,0},{64,32},{96,64},{128,96},{160,128},{192,160},{224,1... | collective-permute-start | bytes 884744 | tf_op jit(solution)/shard_map/ppermute | solution.py:43
  33.6 5.2 %copy-start.5 = (bf16[512,256]{1,0:T(8,128)(2,1)S(1)}, bf16[512,256]{1,0:T(8,128)(2,1)}, u32[]{:S(2)}) copy-start(bf16[512,256]{1,0:T(8,128)(2,1)} %get-tuple-element.59.refs_3_.refs_5_) | copy-start | bytes 786436
  38.8 7.1 %collective-permute-start.9 = (bf16[144,1024]{1,0:T(8,128)(2,1)S(1)}, bf16[144,1024]{1,0:T(8,128)(2,1)S(1)}, u32[]{:S(2)}, u32[]{:S(2)}) collective-permute-start(bf16[144,1024]{1,0:T(8,128)(2,1)S(1)} %collective-permute-done.4.refs_0_), channel_id=1, source_target_pairs={{0,32},{32,64},{64,96},{96,128},{128,160},{160,192},{192,224},{224... | collective-permute-start | bytes 884744 | tf_op jit(solution)/shard_map/ppermute | solution.py:43
  44.3 10.4 %collective-permute-start.10 = (bf16[512,512]{1,0:T(8,128)(2,1)S(1)}, bf16[512,512]{1,0:T(8,128)(2,1)S(1)}, u32[]{:S(2)}, u32[]{:S(2)}) collective-permute-start(bf16[512,512]{1,0:T(8,128)(2,1)S(1)} %get-tuple-element.86), channel_id=1, source_target_pairs={{0,32},{32,0},{1,33},{33,1},{2,34},{34,2},{3,35},{35,3},{4,36},{36... | collective-permute-start | bytes 1572872 | tf_op jit(solution)/shard_map/ppermute | solution.py:442
  48.2 6.9 %collective-permute-start.11 = (bf16[512,256]{1,0:T(8,128)(2,1)S(1)}, bf16[512,256]{1,0:T(8,128)(2,1)S(1)}, u32[]{:S(2)}, u32[]{:S(2)}) collective-permute-start(bf16[512,256]{1,0:T(8,128)(2,1)S(1)} %get-tuple-element.93), channel_id=1, source_target_pairs={{0,16},{8,24},{16,0},{24,8},{1,17},{9,25},{17,1},{25,9},{2,18},{10... | collective-permute-start | bytes 786440 | tf_op jit(solution)/shard_map/ppermute | solution.py:43
  49.7 8.0 %collective-permute-start.12 = (bf16[512,256]{1,0:T(8,128)(2,1)S(1)}, bf16[512,256]{1,0:T(8,128)(2,1)S(1)}, u32[]{:S(2)}, u32[]{:S(2)}) collective-permute-start(bf16[512,256]{1,0:T(8,128)(2,1)S(1)} %get-tuple-element.94), channel_id=1, source_target_pairs={{0,24},{8,0},{16,8},{24,16},{1,25},{9,1},{17,9},{25,17},{2,26},{10... | collective-permute-start | bytes 786440 | tf_op jit(solution)/shard_map/ppermute | solution.py:43
  51.0 8.6 %collective-permute-start.13 = (bf16[512,256]{1,0:T(8,128)(2,1)S(1)}, bf16[512,256]{1,0:T(8,128)(2,1)S(1)}, u32[]{:S(2)}, u32[]{:S(2)}) collective-permute-start(bf16[512,256]{1,0:T(8,128)(2,1)S(1)} %get-tuple-element.95), channel_id=1, source_target_pairs={{0,8},{8,16},{16,24},{24,0},{1,9},{9,17},{17,25},{25,1},{2,10},{10... | collective-permute-start | bytes 786440 | tf_op jit(solution)/shard_map/ppermute | solution.py:43
  51.1 8.4 %copy-start.2 = (s32[1024,1]{0,1:T(1,128)S(1)}, s32[1024,1]{0,1:T(1,128)}, u32[]{:S(2)}) copy-start(s32[1024,1]{0,1:T(1,128)} %param.19) | copy-start | bytes 12292
  54.7 47.6 %copy-start = (bf16[1024,1024]{1,0:T(8,128)(2,1)S(1)}, bf16[1024,1024]{1,0:T(8,128)(2,1)}, u32[]{:S(2)}) copy-start(bf16[1024,1024]{1,0:T(8,128)(2,1)} %wk_ref.1) | copy-start | bytes 6291460
  54.7 47.6 %copy-start.1 = (bf16[1024,1024]{1,0:T(8,128)(2,1)S(1)}, bf16[1024,1024]{1,0:T(8,128)(2,1)}, u32[]{:S(2)}) copy-start(bf16[1024,1024]{1,0:T(8,128)(2,1)} %wv_ref.1) | copy-start | bytes 6291460
  81.5 12.9 %collective-permute-start.14 = (bf16[1024,256]{1,0:T(8,128)(2,1)S(1)}, bf16[1024,256]{1,0:T(8,128)(2,1)S(1)}, u32[]{:S(2)}, u32[]{:S(2)}) collective-permute-start(bf16[1024,256]{1,0:T(8,128)(2,1)S(1)} %bitcast.4), channel_id=1, source_target_pairs={{0,2},{1,7},{2,4},{3,1},{4,6},{5,3},{6,0},{7,5},{8,10},{9,15},{10,... | collective-permute-start | bytes 1572872 | tf_op jit(solution)/shard_map/ppermute | solution.py:51
  84.0 11.6 %collective-permute-start.15 = (bf16[1024,256]{1,0:T(8,128)(2,1)S(1)}, bf16[1024,256]{1,0:T(8,128)(2,1)S(1)}, u32[]{:S(2)}, u32[]{:S(2)}) collective-permute-start(bf16[1024,256]{1,0:T(8,128)(2,1)S(1)} %bitcast.5), channel_id=1, source_target_pairs={{0,6},{1,3},{2,0},{3,5},{4,2},{5,7},{6,4},{7,1},{8,14},{9,11},{10,... | collective-permute-start | bytes 1572872 | tf_op jit(solution)/shard_map/ppermute | solution.py:51
  84.0 10.4 %collective-permute-start.16 = (bf16[128,512]{1,0:T(8,128)(2,1)S(1)}, bf16[128,512]{1,0:T(8,128)(2,1)S(1)}, u32[]{:S(2)}, u32[]{:S(2)}) collective-permute-start(bf16[128,512]{1,0:T(8,128)(2,1)S(1)} %get-tuple-element.100), channel_id=1, source_target_pairs={{0,64},{32,96},{64,128},{96,160},{128,192},{160,224},{192,0},{224,... | collective-permute-start | bytes 393224 | tf_op jit(solution)/shard_map/ppermute | solution.py:43
  86.2 8.2 %collective-permute-start.17 = (bf16[128,512]{1,0:T(8,128)(2,1)S(1)}, bf16[128,512]{1,0:T(8,128)(2,1)S(1)}, u32[]{:S(2)}, u32[]{:S(2)}) collective-permute-start(bf16[128,512]{1,0:T(8,128)(2,1)S(1)} %get-tuple-element.101), channel_id=1, source_target_pairs={{0,192},{32,224},{64,0},{96,32},{128,64},{160,96},{192,128},{224,1... | collective-permute-start | bytes 393224 | tf_op jit(solution)/shard_map/ppermute | solution.py:43
  87.6 16.0 %collective-permute-start.20 = (bf16[1024,256]{1,0:T(8,128)(2,1)S(1)}, bf16[1024,256]{1,0:T(8,128)(2,1)S(1)}, u32[]{:S(2)}, u32[]{:S(2)}) collective-permute-start(bf16[1024,256]{1,0:T(8,128)(2,1)S(1)} %bitcast.6), channel_id=1, source_target_pairs={{0,1},{1,0},{2,3},{3,2},{4,5},{5,4},{6,7},{7,6},{8,9},{9,8},{10,11... | collective-permute-start | bytes 1572872 | tf_op jit(solution)/shard_map/ppermute | solution.py:43
  95.6 8.0 %collective-permute-start.21 = (bf16[1024,256]{1,0:T(8,128)(2,1)S(1)}, bf16[1024,256]{1,0:T(8,128)(2,1)S(1)}, u32[]{:S(2)}, u32[]{:S(2)}) collective-permute-start(bf16[1024,256]{1,0:T(8,128)(2,1)S(1)} %collective-permute-done.14._.refs_2_), channel_id=1, source_target_pairs={{0,1},{1,0},{2,3},{3,2},{4,5},{5,4},{6,7},{7,6},{8,9},{9,8},{10,11... | collective-permute-start | bytes 1572872 | tf_op jit(solution)/shard_map/ppermute | solution.py:43
  99.6 4.0 %collective-permute-start.22 = (bf16[1024,256]{1,0:T(8,128)(2,1)S(1)}, bf16[1024,256]{1,0:T(8,128)(2,1)S(1)}, u32[]{:S(2)}, u32[]{:S(2)}) collective-permute-start(bf16[1024,256]{1,0:T(8,128)(2,1)S(1)} %collective-permute-done.15.refs_4_), channel_id=1, source_target_pairs={{0,1},{1,0},{2,3},{3,2},{4,5},{5,4},{6,7},{7,6},{8,9},{9,8},{10,11... | collective-permute-start | bytes 1572872 | tf_op jit(solution)/shard_map/ppermute | solution.py:43
  99.6 10.1 %collective-permute-start.18 = (bf16[1024,256]{1,0:T(8,128)(2,1)S(1)}, bf16[1024,256]{1,0:T(8,128)(2,1)S(1)}, u32[]{:S(2)}, u32[]{:S(2)}) collective-permute-start(bf16[1024,256]{1,0:T(8,128)(2,1)S(1)} %collective-permute-done.14._.refs_2_), channel_id=1, source_target_pairs={{0,2},{1,7},{2,4},{3,1},{4,6},{5,3},{6,0},{7,5},{8,10},{9,15},{10,... | collective-permute-start | bytes 1572872 | tf_op jit(solution)/shard_map/ppermute | solution.py:51
  100.4 9.3 %collective-permute-start.19 = (bf16[128,512]{1,0:T(8,128)(2,1)S(1)}, bf16[128,512]{1,0:T(8,128)(2,1)S(1)}, u32[]{:S(2)}, u32[]{:S(2)}) collective-permute-start(bf16[128,512]{1,0:T(8,128)(2,1)S(1)} %get-tuple-element.103), channel_id=1, source_target_pairs={{0,128},{32,160},{64,192},{96,224},{128,0},{160,32},{192,64},{224,... | collective-permute-start | bytes 393224 | tf_op jit(solution)/shard_map/ppermute | solution.py:43
  109.7 2.3 %collective-permute-start.23 = (bf16[1024,256]{1,0:T(8,128)(2,1)S(1)}, bf16[1024,256]{1,0:T(8,128)(2,1)S(1)}, u32[]{:S(2)}, u32[]{:S(2)}) collective-permute-start(bf16[1024,256]{1,0:T(8,128)(2,1)S(1)} %collective-permute-done.18.refs_0_), channel_id=1, source_target_pairs={{0,1},{1,0},{2,3},{3,2},{4,5},{5,4},{6,7},{7,6},{8,9},{9,8},{10,11... | collective-permute-start | bytes 1572872 | tf_op jit(solution)/shard_map/ppermute | solution.py:43

commit v5 on v4

--- a/solution.py
+++ b/solution.py
@@ -163,8 +163,9 @@
     operands = list(messages) + list(blocks) + in_acc + in_dq + in_odd
     n_in = len(operands)
     n_dq = 1 if odd else n
-    in_place = acc_type == jnp.float32 and len(in_acc) == nb
-    aliases = {n + nb + b: n_dq + b for b in range(nb)} if in_place else {}
+    in_place = acc_type == jnp.float32
+    given = [b for b in range(nb) if accs[b] is not None]
+    aliases = {n + nb + i: n_dq + b for i, b in enumerate(given)} if in_place else {}
 
     def body(*refs):
         ins = list(refs[:n_in])
@@ -179,9 +180,10 @@
             load_message(msg_refs[c], c, q_at, g_at, stat_at)
             if dq_ins[c] is not None:
                 dq_at[c * HD : (c + 1) * HD, :] = dq_ins[c][...]
-        if not in_place and n > 1:
+        if n > 1:
             for b in range(nb):
-                out_refs[b][...] = jnp.zeros_like(out_refs[b])
+                if acc_refs[b] is None:
+                    out_refs[b][...] = jnp.zeros_like(out_refs[b])
 
         def step(c, carry):
             dq = 0.0
@@ -422,14 +424,18 @@
 
     near = [msg, up1, down1]
     dq, (own,) = attend("home_first", near, [kv0], none[:1], none[:3], [f32] * 3, f32, False)
-    up2, down2, own = lax.optimization_barrier((up2, down2, own))
+    dq, acc = attend("away_near", near, away[:2], none[:2], dq, [f32] * 3, f32, False)
+    up2, down2, acc[0] = lax.optimization_barrier((up2, down2, acc[0]))
     up3, down3 = shift(up2, "z", 1), shift(down2, "z", -1)
-    dq, acc = attend("away_near", near, away, none[:3], dq, [f32, bf16, bf16], f32, False)
-    dq_0, dq_u1, dq_d1 = dq
-    up3, down3, dq_0 = lax.optimization_barrier((up3, down3, dq_0))
+    two = [up2, down2]
+    (dq_u2, dq_d2), acc = attend(
+        "away_two", two, away, acc + [None], none[:2], [f32] * 2, f32, False
+    )
+    up3, down3, acc[0] = lax.optimization_barrier((up3, down3, acc[0]))
     far = shift(up3, "z", 1)
-    two = [up2, down2]
-    (dq_u2, dq_d2), acc = attend("away_two", two, away, acc, none[:2], [f32] * 2, f32, False)
+    (dq_0, dq_u1, dq_d1), acc[2:] = attend(
+        "away_across", near, away[2:], acc[2:], dq, [f32, bf16, bf16], f32, False
+    )
     three = [up3, down3]
     (odd,), acc = attend(
         "all_three", three, away + [kv0], acc + [own], none[:2], bf16, f32, False, (dq_u1, dq_d1)

time: 115 us -> 115 us (level)
    ppermute x20, starting transfers between devices: 36.4 us -> 38.2 us  [shift(): lax.ppermute(a, Z if axis == 'z' else axis, [(i, (i + k) % n) for i in ra...]
    ppermute x1, starting transfers between devices: 1.57 us -> 0.4 us  [on_device(): got = lax.ppermute(odd, 'zp', [(0, 1), (1, 0)])]
    pallas_call x6 -> x7, Pallas kernels: 22.6 us -> 22.8 us  [attend(): pl.pallas_call(body, out_shape=out_shape, scratch_shapes=message_scratch(...]
  transfers between devices with their start and end apart: 24 -> 24, of which waited for: 10 -> 8; matrix products, arithmetic and copies ran while one was open for 0% -> 0% of each run, Pallas kernels for 25% -> 25%
where the time goes in v5:
time: 115 us; the launch traced here: 114 us
  starting transfers between devices  41.5 us (36%)
  Pallas kernels  33.5 us (29%)
  blocking collectives  20.5 us (18%)
  waiting for transfers between devices  15.8 us (14%)
  local copies, waits for them, and re-layouts  1.93 us (2%)
    ppermute x20, starting transfers between devices, shift(): lax.ppermute(a, Z if axis == 'z' else axis, [(i, (i + k) % n) for i in ra...  38.2 us
    pallas_call x7, Pallas kernels, attend(): pl.pallas_call(body, out_shape=out_shape, scratch_shapes=message_scratch(...  22.8 us
    all_to_all x1, blocking collectives, on_device(): lax.all_to_all(outgoing, Z + ('y',), split_axis=0, concat_axis=0, tiled=T...  20.5 us
    ppermute x20, waiting for transfers between devices, shift(): lax.ppermute(a, Z if axis == 'z' else axis, [(i, (i + k) % n) for i in ra...  13.4 us
    pallas_call x2, Pallas kernels, project(): pl.pallas_call(body_final if final else body_first, out_shape=jax.ShapeDt...  5.57 us
    ppermute x3, starting transfers between devices, shift_by_core(): return lax.ppermute(a, ('x', 'core'), pairs)  2.95 us
  transfers between devices with their start and end apart: 24, of which 8 were waited for; matrix products, arithmetic and copies ran while one was open for 0% of the time, Pallas kernels for 25%

profile of v5, /device:TPU:1, one launch (start us, length us, event | category | flops | bytes accessed | tf_op | source)
XLA Modules:
  0.0 114.2 jit_solution(8301944309556524997)
XLA Ops:
  0.6 2.0 %pack.1 = (bf16[144,1024]{1,0:T(8,128)(2,1)}, bf16[512,256]{1,0:T(8,128)(2,1)}) custom-call(s32[32]{0:T(128)} %len_ref.1, bf16[64,1024]{1,0:T(8,128)(2,1)} %q_ref.1, bf16[64,1024]{1,0:T(8,128)(2,1)} %g_ref.1, bf16[8,64]{1,0:T(8,128)(2,1)} %total_ref.1, bf16[8,64]{1,0:T(8,128)(2,1)} %dot_ref.1, bf16[512,128]{1,0:T(8,128)(2,1)} %k_ref.1, bf16[512,128]{1,0:T(8,128)(2,1)} %v_ref.1), custom_call_target="tpu_custom_call" | custom-call | bytes 1048576 | tf_op jit(solution)/shard_map/pack/pallas_call | solution.py:97
  2.6 2.5 %collective-permute-start = (bf16[144,1024]{1,0:T(8,128)(2,1)}, bf16[144,1024]{1,0:T(8,128)(2,1)S(1)}, u32[]{:S(2)}, u32[]{:S(2)}) collective-permute-start(bf16[144,1024]{1,0:T(8,128)(2,1)} %get-tuple-element.61.refs_0_), channel_id=1, source_target_pairs={{0,32},{32,64},{64,96},{96,128},{128,160},{160,192},{192,224},{224... | collective-permute-start | bytes 884744 | tf_op jit(solution)/shard_map/ppermute | solution.py:43
  5.2 4.0 %collective-permute-start.2 = (bf16[144,1024]{1,0:T(8,128)(2,1)}, bf16[144,1024]{1,0:T(8,128)(2,1)S(1)}, u32[]{:S(2)}, u32[]{:S(2)}) collective-permute-start(bf16[144,1024]{1,0:T(8,128)(2,1)} %get-tuple-element.61.refs_0_), channel_id=1, source_target_pairs={{0,224},{32,0},{64,32},{96,64},{128,96},{160,128},{192,160},{224,1... | collective-permute-start | bytes 884744 | tf_op jit(solution)/shard_map/ppermute | solution.py:43
  9.2 1.3 %collective-permute-start.4 = (bf16[512,256]{1,0:T(8,128)(2,1)}, bf16[512,256]{1,0:T(8,128)(2,1)S(1)}, u32[]{:S(2)}, u32[]{:S(2)}) collective-permute-start(bf16[512,256]{1,0:T(8,128)(2,1)} %get-tuple-element.62.refs_3_.refs_5_), channel_id=1, source_target_pairs={{0,8},{8,16},{16,24},{24,0},{1,9},{9,17},{17,25},{25,1},{2,10},{10... | collective-permute-start | bytes 786440 | tf_op jit(solution)/shard_map/ppermute | solution.py:43
  10.5 1.4 %collective-permute-start.5 = (bf16[512,256]{1,0:T(8,128)(2,1)}, bf16[512,256]{1,0:T(8,128)(2,1)S(1)}, u32[]{:S(2)}, u32[]{:S(2)}) collective-permute-start(bf16[512,256]{1,0:T(8,128)(2,1)} %get-tuple-element.62.refs_3_.refs_5_), channel_id=1, source_target_pairs={{0,24},{8,0},{16,8},{24,16},{1,25},{9,1},{17,9},{25,17},{2,26},{10... | collective-permute-start | bytes 786440 | tf_op jit(solution)/shard_map/ppermute | solution.py:43
  11.9 1.6 %collective-permute-start.8 = (bf16[512,256]{1,0:T(8,128)(2,1)}, bf16[512,256]{1,0:T(8,128)(2,1)S(1)}, u32[]{:S(2)}, u32[]{:S(2)}) collective-permute-start(bf16[512,256]{1,0:T(8,128)(2,1)} %get-tuple-element.62.refs_3_.refs_5_), channel_id=1, source_target_pairs={{0,16},{8,24},{16,0},{24,8},{1,17},{9,25},{17,1},{25,9},{2,18},{10... | collective-permute-start | bytes 786440 | tf_op jit(solution)/shard_map/ppermute | solution.py:43
  13.6 2.5 %collective-permute-done.refs_1_ = bf16[144,1024]{1,0:T(8,128)(2,1)S(1)} collective-permute-done((bf16[144,1024]{1,0:T(8,128)(2,1)}, bf16[144,1024]{1,0:T(8,128)(2,1)S(1)}, u32[]{:S(2)}, u32[]{:S(2)}) %collective-permute-start) | collective-permute-done | bytes 294944 | tf_op jit(solution)/shard_map/ppermute | solution.py:43
  16.0 0.0 collective-permute-start.1
  16.1 0.0 collective-permute-done.2.refs_2_
  16.1 2.7 %collective-permute-start.3 = (bf16[144,1024]{1,0:T(8,128)(2,1)S(1)}, bf16[144,1024]{1,0:T(8,128)(2,1)S(1)}, u32[]{:S(2)}, u32[]{:S(2)}) collective-permute-start(bf16[144,1024]{1,0:T(8,128)(2,1)S(1)} %collective-permute-done.2.refs_2_), channel_id=1, source_target_pairs={{0,224},{32,0},{64,32},{96,64},{128,96},{160,128},{192,160},{224,1... | collective-permute-start | bytes 884744 | tf_op jit(solution)/shard_map/ppermute | solution.py:43
  18.7 1.0 copy-done.3
  19.7 0.9 copy-done.5
  20.6 2.0 %home_first.1 = (f32[128,512]{1,0:T(8,128)S(1)}, f32[128,512]{1,0:T(8,128)S(1)}, f32[128,512]{1,0:T(8,128)S(1)}, f32[512,256]{1,0:T(8,128)S(1)}) custom-call(bf16[144,1024]{1,0:T(8,128)(2,1)S(1)} %copy-done.3, bf16[144,1024]{1,0:T(8,128)(2,1)S(1)} %collective-permute-done.refs_1_, bf16[144,1024]{1,0:T(8,128)(2,1)S(1)} %collective-permute-done.2.refs_2_, ...), custom_call_target="tpu_custom_call" | custom-call | flops 2013265920 | bytes 2097152 | tf_op jit(solution)/shard_map/home_first/pallas_call | solution.py:229
  22.7 0.0 collective-permute-done.4.refs_3_.refs_2_.refs_1_
  22.7 0.0 collective-permute-done.5.refs_4_.refs_3_.refs_2_
  22.7 4.6 %away_near.1 = (f32[128,512]{1,0:T(8,128)S(1)}, f32[128,512]{1,0:T(8,128)S(1)}, f32[128,512]{1,0:T(8,128)S(1)}, f32[512,256]{1,0:T(8,128)S(1)}, f32[512,256]{1,0:T(8,128)S(1)}) custom-call(bf16[144,1024]{1,0:T(8,128)(2,1)S(1)} %copy-done.3, bf16[144,1024]{1,0:T(8,128)(2,1)S(1)} %collective-permute-done.refs_1_, ...), custom_call_target="tpu_custom_call" | custom-call | flops 4026531840 | bytes 2097152 | tf_op jit(solution)/shard_map/away_near/pallas_call | solution.py:229
  27.3 0.0 collective-permute-done.1.refs_0_
  27.3 0.0 collective-permute-done.3.refs_1_
  27.3 0.1 collective-permute-start.6
  27.4 2.7 %collective-permute-start.7 = (bf16[144,1024]{1,0:T(8,128)(2,1)S(1)}, bf16[144,1024]{1,0:T(8,128)(2,1)S(1)}, u32[]{:S(2)}, u32[]{:S(2)}) collective-permute-start(bf16[144,1024]{1,0:T(8,128)(2,1)S(1)} %collective-permute-done.3.refs_1_), channel_id=1, source_target_pairs={{0,224},{32,0},{64,32},{96,64},{128,96},{160,128},{192,160},{224,1... | collective-permute-start | bytes 884744 | tf_op jit(solution)/shard_map/ppermute | solution.py:43
  30.1 0.0 collective-permute-done.8.refs_4_.refs_3_
  30.1 4.3 %away_two.1 = (f32[128,512]{1,0:T(8,128)S(1)}, f32[128,512]{1,0:T(8,128)S(1)}, f32[512,256]{1,0:T(8,128)S(1)}, f32[512,256]{1,0:T(8,128)S(1)}, f32[512,256]{1,0:T(8,128)S(1)}) custom-call(bf16[144,1024]{1,0:T(8,128)(2,1)S(1)} %collective-permute-done.1.refs_0_, ...), custom_call_target="tpu_custom_call", output_to_operand_aliasing={{2}: (5, {}), {3}: (6, {})} | custom-call | flops 4026531840 | bytes 2097152 | tf_op jit(solution)/shard_map/away_two/pallas_call | solution.py:229
  34.4 2.0 %away_across.1 = (f32[128,512]{1,0:T(8,128)S(1)}, bf16[128,512]{1,0:T(8,128)(2,1)S(1)}, bf16[128,512]{1,0:T(8,128)(2,1)S(1)}, f32[512,256]{1,0:T(8,128)S(1)}) custom-call(bf16[144,1024]{1,0:T(8,128)(2,1)S(1)} %copy-done.4, bf16[144,1024]{1,0:T(8,128)(2,1)S(1)} %collective-permute-done.refs_1_, ...), custom_call_target="tpu_custom_call", output_to_operand_aliasing={{3}: (4, {})} | custom-call | flops 2013265920 | bytes 2097152 | tf_op jit(solution)/shard_map/away_across/pallas_call | solution.py:229
  36.4 0.0 collective-permute-done.6.refs_0_
  36.4 0.0 collective-permute-done.7.refs_1_
  36.4 0.1 collective-permute-start.9
  36.5 5.5 %all_three.1 = (bf16[512,512]{1,0:T(8,128)(2,1)S(1)}, f32[512,256]{1,0:T(8,128)S(1)}, f32[512,256]{1,0:T(8,128)S(1)}, f32[512,256]{1,0:T(8,128)S(1)}, f32[512,256]{1,0:T(8,128)S(1)}) custom-call(bf16[144,1024]{1,0:T(8,128)(2,1)S(1)} %collective-permute-done.6.refs_0_, ...), custom_call_target="tpu_custom_call", output_to_operand_aliasing={{1}: (6, {}), {2}: (7, {}), {3}: (8, {}), {4}: (9, {})} | custom-call | flops 5368709120 | bytes 2097152 | tf_op jit(solution)/shard_map/all_three/pallas_call | solution.py:229
  42.1 0.4 collective-permute-start.10
  42.5 1.4 %collective-permute-done.9.refs_0_.refs_2_ = bf16[144,1024]{1,0:T(8,128)(2,1)S(1)} collective-permute-done((bf16[144,1024]{1,0:T(8,128)(2,1)S(1)}, bf16[144,1024]{1,0:T(8,128)(2,1)S(1)}, u32[]{:S(2)}, u32[]{:S(2)}) %collective-permute-start.9) | collective-permute-done | bytes 294944 | tf_op jit(solution)/shard_map/ppermute | solution.py:43
  43.9 2.3 %away_far.1 = (f32[128,512]{1,0:T(8,128)S(1)}, bf16[512,256]{1,0:T(8,128)(2,1)S(1)}, bf16[512,256]{1,0:T(8,128)(2,1)S(1)}, bf16[512,256]{1,0:T(8,128)(2,1)S(1)}) custom-call(bf16[144,1024]{1,0:T(8,128)(2,1)S(1)} %collective-permute-done.9.refs_0_.refs_2_, bf16[512,256]{1,0:T(8,128)(2,1)S(1)} %collective-permute-done.4.refs_3_.refs_2_.refs_1_, ...), custom_call_target="tpu_custom_call" | custom-call | flops 2013265920 | bytes 2097152 | tf_op jit(solution)/shard_map/away_far/pallas_call | solution.py:229
  46.2 3.0 %collective-permute-start.11 = (bf16[512,256]{1,0:T(8,128)(2,1)S(1)}, bf16[512,256]{1,0:T(8,128)(2,1)S(1)}, u32[]{:S(2)}, u32[]{:S(2)}) collective-permute-start(bf16[512,256]{1,0:T(8,128)(2,1)S(1)} %get-tuple-element.99), channel_id=1, source_target_pairs={{0,16},{8,24},{16,0},{24,8},{1,17},{9,25},{17,1},{25,9},{2,18},{10... | collective-permute-start | bytes 786440 | tf_op jit(solution)/shard_map/ppermute | solution.py:43
  49.2 0.8 collective-permute-start.12
  50.0 0.7 collective-permute-start.13
  50.7 2.0 %home_last.1 = (f32[128,512]{1,0:T(8,128)S(1)}, f32[128,512]{1,0:T(8,128)S(1)}, f32[128,512]{1,0:T(8,128)S(1)}, f32[512,256]{1,0:T(8,128)S(1)}) custom-call(bf16[144,1024]{1,0:T(8,128)(2,1)S(1)} %collective-permute-done.1.refs_0_, bf16[144,1024]{1,0:T(8,128)(2,1)S(1)} %collective-permute-done.3.refs_1_, ...), custom_call_target="tpu_custom_call", output_to_operand_aliasing={{3}: (4, {})} | custom-call | flops 2013265920 | bytes 2097152 | tf_op jit(solution)/shard_map/home_last/pallas_call | solution.py:229
  52.7 0.5 collective-permute-done.10.got_ref
  53.2 0.1 pair.1
  53.3 0.0 collective-permute-done.11.a_ref
  53.3 4.9 %collective-permute-done.12.b_ref = bf16[512,256]{1,0:T(8,128)(2,1)S(1)} collective-permute-done((bf16[512,256]{1,0:T(8,128)(2,1)S(1)}, bf16[512,256]{1,0:T(8,128)(2,1)S(1)}, u32[]{:S(2)}, u32[]{:S(2)}) %collective-permute-start.12) | collective-permute-done | bytes 262176 | tf_op jit(solution)/shard_map/ppermute | solution.py:43
  58.2 1.7 %collective-permute-done.13.c_ref = bf16[512,256]{1,0:T(8,128)(2,1)S(1)} collective-permute-done((bf16[512,256]{1,0:T(8,128)(2,1)S(1)}, bf16[512,256]{1,0:T(8,128)(2,1)S(1)}, u32[]{:S(2)}, u32[]{:S(2)}) %collective-permute-start.13) | collective-permute-done | bytes 262176 | tf_op jit(solution)/shard_map/ppermute | solution.py:43
  59.9 1.0 dispatch.1
  61.0 20.5 %all_to_all.12 = bf16[32,32,256]{2,1,0:T(8,128)(2,1)S(1)} all-to-all(bf16[32,32,256]{2,1,0:T(8,128)(2,1)S(1)} %bitcast.3), channel_id=1, replica_groups=mesh['zq'=4,'zp'=2,'y'=4,'x'=4,'core'=2] {'zq','zp','y'}, dimensions={0} | all-to-all | bytes 1048576 | tf_op jit(solution)/shard_map/all_to_all | solution.py:458
  81.4 2.5 %collective-permute-start.14 = (bf16[1024,256]{1,0:T(8,128)(2,1)S(1)}, bf16[1024,256]{1,0:T(8,128)(2,1)S(1)}, u32[]{:S(2)}, u32[]{:S(2)}) collective-permute-start(bf16[1024,256]{1,0:T(8,128)(2,1)S(1)} %bitcast.4), channel_id=1, source_target_pairs={{0,2},{1,7},{2,4},{3,1},{4,6},{5,3},{6,0},{7,5},{8,10},{9,15},{10,... | collective-permute-start | bytes 1572872 | tf_op jit(solution)/shard_map/ppermute | solution.py:51
  83.9 0.0 collective-permute-start.15
  83.9 2.0 %collective-permute-start.16 = (bf16[128,512]{1,0:T(8,128)(2,1)S(1)}, bf16[128,512]{1,0:T(8,128)(2,1)S(1)}, u32[]{:S(2)}, u32[]{:S(2)}) collective-permute-start(bf16[128,512]{1,0:T(8,128)(2,1)S(1)} %get-tuple-element.106), channel_id=1, source_target_pairs={{0,64},{32,96},{64,128},{96,160},{128,192},{160,224},{192,0},{224,... | collective-permute-start | bytes 393224 | tf_op jit(solution)/shard_map/ppermute | solution.py:43
  85.9 1.6 %collective-permute-start.17 = (bf16[128,512]{1,0:T(8,128)(2,1)S(1)}, bf16[128,512]{1,0:T(8,128)(2,1)S(1)}, u32[]{:S(2)}, u32[]{:S(2)}) collective-permute-start(bf16[128,512]{1,0:T(8,128)(2,1)S(1)} %get-tuple-element.107), channel_id=1, source_target_pairs={{0,192},{32,224},{64,0},{96,32},{128,64},{160,96},{192,128},{224,1... | collective-permute-start | bytes 393224 | tf_op jit(solution)/shard_map/ppermute | solution.py:43
  87.5 6.5 %collective-permute-start.20 = (bf16[1024,256]{1,0:T(8,128)(2,1)S(1)}, bf16[1024,256]{1,0:T(8,128)(2,1)S(1)}, u32[]{:S(2)}, u32[]{:S(2)}) collective-permute-start(bf16[1024,256]{1,0:T(8,128)(2,1)S(1)} %bitcast.6), channel_id=1, source_target_pairs={{0,1},{1,0},{2,3},{3,2},{4,5},{5,4},{6,7},{7,6},{8,9},{9,8},{10,11... | collective-permute-start | bytes 1572872 | tf_op jit(solution)/shard_map/ppermute | solution.py:43
  94.0 0.0 collective-permute-done.16.a_ref
  94.0 0.0 collective-permute-done.17.b_ref
  94.0 0.0 collective-permute-done.14._.refs_2_
  94.0 1.9 %collective-permute-done.15.refs_4_ = bf16[1024,256]{1,0:T(8,128)(2,1)S(1)} collective-permute-done((bf16[1024,256]{1,0:T(8,128)(2,1)S(1)}, bf16[1024,256]{1,0:T(8,128)(2,1)S(1)}, u32[]{:S(2)}, u32[]{:S(2)}) %collective-permute-start.15) | collective-permute-done | bytes 524320 | tf_op jit(solution)/shard_map/ppermute | solution.py:51
  95.9 3.6 %collective-permute-start.21 = (bf16[1024,256]{1,0:T(8,128)(2,1)S(1)}, bf16[1024,256]{1,0:T(8,128)(2,1)S(1)}, u32[]{:S(2)}, u32[]{:S(2)}) collective-permute-start(bf16[1024,256]{1,0:T(8,128)(2,1)S(1)} %collective-permute-done.14._.refs_2_), channel_id=1, source_target_pairs={{0,1},{1,0},{2,3},{3,2},{4,5},{5,4},{6,7},{7,6},{8,9},{9,8},{10,11... | collective-permute-start | bytes 1572872 | tf_op jit(solution)/shard_map/ppermute | solution.py:43
  99.5 0.0 collective-permute-start.22
  99.5 0.5 collective-permute-start.18
  99.9 2.2 %collective-permute-start.19 = (bf16[128,512]{1,0:T(8,128)(2,1)S(1)}, bf16[128,512]{1,0:T(8,128)(2,1)S(1)}, u32[]{:S(2)}, u32[]{:S(2)}) collective-permute-start(bf16[128,512]{1,0:T(8,128)(2,1)S(1)} %get-tuple-element.109), channel_id=1, source_target_pairs={{0,128},{32,160},{64,192},{96,224},{128,0},{160,32},{192,64},{224,... | collective-permute-start | bytes 393224 | tf_op jit(solution)/shard_map/ppermute | solution.py:43
  102.1 1.2 %merge.1.refs_6_.refs_2_ = bf16[1024,2048]{1,0:T(8,128)(2,1)S(1)} custom-call(bf16[1024,256]{1,0:T(8,128)(2,1)S(1)} %collective-permute-done.14._.refs_2_, bf16[1024,1024]{1,0:T(8,128)(2,1)S(1)} %copy-done, bf16[1024,1024]{1,0:T(8,128)(2,1)S(1)} %copy-done.1), custom_call_target="tpu_custom_call" | custom-call | bytes 8388608 | tf_op jit(solution)/shard_map/merge/pallas_call | solution.py:326
  103.3 0.0 collective-permute-done.20.refs_1_
  103.3 0.0 collective-permute-done.22.refs_5_
  103.3 3.5 %project_near.1.refs_3_ = f32[1024,1024]{1,0:T(8,128)S(1)} custom-call(bf16[1024,256]{1,0:T(8,128)(2,1)S(1)} %bitcast.7, bf16[1024,256]{1,0:T(8,128)(2,1)S(1)} %collective-permute-done.20.refs_1_, bf16[1024,256]{1,0:T(8,128)(2,1)S(1)} %collective-permute-done.14._.refs_2_, bf16[1024,256]{1,0:T(8,128)(2,1)S(1)} %collective-permute-done.21.refs_3_, ...), custom_call_target="tpu_custom_call" | custom-call | flops 3221225472 | bytes 6291456 | tf_op jit(solution)/shard_map/project_near/pallas_call | solution.py:369
  106.8 2.1 %collective-permute-done.19.c_ref = bf16[128,512]{1,0:T(8,128)(2,1)S(1)} collective-permute-done((bf16[128,512]{1,0:T(8,128)(2,1)S(1)}, bf16[128,512]{1,0:T(8,128)(2,1)S(1)}, u32[]{:S(2)}, u32[]{:S(2)}) %collective-permute-start.19) | collective-permute-done | bytes 131104 | tf_op jit(solution)/shard_map/ppermute | solution.py:43
  108.9 0.0 collective-permute-done.18.refs_0_
  108.9 1.4 %collective-permute-start.23 = (bf16[1024,256]{1,0:T(8,128)(2,1)S(1)}, bf16[1024,256]{1,0:T(8,128)(2,1)S(1)}, u32[]{:S(2)}, u32[]{:S(2)}) collective-permute-start(bf16[1024,256]{1,0:T(8,128)(2,1)S(1)} %collective-permute-done.18.refs_0_), channel_id=1, source_target_pairs={{0,1},{1,0},{2,3},{3,2},{4,5},{5,4},{6,7},{7,6},{8,9},{9,8},{10,11... | collective-permute-start | bytes 1572872 | tf_op jit(solution)/shard_map/ppermute | solution.py:43
  110.4 0.8 finish.1
  111.2 0.7 collective-permute-done.23.refs_1_
  111.9 2.1 %project_across.1 = bf16[1024,1024]{1,0:T(8,128)(2,1)} custom-call(bf16[1024,256]{1,0:T(8,128)(2,1)S(1)} %collective-permute-done.18.refs_0_, bf16[1024,256]{1,0:T(8,128)(2,1)S(1)} %collective-permute-done.23.refs_1_, bf16[1024,2048]{1,0:T(8,128)(2,1)S(1)} %merge.1.refs_6_.refs_2_, f32[1024,1024]{1,0:T(8,128)S(1)} %project_near.1.refs_3_), custom_call_target="tpu_custom_call" | custom-call | flops 1073741824 | bytes 6291456 | tf_op jit(solution)/shard_map/project_across/pallas_call | solution.py:369
  (13 shorter events, 0.0 us)
Async XLA Ops:
  2.6 13.4 %collective-permute-start = (bf16[144,1024]{1,0:T(8,128)(2,1)}, bf16[144,1024]{1,0:T(8,128)(2,1)S(1)}, u32[]{:S(2)}, u32[]{:S(2)}) collective-permute-start(bf16[144,1024]{1,0:T(8,128)(2,1)} %get-tuple-element.61.refs_0_), channel_id=1, source_target_pairs={{0,32},{32,64},{64,96},{96,128},{128,160},{160,192},{192,224},{224... | collective-permute-start | bytes 884744 | tf_op jit(solution)/shard_map/ppermute | solution.py:43
  5.2 10.9 %collective-permute-start.2 = (bf16[144,1024]{1,0:T(8,128)(2,1)}, bf16[144,1024]{1,0:T(8,128)(2,1)S(1)}, u32[]{:S(2)}, u32[]{:S(2)}) collective-permute-start(bf16[144,1024]{1,0:T(8,128)(2,1)} %get-tuple-element.61.refs_0_), channel_id=1, source_target_pairs={{0,224},{32,0},{64,32},{96,64},{128,96},{160,128},{192,160},{224,1... | collective-permute-start | bytes 884744 | tf_op jit(solution)/shard_map/ppermute | solution.py:43
  9.2 13.5 %collective-permute-start.4 = (bf16[512,256]{1,0:T(8,128)(2,1)}, bf16[512,256]{1,0:T(8,128)(2,1)S(1)}, u32[]{:S(2)}, u32[]{:S(2)}) collective-permute-start(bf16[512,256]{1,0:T(8,128)(2,1)} %get-tuple-element.62.refs_3_.refs_5_), channel_id=1, source_target_pairs={{0,8},{8,16},{16,24},{24,0},{1,9},{9,17},{17,25},{25,1},{2,10},{10... | collective-permute-start | bytes 786440 | tf_op jit(solution)/shard_map/ppermute | solution.py:43
  10.5 12.2 %collective-permute-start.5 = (bf16[512,256]{1,0:T(8,128)(2,1)}, bf16[512,256]{1,0:T(8,128)(2,1)S(1)}, u32[]{:S(2)}, u32[]{:S(2)}) collective-permute-start(bf16[512,256]{1,0:T(8,128)(2,1)} %get-tuple-element.62.refs_3_.refs_5_), channel_id=1, source_target_pairs={{0,24},{8,0},{16,8},{24,16},{1,25},{9,1},{17,9},{25,17},{2,26},{10... | collective-permute-start | bytes 786440 | tf_op jit(solution)/shard_map/ppermute | solution.py:43
  11.9 18.1 %collective-permute-start.8 = (bf16[512,256]{1,0:T(8,128)(2,1)}, bf16[512,256]{1,0:T(8,128)(2,1)S(1)}, u32[]{:S(2)}, u32[]{:S(2)}) collective-permute-start(bf16[512,256]{1,0:T(8,128)(2,1)} %get-tuple-element.62.refs_3_.refs_5_), channel_id=1, source_target_pairs={{0,16},{8,24},{16,0},{24,8},{1,17},{9,25},{17,1},{25,9},{2,18},{10... | collective-permute-start | bytes 786440 | tf_op jit(solution)/shard_map/ppermute | solution.py:43
  16.0 11.2 %collective-permute-start.1 = (bf16[144,1024]{1,0:T(8,128)(2,1)S(1)}, bf16[144,1024]{1,0:T(8,128)(2,1)S(1)}, u32[]{:S(2)}, u32[]{:S(2)}) collective-permute-start(bf16[144,1024]{1,0:T(8,128)(2,1)S(1)} %collective-permute-done.refs_1_), channel_id=1, source_target_pairs={{0,32},{32,64},{64,96},{96,128},{128,160},{160,192},{192,224},{224... | collective-permute-start | bytes 884744 | tf_op jit(solution)/shard_map/ppermute | solution.py:43
  16.1 11.2 %collective-permute-start.3 = (bf16[144,1024]{1,0:T(8,128)(2,1)S(1)}, bf16[144,1024]{1,0:T(8,128)(2,1)S(1)}, u32[]{:S(2)}, u32[]{:S(2)}) collective-permute-start(bf16[144,1024]{1,0:T(8,128)(2,1)S(1)} %collective-permute-done.2.refs_2_), channel_id=1, source_target_pairs={{0,224},{32,0},{64,32},{96,64},{128,96},{160,128},{192,160},{224,1... | collective-permute-start | bytes 884744 | tf_op jit(solution)/shard_map/ppermute | solution.py:43
  18.7 1.0 copy-start.3
  19.7 0.9 copy-start.5
  27.3 9.1 %collective-permute-start.6 = (bf16[144,1024]{1,0:T(8,128)(2,1)S(1)}, bf16[144,1024]{1,0:T(8,128)(2,1)S(1)}, u32[]{:S(2)}, u32[]{:S(2)}) collective-permute-start(bf16[144,1024]{1,0:T(8,128)(2,1)S(1)} %collective-permute-done.1.refs_0_), channel_id=1, source_target_pairs={{0,32},{32,64},{64,96},{96,128},{128,160},{160,192},{192,224},{224... | collective-permute-start | bytes 884744 | tf_op jit(solution)/shard_map/ppermute | solution.py:43
  27.4 9.0 %collective-permute-start.7 = (bf16[144,1024]{1,0:T(8,128)(2,1)S(1)}, bf16[144,1024]{1,0:T(8,128)(2,1)S(1)}, u32[]{:S(2)}, u32[]{:S(2)}) collective-permute-start(bf16[144,1024]{1,0:T(8,128)(2,1)S(1)} %collective-permute-done.3.refs_1_), channel_id=1, source_target_pairs={{0,224},{32,0},{64,32},{96,64},{128,96},{160,128},{192,160},{224,1... | collective-permute-start | bytes 884744 | tf_op jit(solution)/shard_map/ppermute | solution.py:43
  30.1 4.3 %copy-start.4 = (bf16[144,1024]{1,0:T(8,128)(2,1)S(1)}, bf16[144,1024]{1,0:T(8,128)(2,1)}, u32[]{:S(2)}) copy-start(bf16[144,1024]{1,0:T(8,128)(2,1)} %get-tuple-element.61.refs_0_) | copy-start | bytes 884740
  34.4 2.2 %copy-start.6 = (bf16[512,256]{1,0:T(8,128)(2,1)S(1)}, bf16[512,256]{1,0:T(8,128)(2,1)}, u32[]{:S(2)}) copy-start(bf16[512,256]{1,0:T(8,128)(2,1)} %get-tuple-element.62.refs_3_.refs_5_) | copy-start | bytes 786436
  36.4 7.4 %collective-permute-start.9 = (bf16[144,1024]{1,0:T(8,128)(2,1)S(1)}, bf16[144,1024]{1,0:T(8,128)(2,1)S(1)}, u32[]{:S(2)}, u32[]{:S(2)}) collective-permute-start(bf16[144,1024]{1,0:T(8,128)(2,1)S(1)} %collective-permute-done.6.refs_0_), channel_id=1, source_target_pairs={{0,32},{32,64},{64,96},{96,128},{128,160},{160,192},{192,224},{224... | collective-permute-start | bytes 884744 | tf_op jit(solution)/shard_map/ppermute | solution.py:43
  42.1 11.2 %collective-permute-start.10 = (bf16[512,512]{1,0:T(8,128)(2,1)S(1)}, bf16[512,512]{1,0:T(8,128)(2,1)S(1)}, u32[]{:S(2)}, u32[]{:S(2)}) collective-permute-start(bf16[512,512]{1,0:T(8,128)(2,1)S(1)} %get-tuple-element.92), channel_id=1, source_target_pairs={{0,32},{32,0},{1,33},{33,1},{2,34},{34,2},{3,35},{35,3},{4,36},{36... | collective-permute-start | bytes 1572872 | tf_op jit(solution)/shard_map/ppermute | solution.py:448
  46.2 7.1 %collective-permute-start.11 = (bf16[512,256]{1,0:T(8,128)(2,1)S(1)}, bf16[512,256]{1,0:T(8,128)(2,1)S(1)}, u32[]{:S(2)}, u32[]{:S(2)}) collective-permute-start(bf16[512,256]{1,0:T(8,128)(2,1)S(1)} %get-tuple-element.99), channel_id=1, source_target_pairs={{0,16},{8,24},{16,0},{24,8},{1,17},{9,25},{17,1},{25,9},{2,18},{10... | collective-permute-start | bytes 786440 | tf_op jit(solution)/shard_map/ppermute | solution.py:43
  49.2 9.0 %collective-permute-start.12 = (bf16[512,256]{1,0:T(8,128)(2,1)S(1)}, bf16[512,256]{1,0:T(8,128)(2,1)S(1)}, u32[]{:S(2)}, u32[]{:S(2)}) collective-permute-start(bf16[512,256]{1,0:T(8,128)(2,1)S(1)} %get-tuple-element.100), channel_id=1, source_target_pairs={{0,24},{8,0},{16,8},{24,16},{1,25},{9,1},{17,9},{25,17},{2,26},{10... | collective-permute-start | bytes 786440 | tf_op jit(solution)/shard_map/ppermute | solution.py:43
  50.0 10.0 %collective-permute-start.13 = (bf16[512,256]{1,0:T(8,128)(2,1)S(1)}, bf16[512,256]{1,0:T(8,128)(2,1)S(1)}, u32[]{:S(2)}, u32[]{:S(2)}) collective-permute-start(bf16[512,256]{1,0:T(8,128)(2,1)S(1)} %get-tuple-element.101), channel_id=1, source_target_pairs={{0,8},{8,16},{16,24},{24,0},{1,9},{9,17},{17,25},{25,1},{2,10},{10... | collective-permute-start | bytes 786440 | tf_op jit(solution)/shard_map/ppermute | solution.py:43
  50.7 9.3 %copy-start.2 = (s32[1024,1]{0,1:T(1,128)S(1)}, s32[1024,1]{0,1:T(1,128)}, u32[]{:S(2)}) copy-start(s32[1024,1]{0,1:T(1,128)} %param.19) | copy-start | bytes 12292
  53.2 48.9 %copy-start = (bf16[1024,1024]{1,0:T(8,128)(2,1)S(1)}, bf16[1024,1024]{1,0:T(8,128)(2,1)}, u32[]{:S(2)}) copy-start(bf16[1024,1024]{1,0:T(8,128)(2,1)} %wk_ref.1) | copy-start | bytes 6291460
  53.2 48.9 %copy-start.1 = (bf16[1024,1024]{1,0:T(8,128)(2,1)S(1)}, bf16[1024,1024]{1,0:T(8,128)(2,1)}, u32[]{:S(2)}) copy-start(bf16[1024,1024]{1,0:T(8,128)(2,1)} %wv_ref.1) | copy-start | bytes 6291460
  81.4 12.5 %collective-permute-start.14 = (bf16[1024,256]{1,0:T(8,128)(2,1)S(1)}, bf16[1024,256]{1,0:T(8,128)(2,1)S(1)}, u32[]{:S(2)}, u32[]{:S(2)}) collective-permute-start(bf16[1024,256]{1,0:T(8,128)(2,1)S(1)} %bitcast.4), channel_id=1, source_target_pairs={{0,2},{1,7},{2,4},{3,1},{4,6},{5,3},{6,0},{7,5},{8,10},{9,15},{10,... | collective-permute-start | bytes 1572872 | tf_op jit(solution)/shard_map/ppermute | solution.py:51
  83.9 12.0 %collective-permute-start.15 = (bf16[1024,256]{1,0:T(8,128)(2,1)S(1)}, bf16[1024,256]{1,0:T(8,128)(2,1)S(1)}, u32[]{:S(2)}, u32[]{:S(2)}) collective-permute-start(bf16[1024,256]{1,0:T(8,128)(2,1)S(1)} %bitcast.5), channel_id=1, source_target_pairs={{0,6},{1,3},{2,0},{3,5},{4,2},{5,7},{6,4},{7,1},{8,14},{9,11},{10,... | collective-permute-start | bytes 1572872 | tf_op jit(solution)/shard_map/ppermute | solution.py:51
  83.9 10.0 %collective-permute-start.16 = (bf16[128,512]{1,0:T(8,128)(2,1)S(1)}, bf16[128,512]{1,0:T(8,128)(2,1)S(1)}, u32[]{:S(2)}, u32[]{:S(2)}) collective-permute-start(bf16[128,512]{1,0:T(8,128)(2,1)S(1)} %get-tuple-element.106), channel_id=1, source_target_pairs={{0,64},{32,96},{64,128},{96,160},{128,192},{160,224},{192,0},{224,... | collective-permute-start | bytes 393224 | tf_op jit(solution)/shard_map/ppermute | solution.py:43
  85.9 8.1 %collective-permute-start.17 = (bf16[128,512]{1,0:T(8,128)(2,1)S(1)}, bf16[128,512]{1,0:T(8,128)(2,1)S(1)}, u32[]{:S(2)}, u32[]{:S(2)}) collective-permute-start(bf16[128,512]{1,0:T(8,128)(2,1)S(1)} %get-tuple-element.107), channel_id=1, source_target_pairs={{0,192},{32,224},{64,0},{96,32},{128,64},{160,96},{192,128},{224,1... | collective-permute-start | bytes 393224 | tf_op jit(solution)/shard_map/ppermute | solution.py:43
  87.5 15.8 %collective-permute-start.20 = (bf16[1024,256]{1,0:T(8,128)(2,1)S(1)}, bf16[1024,256]{1,0:T(8,128)(2,1)S(1)}, u32[]{:S(2)}, u32[]{:S(2)}) collective-permute-start(bf16[1024,256]{1,0:T(8,128)(2,1)S(1)} %bitcast.6), channel_id=1, source_target_pairs={{0,1},{1,0},{2,3},{3,2},{4,5},{5,4},{6,7},{7,6},{8,9},{9,8},{10,11... | collective-permute-start | bytes 1572872 | tf_op jit(solution)/shard_map/ppermute | solution.py:43
  95.9 7.5 %collective-permute-start.21 = (bf16[1024,256]{1,0:T(8,128)(2,1)S(1)}, bf16[1024,256]{1,0:T(8,128)(2,1)S(1)}, u32[]{:S(2)}, u32[]{:S(2)}) collective-permute-start(bf16[1024,256]{1,0:T(8,128)(2,1)S(1)} %collective-permute-done.14._.refs_2_), channel_id=1, source_target_pairs={{0,1},{1,0},{2,3},{3,2},{4,5},{5,4},{6,7},{7,6},{8,9},{9,8},{10,11... | collective-permute-start | bytes 1572872 | tf_op jit(solution)/shard_map/ppermute | solution.py:43
  99.5 3.9 %collective-permute-start.22 = (bf16[1024,256]{1,0:T(8,128)(2,1)S(1)}, bf16[1024,256]{1,0:T(8,128)(2,1)S(1)}, u32[]{:S(2)}, u32[]{:S(2)}) collective-permute-start(bf16[1024,256]{1,0:T(8,128)(2,1)S(1)} %collective-permute-done.15.refs_4_), channel_id=1, source_target_pairs={{0,1},{1,0},{2,3},{3,2},{4,5},{5,4},{6,7},{7,6},{8,9},{9,8},{10,11... | collective-permute-start | bytes 1572872 | tf_op jit(solution)/shard_map/ppermute | solution.py:43
  99.5 9.5 %collective-permute-start.18 = (bf16[1024,256]{1,0:T(8,128)(2,1)S(1)}, bf16[1024,256]{1,0:T(8,128)(2,1)S(1)}, u32[]{:S(2)}, u32[]{:S(2)}) collective-permute-start(bf16[1024,256]{1,0:T(8,128)(2,1)S(1)} %collective-permute-done.14._.refs_2_), channel_id=1, source_target_pairs={{0,2},{1,7},{2,4},{3,1},{4,6},{5,3},{6,0},{7,5},{8,10},{9,15},{10,... | collective-permute-start | bytes 1572872 | tf_op jit(solution)/shard_map/ppermute | solution.py:51
  99.9 9.0 %collective-permute-start.19 = (bf16[128,512]{1,0:T(8,128)(2,1)S(1)}, bf16[128,512]{1,0:T(8,128)(2,1)S(1)}, u32[]{:S(2)}, u32[]{:S(2)}) collective-permute-start(bf16[128,512]{1,0:T(8,128)(2,1)S(1)} %get-tuple-element.109), channel_id=1, source_target_pairs={{0,128},{32,160},{64,192},{96,224},{128,0},{160,32},{192,64},{224,... | collective-permute-start | bytes 393224 | tf_op jit(solution)/shard_map/ppermute | solution.py:43
  108.9 3.0 %collective-permute-start.23 = (bf16[1024,256]{1,0:T(8,128)(2,1)S(1)}, bf16[1024,256]{1,0:T(8,128)(2,1)S(1)}, u32[]{:S(2)}, u32[]{:S(2)}) collective-permute-start(bf16[1024,256]{1,0:T(8,128)(2,1)S(1)} %collective-permute-done.18.refs_0_), channel_id=1, source_target_pairs={{0,1},{1,0},{2,3},{3,2},{4,5},{5,4},{6,7},{7,6},{8,9},{9,8},{10,11... | collective-permute-start | bytes 1572872 | tf_op jit(solution)/shard_map/ppermute | solution.py:43
